TPU v7x, 128 devices: a whole 4x4x4 slice. The times are simulated.
128 devices in a mesh: chan: 8 (over z, y_hi), tblk: 16 (over y_lo, x, core).
Axes of the slice: x: 4, y: 4 (y_hi: 2, y_lo: 2; y = y_hi * 2 + y_lo), z: 4, core: 2. Of those that a mesh axis runs over, the one named last changes fastest.
Arguments:
- sky_image: float32 [8, 512, 1024], P(None, 'tblk', 'chan'), may hold values from 0 to 2
- dual_coefs: float32 [9, 8, 512, 1024], P(None, None, 'tblk', 'chan'), may hold values from -3 to 3
- phase_screen: float32 [8, 16, 512, 1024], P('chan', 'tblk'), may hold values from -3.140625 to 3.140625
- grid_rows: int32 [8, 16, 64], P('chan', 'tblk'), may hold values from 0 to 511
- grid_weight: float32 [8, 16, 1024, 256], P('chan', 'tblk'), may hold values from -0.1875 to 0.1875
- visibilities: float32 [8, 16, 2, 64, 256], P('chan', 'tblk'), may hold values from -6 to 6
- filters: float32 [9, 2, 3], replicated, may hold values from -1 to 1
- level_counts: int32 [9], replicated, may hold values from 1 to 3, as said below
- radius: float32 [9], replicated, may hold values from 0.5 to 4
Outputs:
- sky_update: float32 [8, 512, 1024], P(None, 'tblk', 'chan')
- dual_update: float32 [9, 8, 512, 1024], P(None, None, 'tblk', 'chan')
Inputs may be any that keep to these rules, and one draw needn't show every extreme that they name: `level_counts`: at least one basis has 3 levels.
All inputs are finite; a program needn't handle non-finite values.
Results may differ from a plain program's by a relative error of at most 0.00011.
Values sent between devices are 32-bit elements; how exact they have to be, the bound alone decides.
No kernel may reach another device: no remote copies, remote signals or barrier semaphores. Data moves between devices by JAX's collectives and lax.ppermute only.
A program may use at most 128 MiB of HBM per device.

v0:
```python
import math

import jax
import jax.numpy as jnp
from jax import lax
from jax.sharding import PartitionSpec as P

NBASIS = 9
ITERS = 2
HALO = 4


FULL_PRECISION = lax.Precision.HIGHEST
STEP_PRIMAL = 0.5
STEP_DUAL = 0.5


def split_up(value, dim, size):
    before, after = (value.shape[:dim], value.shape[dim + 1 :])
    return jnp.moveaxis(value.reshape(*before, size, -1, *after), dim, 0)


def summed_on_arrival(value, axis, dim):
    size = lax.axis_size(axis)
    pieces = lax.all_to_all(split_up(value, dim, size), axis, 0, 0, tiled=True)
    return jnp.sum(pieces, axis=0)


def shifted(block, axis, distance):
    devices = range(lax.axis_size(axis))
    route = [(i - distance, i) for i in devices if i - distance in devices]
    return lax.ppermute(block, axis, route)


def padded_2(block, sides, width):
    for axis, dim in sides:
        count = lax.axis_size(axis)
        forward = [(i, i + 1) for i in range(count - 1)]
        backward = [(target, source) for source, target in forward]
        low = lax.ppermute(
            lax.slice_in_dim(block, block.shape[dim] - width, None, axis=dim), axis, forward
        )
        high = lax.ppermute(lax.slice_in_dim(block, 0, width, axis=dim), axis, backward)
        block = jnp.concatenate([low, block, high], axis=dim)
    return block


def product(form, left, right):
    return jnp.einsum(
        form, left, right, precision=FULL_PRECISION, preferred_element_type=jnp.float32
    )


def filter_forward(padded, filter_taps, stride, rows_out, cols_out):
    across = jnp.zeros(padded.shape[:2] + (cols_out,), jnp.float32)
    for offset in (-1, 0, 1):
        first_col = HALO + offset * stride
        across = across + filter_taps[1, offset + 1] * lax.dynamic_slice_in_dim(
            padded, first_col, cols_out, 2
        )
    result = jnp.zeros((padded.shape[0], rows_out, cols_out), jnp.float32)
    for offset in (-1, 0, 1):
        first_row = HALO + offset * stride
        result = result + filter_taps[0, offset + 1] * lax.dynamic_slice_in_dim(
            across, first_row, rows_out, 1
        )
    return result


def filter_back(padded, filter_taps, stride, rows_out, cols_out):
    across = jnp.zeros(padded.shape[:2] + (cols_out,), jnp.float32)
    for offset in (-1, 0, 1):
        first_col = HALO - offset * stride
        across = across + filter_taps[1, offset + 1] * lax.dynamic_slice_in_dim(
            padded, first_col, cols_out, 2
        )
    result = jnp.zeros((padded.shape[0], rows_out, cols_out), jnp.float32)
    for offset in (-1, 0, 1):
        first_row = HALO - offset * stride
        result = result + filter_taps[0, offset + 1] * lax.dynamic_slice_in_dim(
            across, first_row, rows_out, 1
        )
    return result


def per_device(
    sky_image,
    dual_coefs,
    phase_screen,
    grid_rows,
    grid_weight,
    visibilities,
    filters,
    level_counts,
    radius,
):
    channels = sky_image.shape[0]
    facet_rows = sky_image.shape[1]
    facet_cols = sky_image.shape[2]
    full_rows = facet_rows * lax.axis_size("tblk")
    full_cols = phase_screen.shape[3]
    screen = jnp.transpose(phase_screen[:, 0], (1, 0, 2))
    cos_screen = jnp.cos(screen)
    sin_screen = jnp.sin(screen)
    weight = grid_weight[:, 0]
    data_real = visibilities[:, 0, 0]
    data_imag = visibilities[:, 0, 1]
    col_index = jnp.arange(full_cols, dtype=jnp.int32)
    col_angle = (col_index[:, None] * col_index[None, :] % full_cols).astype(jnp.float32) * (
        2.0 * math.pi / full_cols
    )
    cols_real = jnp.cos(col_angle) / math.sqrt(full_cols)
    cols_imag = -jnp.sin(col_angle) / math.sqrt(full_cols)
    row_index = jnp.arange(full_rows, dtype=jnp.int32)
    row_angle = (grid_rows[:, 0][:, :, None] * row_index[None, None, :] % full_rows).astype(
        jnp.float32
    ) * (2.0 * math.pi / full_rows)
    rows_real = jnp.cos(row_angle) / math.sqrt(full_rows)
    rows_imag = -jnp.sin(row_angle) / math.sqrt(full_rows)
    spacing = lax.shift_left(jnp.ones_like(level_counts), level_counts - 1)
    radius_cells = radius[:, None, None, None]
    current = sky_image
    dual_now = dual_coefs
    for sweep_index in range(ITERS):
        spread = lax.all_to_all(current, "chan", split_axis=0, concat_axis=2, tiled=True)
        image_strip = jnp.transpose(spread, (1, 0, 2))
        whole_image = lax.all_gather(image_strip, "tblk", axis=0, tiled=True)
        screened_real = cos_screen * whole_image
        screened_imag = sin_screen * whole_image
        spec_real = product("crk,kcl->crl", rows_real, screened_real) - product(
            "crk,kcl->crl", rows_imag, screened_imag
        )
        spec_imag = product("crk,kcl->crl", rows_real, screened_imag) + product(
            "crk,kcl->crl", rows_imag, screened_real
        )
        sky_real = product("crl,lm->crm", spec_real, cols_real) - product(
            "crl,lm->crm", spec_imag, cols_imag
        )
        sky_imag = product("crl,lm->crm", spec_real, cols_imag) + product(
            "crl,lm->crm", spec_imag, cols_real
        )
        misfit_real = product("crm,cmv->crv", sky_real, weight) - data_real
        misfit_imag = product("crm,cmv->crv", sky_imag, weight) - data_imag
        gridded_real = product("crv,cmv->crm", misfit_real, weight)
        gridded_imag = product("crv,cmv->crm", misfit_imag, weight)
        gradient_back_real = product("crm,ml->crl", gridded_real, cols_real) + product(
            "crm,ml->crl", gridded_imag, cols_imag
        )
        gradient_back_imag = product("crm,ml->crl", gridded_imag, cols_real) - product(
            "crm,ml->crl", gridded_real, cols_imag
        )
        grid_real = product("crk,crl->kcl", rows_real, gradient_back_real) + product(
            "crk,crl->kcl", rows_imag, gradient_back_imag
        )
        grid_imag = product("crk,crl->kcl", rows_real, gradient_back_imag) - product(
            "crk,crl->kcl", rows_imag, gradient_back_real
        )
        summed = summed_on_arrival(cos_screen * grid_real + sin_screen * grid_imag, "tblk", 0)
        gradient = lax.all_to_all(
            jnp.transpose(summed, (1, 0, 2)), "chan", split_axis=2, concat_axis=0, tiled=True
        )
        padded = jnp.pad(dual_now, ((0, 0), (0, 0), (2 * HALO, 2 * HALO), (2 * HALO, 2 * HALO)))
        widened = jnp.zeros((channels, facet_rows + 2 * HALO, facet_cols + 2 * HALO), jnp.float32)
        for synthesis_basis_index in range(NBASIS):
            widened = widened + filter_back(
                padded[synthesis_basis_index],
                filters[synthesis_basis_index],
                spacing[synthesis_basis_index],
                facet_rows + 2 * HALO,
                facet_cols + 2 * HALO,
            )
        from_left = shifted(widened[:, :, facet_cols + HALO :], "chan", 1)
        from_right = shifted(widened[:, :, :HALO], "chan", -1)
        middle = widened[:, :, HALO : HALO + facet_cols]
        middle = (
            middle
            + jnp.pad(from_left, ((0, 0), (0, 0), (0, facet_cols - HALO)))
            + jnp.pad(from_right, ((0, 0), (0, 0), (facet_cols - HALO, 0)))
        )
        from_above = shifted(middle[:, facet_rows + HALO :], "tblk", 1)
        from_below = shifted(middle[:, :HALO], "tblk", -1)
        core = middle[:, HALO : HALO + facet_rows]
        synthesised = (
            core
            + jnp.pad(from_above, ((0, 0), (0, facet_rows - HALO), (0, 0)))
            + jnp.pad(from_below, ((0, 0), (facet_rows - HALO, 0), (0, 0)))
        )
        updated = jnp.maximum(current - STEP_PRIMAL * (gradient + synthesised), 0.0)
        leading = 2.0 * updated - current
        extended = padded_2(leading, (("chan", 2), ("tblk", 1)), HALO)
        coefficients = jnp.stack(
            [
                filter_forward(
                    extended, filters[basis_index], spacing[basis_index], facet_rows, facet_cols
                )
                for basis_index in range(NBASIS)
            ]
        )
        raised = dual_now + STEP_DUAL * coefficients
        norm_cells = jnp.sqrt(jnp.sum(raised * raised, axis=1, keepdims=True))
        dual_now = raised * radius_cells / jnp.maximum(norm_cells, radius_cells)
        current = updated
    return (current, dual_now)


def solution(mesh):
    placed = (
        P(None, "tblk", "chan"),
        P(None, None, "tblk", "chan"),
        P("chan", "tblk", None, None),
        P("chan", "tblk", None),
        P("chan", "tblk", None, None),
        P("chan", "tblk", None, None, None),
        P(),
        P(),
        P(),
    )
    return jax.shard_map(
        per_device,
        mesh=mesh,
        in_specs=placed,
        out_specs=(P(None, "tblk", "chan"), P(None, None, "tblk", "chan")),
        check_vma=False,
    )
```

profile of v0, /device:TPU:24, one launch (start us, length us, event | category | flops | bytes accessed | tf_op | source)
XLA Modules:
  0.0 752.3 jit_solution(17351683123077583894)
XLA Ops:
  7.2 13.8 %all_to_all.76 = f32[8,32,128]{2,1,0:T(8,128)S(1)} all-to-all(f32[8,32,128]{2,1,0:T(8,128)} %param.9), channel_id=1, replica_groups=mesh['chan'=8,'tblk'=16] {'chan'}, dimensions={0} | all-to-all | bytes 262144 | tf_op jit(solution)/shard_map/all_to_all | solution.py:125
  60.2 8.1 %fusion.466 = (f32[1,1,512,1024]{3,2,1,0:T(8,128)S(1)}, f32[1,1,512,1024]{3,2,1,0:T(8,128)}) fusion(f32[1,1,512,1024]{3,2,1,0:T(8,128)S(1)} %copy-done.23), kind=kLoop, calls=%fused_computation.588 | loop fusion | bytes 6291456 | tf_op jit(solution)/shard_map/cos | solution.py:103
  74.7 18.4 %fusion.31 = f32[64,1024]{1,0:T(8,128)S(1)} fusion(f32[64,1024]{1,0:T(8,128)S(1)} %fusion.40), kind=kOutput, calls=%fused_computation.62 | convolution fusion | flops 821035008 | bytes 524288 | tf_op jit(solution)/shard_map/crl,lm->crm/dot_general | solution.py:49
  97.2 18.5 %fusion.29 = f32[64,1024]{1,0:T(8,128)S(1)} fusion(f32[64,1024]{1,0:T(8,128)S(1)} %fusion.43), kind=kOutput, calls=%fused_computation.60 | convolution fusion | flops 821035008 | bytes 524288 | tf_op jit(solution)/shard_map/crl,lm->crm/dot_general | solution.py:49
  115.7 18.3 %fusion.52 = f32[64,1024]{1,0:T(8,128)S(1)} fusion(f32[64,1024]{1,0:T(8,128)S(1)} %fusion.31, f32[64,1024]{1,0:T(8,128)S(1)} %fusion.43), kind=kOutput, calls=%fused_computation.81 | convolution fusion | flops 822149120 | bytes 786432 | tf_op jit(solution)/shard_map/crl,lm->crm/dot_general | solution.py:49
  135.9 18.7 %fusion.30 = f32[64,1024]{1,0:T(8,128)S(1)} fusion(f32[64,1024]{1,0:T(8,128)S(1)} %fusion.69), kind=kOutput, calls=%fused_computation.61 | convolution fusion | flops 821035008 | bytes 524288 | tf_op jit(solution)/shard_map/crm,ml->crl/dot_general | solution.py:49
  154.5 18.4 %fusion.53 = f32[64,1024]{1,0:T(8,128)S(1)} fusion(f32[64,1024]{1,0:T(8,128)S(1)} %fusion.29, f32[64,1024]{1,0:T(8,128)S(1)} %fusion.40), kind=kOutput, calls=%fused_computation.82 | convolution fusion | flops 822149120 | bytes 786432 | tf_op jit(solution)/shard_map/crl,lm->crm/dot_general | solution.py:49
  174.7 18.4 %fusion.28 = f32[64,1024]{1,0:T(8,128)S(1)} fusion(f32[64,1024]{1,0:T(8,128)S(1)} %fusion.66), kind=kOutput, calls=%fused_computation.59 | convolution fusion | flops 821035008 | bytes 524288 | tf_op jit(solution)/shard_map/crm,ml->crl/dot_general | solution.py:49
  193.1 18.6 %fusion.55 = f32[64,1024]{1,0:T(8,128)S(1)} fusion(f32[64,1024]{1,0:T(8,128)S(1)} %fusion.28, f32[64,1024]{1,0:T(8,128)S(1)} %fusion.69), kind=kOutput, calls=%fused_computation.84 | convolution fusion | flops 822149120 | bytes 786432 | tf_op jit(solution)/shard_map/crm,ml->crl/dot_general | solution.py:49
  216.4 18.8 %fusion.54 = f32[64,1024]{1,0:T(8,128)S(1)} fusion(f32[64,1024]{1,0:T(8,128)S(1)} %fusion.30, f32[64,1024]{1,0:T(8,128)S(1)} %fusion.66), kind=kOutput, calls=%fused_computation.83 | convolution fusion | flops 822149120 | bytes 786432 | tf_op jit(solution)/shard_map/crm,ml->crl/dot_general | solution.py:49
  248.3 6.1 fusion.103
  268.0 17.5 %fusion.136 = f32[8,40,136]{2,0,1:T(8,128)S(1)} fusion(f32[8,48,136]{2,0,1:T(8,128)S(1)} %get-tuple-element.160, f32[8,48,136]{2,0,1:T(8,128)S(1)} %get-tuple-element.161, f32[8,48,136]{2,0,1:T(8,128)S(1)} %get-tuple-element.162, f32[8,48,136]{2,0,1:T(8,128)S(1)} %get-tuple-element.163, f32[8,48,136]{2,0,1:T(8,128)S(1)} %get-tuple-element.164, ...), kind=kLoop, calls=%fused_computation.197 | loop fusion | flops 2306560 | bytes 4874420 | tf_op jit(solution)/shard_map/add | solution.py:165
  309.5 6.3 all-to-all-start.2
  317.7 5.9 collective-permute-start.3
  368.6 6.9 all-to-all-start.3
  376.7 6.8 multiply_add_fusion.15
  383.5 6.7 multiply_add_fusion.13
  403.3 6.2 multiply_add_fusion.11
  449.5 18.5 %fusion.27 = f32[64,1024]{1,0:T(8,128)S(1)} fusion(f32[64,1024]{1,0:T(8,128)S(1)} %fusion.46), kind=kOutput, calls=%fused_computation.58 | convolution fusion | flops 821035008 | bytes 524288 | tf_op jit(solution)/shard_map/crl,lm->crm/dot_general | solution.py:49
  472.1 18.7 %fusion.25 = f32[64,1024]{1,0:T(8,128)S(1)} fusion(f32[64,1024]{1,0:T(8,128)S(1)} %fusion.49), kind=kOutput, calls=%fused_computation.56 | convolution fusion | flops 821035008 | bytes 524288 | tf_op jit(solution)/shard_map/crl,lm->crm/dot_general | solution.py:49
  490.8 18.4 %fusion.56 = f32[64,1024]{1,0:T(8,128)S(1)} fusion(f32[64,1024]{1,0:T(8,128)S(1)} %fusion.27, f32[64,1024]{1,0:T(8,128)S(1)} %fusion.49), kind=kOutput, calls=%fused_computation.85 | convolution fusion | flops 822149120 | bytes 786432 | tf_op jit(solution)/shard_map/crl,lm->crm/dot_general | solution.py:49
  511.0 18.4 %fusion.26 = f32[64,1024]{1,0:T(8,128)S(1)} fusion(f32[64,1024]{1,0:T(8,128)S(1)} %fusion.63), kind=kOutput, calls=%fused_computation.57 | convolution fusion | flops 821035008 | bytes 524288 | tf_op jit(solution)/shard_map/crm,ml->crl/dot_general | solution.py:49
  529.4 18.4 %fusion.57 = f32[64,1024]{1,0:T(8,128)S(1)} fusion(f32[64,1024]{1,0:T(8,128)S(1)} %fusion.25, f32[64,1024]{1,0:T(8,128)S(1)} %fusion.46), kind=kOutput, calls=%fused_computation.86 | convolution fusion | flops 822149120 | bytes 786432 | tf_op jit(solution)/shard_map/crl,lm->crm/dot_general | solution.py:49
  549.5 18.5 %fusion.24 = f32[64,1024]{1,0:T(8,128)S(1)} fusion(f32[64,1024]{1,0:T(8,128)S(1)} %fusion.60), kind=kOutput, calls=%fused_computation.55 | convolution fusion | flops 821035008 | bytes 524288 | tf_op jit(solution)/shard_map/crm,ml->crl/dot_general | solution.py:49
  568.0 18.8 %fusion.59 = f32[64,1024]{1,0:T(8,128)S(1)} fusion(f32[64,1024]{1,0:T(8,128)S(1)} %fusion.24, f32[64,1024]{1,0:T(8,128)S(1)} %fusion.63), kind=kOutput, calls=%fused_computation.88 | convolution fusion | flops 822149120 | bytes 786432 | tf_op jit(solution)/shard_map/crm,ml->crl/dot_general | solution.py:49
  591.5 18.5 %fusion.58 = f32[64,1024]{1,0:T(8,128)S(1)} fusion(f32[64,1024]{1,0:T(8,128)S(1)} %fusion.26, f32[64,1024]{1,0:T(8,128)S(1)} %fusion.60), kind=kOutput, calls=%fused_computation.87 | convolution fusion | flops 822149120 | bytes 786432 | tf_op jit(solution)/shard_map/crm,ml->crl/dot_general | solution.py:49
  634.2 17.5 %fusion.110 = f32[8,40,136]{2,0,1:T(8,128)S(1)} fusion(f32[8,48,136]{2,0,1:T(8,128)S(1)} %fusion.73, f32[8,48,136]{2,0,1:T(8,128)S(1)} %fusion.75, f32[8,48,136]{2,0,1:T(8,128)S(1)} %fusion.77, f32[8,48,136]{2,0,1:T(8,128)S(1)} %fusion.79, f32[8,48,136]{2,0,1:T(8,128)S(1)} %fusion.81, f32[8,48,136]{2,0,1:T(8,128)S(1)} %copy-done.11, ...), kind=kLoop, calls=%fused_computation.162 | loop fusion | flops 2306560 | bytes 4874420 | tf_op jit(solution)/shard_map/add | solution.py:165
  669.0 6.9 all-to-all-start.5
  700.4 6.0 collective-permute-start.15
  707.9 6.1 multiply_add_fusion.6
  714.0 6.0 multiply_add_fusion.4
  720.0 6.1 multiply_add_fusion.2
  (254 shorter events, 269.0 us)
Async XLA Ops:
  7.2 126.9 %copy-start = (f32[1,1,1024,256]{3,2,1,0:T(8,128)S(1)}, f32[1,1,1024,256]{3,2,1,0:T(8,128)}, u32[]{:S(2)}) copy-start(f32[1,1,1024,256]{3,2,1,0:T(8,128)} %param.13) | copy-start | bytes 3145732
  7.2 40.1 %copy-start.42 = (f32[9,2,3]{0,1,2:T(2,128)S(1)}, f32[9,2,3]{0,1,2:T(2,128)}, u32[]{:S(2)}) copy-start(f32[9,2,3]{0,1,2:T(2,128)} %param.15) | copy-start | bytes 652
  7.2 61.1 %all-gather.3.cloned.1.call-start = ((), (), s32[]{:S(2)}) async-start(), calls=%async_computation.6 | async-start | bytes 2228224 | tf_op jit(solution)/shard_map/all_gather | solution.py:127
  74.7 18.5 %copy-start.1 = (f32[1,1,512,1024]{3,2,1,0:T(8,128)S(1)}, f32[1,1,512,1024]{3,2,1,0:T(8,128)}, u32[]{:S(2)}) copy-start(f32[1,1,512,1024]{3,2,1,0:T(8,128)} %get-tuple-element.17) | copy-start | bytes 6291460
  115.7 18.4 %copy-start.38 = (f32[1,1,2,64,256]{4,3,2,1,0:T(8,128)S(1)}, f32[1,1,2,64,256]{4,3,2,1,0:T(8,128)}, u32[]{:S(2)}) copy-start(f32[1,1,2,64,256]{4,3,2,1,0:T(8,128)} %param.14) | copy-start | bytes 393220
  241.8 58.8 %all-to-all-start.1 = ((f32[16,32,1,1024]{3,1,2,0:T(8,128)}), f32[16,32,1,1024]{3,1,2,0:T(8,128)}, u32[]{:S(2)}, u32[]{:S(2)}) async-start(f32[16,32,1,1024]{3,1,2,0:T(8,128)} %bitcast.544), calls=%async_computation.1 | async-start | bytes 4194304 | tf_op jit(solution)/shard_map/all_to_all | solution.py:25
  285.6 9.7 %collective-permute-start = (f32[8,40,4]{2,0,1:T(8,128)S(1)}, f32[8,40,4]{2,0,1:T(8,128)S(1)}, u32[]{:S(2)}, u32[]{:S(2)}) collective-permute-start(f32[8,40,4]{2,0,1:T(8,128)S(1)} %get-tuple-element.78), channel_id=1, source_target_pairs={{0,16},{16,32},{32,48},{48,64},{64,80},{80,96},{96,112},{1,17},{17... | collective-permute-start | bytes 15368 | tf_op jit(solution)/shard_map/ppermute | solution.py:32
  290.2 10.3 %collective-permute-start.1 = (f32[8,40,4]{2,0,1:T(8,128)S(1)}, f32[8,40,4]{2,0,1:T(8,128)S(1)}, u32[]{:S(2)}, u32[]{:S(2)}) collective-permute-start(f32[8,40,4]{2,0,1:T(8,128)S(1)} %get-tuple-element.79), channel_id=1, source_target_pairs={{16,0},{32,16},{48,32},{64,48},{80,64},{96,80},{112,96},{17,1},{33... | collective-permute-start | bytes 15368 | tf_op jit(solution)/shard_map/ppermute | solution.py:32
  309.5 14.1 %all-to-all-start.2 = ((f32[8,1,4096]{2,1,0:T(1,128)}), f32[8,1,4096]{2,1,0:T(1,128)}, u32[]{:S(2)}, u32[]{:S(2)}) async-start(f32[8,1,4096]{2,1,0:T(1,128)} %reshape.935), calls=%async_computation.2 | async-start | bytes 262144 | tf_op jit(solution)/shard_map/all_to_all | solution.py:159
  315.8 13.2 %collective-permute-start.2 = (f32[8,4,128]{2,0,1:T(8,128)S(1)}, f32[8,4,128]{2,0,1:T(8,128)S(1)}, u32[]{:S(2)}, u32[]{:S(2)}) collective-permute-start(f32[8,4,128]{2,0,1:T(8,128)S(1)} %get-tuple-element.82), channel_id=1, source_target_pairs={{0,1},{1,2},{2,3},{3,4},{4,5},{5,6},{6,7},{7,8},{8,9},{9,10},{10,1... | collective-permute-start | bytes 49160 | tf_op jit(solution)/shard_map/ppermute | solution.py:32
  317.7 11.3 %collective-permute-start.3 = (f32[8,4,128]{2,0,1:T(8,128)S(1)}, f32[8,4,128]{2,0,1:T(8,128)S(1)}, u32[]{:S(2)}, u32[]{:S(2)}) collective-permute-start(f32[8,4,128]{2,0,1:T(8,128)S(1)} %get-tuple-element.83), channel_id=1, source_target_pairs={{1,0},{2,1},{3,2},{4,3},{5,4},{6,5},{7,6},{8,7},{9,8},{10,9},{11,1... | collective-permute-start | bytes 49160 | tf_op jit(solution)/shard_map/ppermute | solution.py:32
  330.0 45.4 %copy-start.36 = (f32[8,32,128]{2,0,1:T(8,128)}, f32[8,32,128]{2,0,1:T(8,128)S(1)}, u32[]{:S(2)}) copy-start(f32[8,32,128]{2,0,1:T(8,128)S(1)} %get-tuple-element.15) | copy-start | bytes 393220
  330.1 8.4 %collective-permute-start.4 = (f32[8,32,4]{2,0,1:T(8,128)S(1)}, f32[8,32,4]{2,0,1:T(8,128)S(1)}, u32[]{:S(2)}, u32[]{:S(2)}) collective-permute-start(f32[8,32,4]{2,0,1:T(8,128)S(1)} %get-tuple-element.86), channel_id=1, source_target_pairs={{0,16},{16,32},{32,48},{48,64},{64,80},{80,96},{96,112},{1,17},{17... | collective-permute-start | bytes 12296 | tf_op jit(solution)/shard_map/ppermute | solution.py:40
  333.5 9.3 %collective-permute-start.5 = (f32[8,32,4]{2,0,1:T(8,128)S(1)}, f32[8,32,4]{2,0,1:T(8,128)S(1)}, u32[]{:S(2)}, u32[]{:S(2)}) collective-permute-start(f32[8,32,4]{2,0,1:T(8,128)S(1)} %get-tuple-element.87), channel_id=1, source_target_pairs={{16,0},{32,16},{48,32},{64,48},{80,64},{96,80},{112,96},{17,1},{33... | collective-permute-start | bytes 12296 | tf_op jit(solution)/shard_map/ppermute | solution.py:43
  343.5 32.0 %collective-permute-start.6 = (f32[8,4,136]{2,0,1:T(8,128)S(1)}, f32[8,4,136]{2,0,1:T(8,128)S(1)}, u32[]{:S(2)}, u32[]{:S(2)}) collective-permute-start(f32[8,4,136]{2,0,1:T(8,128)S(1)} %get-tuple-element.56), channel_id=1, source_target_pairs={{0,1},{1,2},{2,3},{3,4},{4,5},{5,6},{6,7},{7,8},{8,9},{9,10},{10,1... | collective-permute-start | bytes 52232 | tf_op jit(solution)/shard_map/ppermute | solution.py:40
  345.4 30.1 %collective-permute-start.7 = (f32[8,4,136]{2,0,1:T(8,128)S(1)}, f32[8,4,136]{2,0,1:T(8,128)S(1)}, u32[]{:S(2)}, u32[]{:S(2)}) collective-permute-start(f32[8,4,136]{2,0,1:T(8,128)S(1)} %get-tuple-element.57), channel_id=1, source_target_pairs={{1,0},{2,1},{3,2},{4,3},{5,4},{6,5},{7,6},{8,7},{9,8},{10,9},{11,1... | collective-permute-start | bytes 52232 | tf_op jit(solution)/shard_map/ppermute | solution.py:43
  368.6 24.4 %all-to-all-start.3 = ((f32[8,32,128]{2,1,0:T(8,128)}), f32[8,32,128]{2,1,0:T(8,128)}, u32[]{:S(2)}, u32[]{:S(2)}) async-start(f32[8,32,128]{2,1,0:T(8,128)} %copy.127), calls=%async_computation.3 | async-start | bytes 262144 | tf_op jit(solution)/shard_map/all_to_all | solution.py:125
  375.5 67.7 %all-gather.5.cloned.1.call-start = ((), (), s32[]{:S(2)}) async-start(), calls=%async_computation.7 | async-start | bytes 2228224 | tf_op jit(solution)/shard_map/all_gather | solution.py:127
  396.2 20.8 %copy-start.24 = (f32[8,40,128]{2,0,1:T(8,128)S(1)}, f32[8,40,128]{2,0,1:T(8,128)}, u32[]{:S(2)}) copy-start(f32[8,40,128]{2,0,1:T(8,128)} %get-tuple-element.72) | copy-start | bytes 491524
  403.3 21.5 %copy-start.7 = (f32[9,8,32,128]{3,2,1,0:T(8,128)S(1)}, f32[9,8,32,128]{3,2,1,0:T(8,128)}, u32[]{:S(2)}) copy-start(f32[9,8,32,128]{3,2,1,0:T(8,128)} %param.10) | copy-start | bytes 3538948
  449.5 18.5 %copy-start.2 = (f32[1,1,512,1024]{3,2,1,0:T(8,128)S(1)}, f32[1,1,512,1024]{3,2,1,0:T(8,128)}, u32[]{:S(2)}) copy-start(f32[1,1,512,1024]{3,2,1,0:T(8,128)} %get-tuple-element.17) | copy-start | bytes 6291460
  616.6 49.1 %all-to-all-start.4 = ((f32[16,32,1,1024]{3,1,2,0:T(8,128)}), f32[16,32,1,1024]{3,1,2,0:T(8,128)S(1)}, u32[]{:S(2)}, u32[]{:S(2)}) async-start(f32[16,32,1,1024]{3,1,2,0:T(8,128)} %bitcast.545), calls=%async_computation.4 | async-start | bytes 4194304 | tf_op jit(solution)/shard_map/all_to_all | solution.py:25
  651.8 9.3 %collective-permute-start.8 = (f32[8,40,4]{2,0,1:T(8,128)S(1)}, f32[8,40,4]{2,0,1:T(8,128)S(1)}, u32[]{:S(2)}, u32[]{:S(2)}) collective-permute-start(f32[8,40,4]{2,0,1:T(8,128)S(1)} %get-tuple-element.67), channel_id=1, source_target_pairs={{0,16},{16,32},{32,48},{48,64},{64,80},{80,96},{96,112},{1,17},{17... | collective-permute-start | bytes 15368 | tf_op jit(solution)/shard_map/ppermute | solution.py:32
  655.2 10.4 %collective-permute-start.9 = (f32[8,40,4]{2,0,1:T(8,128)S(1)}, f32[8,40,4]{2,0,1:T(8,128)S(1)}, u32[]{:S(2)}, u32[]{:S(2)}) collective-permute-start(f32[8,40,4]{2,0,1:T(8,128)S(1)} %get-tuple-element.68), channel_id=1, source_target_pairs={{16,0},{32,16},{48,32},{64,48},{80,64},{96,80},{112,96},{17,1},{33... | collective-permute-start | bytes 15368 | tf_op jit(solution)/shard_map/ppermute | solution.py:32
  665.9 19.7 %copy-start.37 = (f32[8,32,128]{2,0,1:T(8,128)S(1)}, f32[8,32,128]{2,0,1:T(8,128)}, u32[]{:S(2)}) copy-start(f32[8,32,128]{2,0,1:T(8,128)} %copy-done.36) | copy-start | bytes 393220
  669.0 14.6 %all-to-all-start.5 = ((f32[8,1,4096]{2,1,0:T(1,128)}), f32[8,1,4096]{2,1,0:T(1,128)S(1)}, u32[]{:S(2)}, u32[]{:S(2)}) async-start(f32[8,1,4096]{2,1,0:T(1,128)} %reshape.937), calls=%async_computation.5 | async-start | bytes 262144 | tf_op jit(solution)/shard_map/all_to_all | solution.py:159
  675.9 9.7 %collective-permute-start.10 = (f32[8,4,128]{2,0,1:T(8,128)S(1)}, f32[8,4,128]{2,0,1:T(8,128)S(1)}, u32[]{:S(2)}, u32[]{:S(2)}) collective-permute-start(f32[8,4,128]{2,0,1:T(8,128)S(1)} %get-tuple-element.80), channel_id=1, source_target_pairs={{0,1},{1,2},{2,3},{3,4},{4,5},{5,6},{6,7},{7,8},{8,9},{9,10},{10,1... | collective-permute-start | bytes 49160 | tf_op jit(solution)/shard_map/ppermute | solution.py:32
  677.8 7.8 %collective-permute-start.11 = (f32[8,4,128]{2,0,1:T(8,128)S(1)}, f32[8,4,128]{2,0,1:T(8,128)S(1)}, u32[]{:S(2)}, u32[]{:S(2)}) collective-permute-start(f32[8,4,128]{2,0,1:T(8,128)S(1)} %get-tuple-element.81), channel_id=1, source_target_pairs={{1,0},{2,1},{3,2},{4,3},{5,4},{6,5},{7,6},{8,7},{9,8},{10,9},{11,1... | collective-permute-start | bytes 49160 | tf_op jit(solution)/shard_map/ppermute | solution.py:32
  685.7 8.4 %collective-permute-start.12 = (f32[8,32,4]{2,0,1:T(8,128)S(1)}, f32[8,32,4]{2,0,1:T(8,128)S(1)}, u32[]{:S(2)}, u32[]{:S(2)}) collective-permute-start(f32[8,32,4]{2,0,1:T(8,128)S(1)} %get-tuple-element.84), channel_id=1, source_target_pairs={{0,16},{16,32},{32,48},{48,64},{64,80},{80,96},{96,112},{1,17},{17... | collective-permute-start | bytes 12296 | tf_op jit(solution)/shard_map/ppermute | solution.py:40
  689.1 9.3 %collective-permute-start.13 = (f32[8,32,4]{2,0,1:T(8,128)S(1)}, f32[8,32,4]{2,0,1:T(8,128)S(1)}, u32[]{:S(2)}, u32[]{:S(2)}) collective-permute-start(f32[8,32,4]{2,0,1:T(8,128)S(1)} %get-tuple-element.85), channel_id=1, source_target_pairs={{16,0},{32,16},{48,32},{64,48},{80,64},{96,80},{112,96},{17,1},{33... | collective-permute-start | bytes 12296 | tf_op jit(solution)/shard_map/ppermute | solution.py:43
  698.5 8.6 %collective-permute-start.14 = (f32[8,4,136]{2,0,1:T(8,128)S(1)}, f32[8,4,136]{2,0,1:T(8,128)S(1)}, u32[]{:S(2)}, u32[]{:S(2)}) collective-permute-start(f32[8,4,136]{2,0,1:T(8,128)S(1)} %get-tuple-element.54), channel_id=1, source_target_pairs={{0,1},{1,2},{2,3},{3,4},{4,5},{5,6},{6,7},{7,8},{8,9},{9,10},{10,1... | collective-permute-start | bytes 52232 | tf_op jit(solution)/shard_map/ppermute | solution.py:40
  700.4 7.3 collective-permute-start.15
  (36 other events, 261.9 us)
Sparse Core Ops, SparseCore 0:
  22.0 32.7 all-gather.2
  396.3 31.9 all-gather.4
where the time goes:
time: 764 us; the launch traced here: 752 us
  matrix products  347 us (45%)
  other arithmetic  180 us (24%)
  starting transfers between devices  90 us (12%)
  between operations  54.6 us (7%)
  local copies, waits for them, and re-layouts  42.1 us (6%)
  waiting for transfers between devices  25.1 us (3%)
  blocking collectives  13.8 us (2%)
    dot_general x40, matrix products, product(): jnp.einsum(form, left, right, precision=FULL_PRECISION, preferred_element...  347 us
    add x14, other arithmetic, filter_back(): across + filter_taps[1, offset + 1] * lax.dynamic_slice_in_dim(padded, fi...  47 us
    unnamed x18, other arithmetic  43.1 us
    add x6, other arithmetic, filter_forward(): across + filter_taps[1, offset + 1] * lax.dynamic_slice_in_dim(padded, fi...  37.8 us
    add x2, other arithmetic, per_device(): widened + filter_back(padded[synthesis_basis_index], filters[synthesis_ba...  35 us
    ppermute x8, starting transfers between devices, shifted(): return lax.ppermute(block, axis, route)  30.2 us
    ppermute x4, starting transfers between devices, padded_2(): lax.ppermute(lax.slice_in_dim(block, 0, width, axis=dim), axis, backward)  19.7 us
  transfers between devices with their start and end apart: 23, of which 9 were waited for; matrix products, arithmetic and copies ran while one was open for 22% of the time, Pallas kernels for 0%

commit v1 on v0

v1 whole, which is shorter than its diff:
```python
import functools
import math

import jax
import jax.numpy as jnp
import ml_dtypes
import numpy as np
from jax import lax
from jax.experimental import pallas as pl
from jax.experimental.pallas import tpu as pltpu
from jax.sharding import Mesh
from jax.sharding import PartitionSpec as P

NBASIS = 9
HALO = 4
F32 = jnp.float32
BF16 = jnp.bfloat16
CHIPS = ("y", "x")
STEPS = (1, 2, 4)
SHIFTS = (0, -1, 1, -2, 2, -4, 4)
MIB = 1024 * 1024
SMEM = pl.BlockSpec(memory_space=pltpu.SMEM)
VMEM = pl.BlockSpec(memory_space=pltpu.VMEM)


def params(grid_dims=0):
    if grid_dims:
        return pltpu.CompilerParams(
            vmem_limit_bytes=48 * MIB, dimension_semantics=("arbitrary",) * grid_dims
        )
    return pltpu.CompilerParams(vmem_limit_bytes=48 * MIB)


def parts(value):
    high = value.astype(BF16)
    return high, (value - high.astype(F32)).astype(BF16)


def dot(left, right):
    return jnp.dot(left, right, preferred_element_type=F32)


def dot_t(left, right):
    return lax.dot_general(left, right, (((1,), (1,)), ((), ())), preferred_element_type=F32)


def sincos(angle):
    y = 0.5 * angle
    z = y * y
    s = F32(2.6050929582509915e-06)
    for a in (-0.00019809011067269285, 0.008333050086782038, -0.16666657944392363, 0.9999999956966753):
        s = s * z + F32(a)
    s = s * y
    c = F32(-2.6050510628158867e-07)
    for a in (
        2.476010151557824e-05,
        -0.0013888360127752544,
        0.041666636147634536,
        -0.4999999935511792,
        0.9999999997790222,
    ):
        c = c * z + F32(a)
    return 2.0 * s * c, 1.0 - 2.0 * s * s


def screens_kernel(own_ref, other_ref, cos_ref, sin_ref):
    for b, ref in enumerate((own_ref, other_ref)):
        s, c = sincos(ref[...])
        cos_ref[b] = c
        sin_ref[b] = s


def screens(own, other):
    rows, cols = own.shape
    tile = 64
    return pl.pallas_call(
        screens_kernel,
        grid=(rows // tile,),
        in_specs=[pl.BlockSpec((tile, cols), lambda i: (i, 0))] * 2,
        out_specs=[pl.BlockSpec((2, tile, cols), lambda i: (0, i, 0))] * 2,
        out_shape=[jax.ShapeDtypeStruct((2, rows, cols), F32)] * 2,
        compiler_params=params(1),
        name="screens",
    )(own, other)


def tables_kernel(gcol_ref, grow_ref, left_ref, right_ref):
    size = 512
    for b in range(2):
        for turned, g_ref, out_ref in ((0, gcol_ref, left_ref), (1, grow_ref, right_ref)):
            shape = (size, 128) if turned else (128, size)
            n = lax.broadcasted_iota(jnp.int32, shape, 0 if turned else 1)
            picked = lax.broadcasted_iota(jnp.int32, shape, 1 if turned else 0)
            index = (g_ref[b] * n) & (size - 1)
            index = jnp.where(index >= size // 2, index - size, index)
            s, c = sincos(index.astype(F32) * F32(2.0 * math.pi / size))
            high, low = parts(jnp.where(picked < 64, c, -s) * F32(1.0 / math.sqrt(size)))
            if turned:
                out_ref[b, :, :128] = high
                out_ref[b, :, 128:] = low
            else:
                out_ref[b, :128, :] = high
                out_ref[b, 128:, :] = low


def tables(rows_both):
    doubled = jnp.concatenate([rows_both, rows_both], axis=1)
    return pl.pallas_call(
        tables_kernel,
        in_specs=[VMEM, VMEM],
        out_specs=[VMEM, VMEM],
        out_shape=[
            jax.ShapeDtypeStruct((2, 256, 512), BF16),
            jax.ShapeDtypeStruct((2, 512, 256), BF16),
        ],
        compiler_params=params(),
        name="tables",
    )(doubled[:, :, None], doubled[:, None, :])


def gridding_kernel(place_ref, own_ref, other_ref, table_ref, out_ref):
    half = place_ref[0]
    odd = lax.broadcasted_iota(jnp.int32, own_ref.shape, 0) & half
    sign = jnp.where(odd == 1, F32(-1.0), F32(1.0))
    for b, ref in enumerate((own_ref, other_ref)):
        high, low = parts(ref[...] * sign)
        for part in range(2):
            value = dot(table_ref[part, 0], high)
            value = value + dot(table_ref[part, 0], low)
            value = value + dot(table_ref[part, 1], high)
            out_ref[b, part, 0], out_ref[b, part, 1] = parts(value)


def column_table():
    angle = (np.arange(512)[:, None] * np.arange(1024)[None, :] % 1024) * (2.0 * np.pi / 1024)
    out = np.zeros((2, 2, 512, 1024), ml_dtypes.bfloat16)
    for part, value in enumerate((np.cos(angle) / 32.0, -np.sin(angle) / 32.0)):
        high = value.astype(ml_dtypes.bfloat16)
        out[part, 0] = high
        out[part, 1] = (value - high.astype(np.float64)).astype(ml_dtypes.bfloat16)
    return out


def gridding(place, own, other):
    return pl.pallas_call(
        gridding_kernel,
        in_specs=[SMEM, VMEM, VMEM, VMEM],
        out_specs=VMEM,
        out_shape=jax.ShapeDtypeStruct((2, 2, 2, 512, 256), BF16),
        compiler_params=params(),
        name="gridding",
    )(place, own, other, column_table())


def thrice(left, high, low, form):
    count = left.shape[0] // 2
    both = form(left, high)
    return both[:count] + both[count:] + form(left[:count], low)


def forward_kernel(image_ref, cos_ref, sin_ref, left_ref, grid_ref, out_ref):
    image = image_ref[...]
    left = left_ref[0]
    from_real = thrice(left, *parts(cos_ref[0] * image), dot)
    from_imag = thrice(left, *parts(sin_ref[0] * image), dot)
    spectrum = jnp.concatenate(
        [from_real[:64] - from_imag[64:], from_imag[:64] + from_real[64:]], axis=0
    )
    spectrum = jnp.concatenate(parts(spectrum), axis=0)
    by_real = thrice(spectrum, grid_ref[0, 0, 0], grid_ref[0, 0, 1], dot)
    by_imag = thrice(spectrum, grid_ref[0, 1, 0], grid_ref[0, 1, 1], dot)
    seen = jnp.concatenate([by_real[:64] - by_imag[64:], by_imag[:64] + by_real[64:]], axis=0)

    @pl.when(pl.program_id(1) == 0)
    def first():
        out_ref[0] = seen

    @pl.when(pl.program_id(1) != 0)
    def later():
        out_ref[0] += seen


def forward(image, cos, sin, left, grid):
    tile = 256
    return pl.pallas_call(
        forward_kernel,
        grid=(2, 512 // tile),
        in_specs=[
            pl.BlockSpec((512, tile), lambda b, c: (0, c)),
            pl.BlockSpec((1, 512, tile), lambda b, c: (b, 0, c)),
            pl.BlockSpec((1, 512, tile), lambda b, c: (b, 0, c)),
            pl.BlockSpec((1, 256, 512), lambda b, c: (b, 0, 0)),
            pl.BlockSpec((1, 2, 2, tile, 256), lambda b, c: (b, 0, 0, c, 0)),
        ],
        out_specs=pl.BlockSpec((1, 128, 256), lambda b, c: (b, 0, 0)),
        out_shape=jax.ShapeDtypeStruct((2, 128, 256), F32),
        compiler_params=params(2),
        name="forward",
    )(image, cos, sin, left, grid)


def backward_kernel(place_ref, mine_ref, theirs_ref, data_ref, grid_ref, right_ref, cos_ref, sin_ref, *rest):
    extra_ref = rest[0] if len(rest) == 3 else None
    out_ref, total_ref = rest[-2:]
    tile = total_ref.shape[1]
    total = None
    for b in range(2):
        misfit = mine_ref[b] + theirs_ref[1 - b] - data_ref[b]
        misfit = jnp.concatenate(parts(misfit), axis=0)
        by_real = thrice(misfit, grid_ref[b, 0, 0], grid_ref[b, 0, 1], dot_t)
        by_imag = thrice(misfit, grid_ref[b, 1, 0], grid_ref[b, 1, 1], dot_t)
        real = by_real[:64] + by_imag[64:]
        imag = by_real[64:] - by_imag[:64]
        spread = jnp.concatenate(
            [jnp.concatenate([real, imag], axis=1), jnp.concatenate([imag, -real], axis=1)], axis=0
        )
        high, low = parts(spread)
        right = right_ref[b]
        pulled = dot(right, jnp.concatenate([high, high], axis=0)) + dot(right[:, :128], low)
        part = cos_ref[b] * pulled[:, :tile] + sin_ref[b] * pulled[:, tile:]
        total = part if total is None else total + part
    total_ref[0:8] = jnp.zeros((8, tile), F32)
    total_ref[520:528] = jnp.zeros((8, tile), F32)
    total_ref[8:520] = total
    for chip in range(8):
        out_ref[chip] = total_ref[64 * chip + 4 : 64 * chip + 76]
    if extra_ref is not None:
        chip = place_ref[1]
        out_ref[chip] += extra_ref[...]

        @pl.when(chip > 0)
        def above():
            out_ref[chip - 1, 64:72] += extra_ref[0:8]

        @pl.when(chip < 7)
        def below():
            out_ref[chip + 1, 0:8] += extra_ref[64:72]


def backward(place, mine, theirs, data, grid, right, cos, sin, extra=None):
    tile = 256
    seen = pl.BlockSpec((2, 128, 256), lambda c: (0, 0, 0))
    screen = pl.BlockSpec((2, 512, tile), lambda c: (0, 0, c))
    specs = [
        SMEM,
        seen,
        seen,
        seen,
        pl.BlockSpec((2, 2, 2, tile, 256), lambda c: (0, 0, 0, c, 0)),
        pl.BlockSpec((2, 512, 256), lambda c: (0, 0, 0)),
        screen,
        screen,
    ]
    args = [place, mine, theirs, data, grid, right, cos, sin]
    if extra is not None:
        specs.append(pl.BlockSpec((72, tile), lambda c: (0, c)))
        args.append(extra)
    return pl.pallas_call(
        backward_kernel,
        grid=(512 // tile,),
        in_specs=specs,
        out_specs=pl.BlockSpec((8, 72, tile), lambda c: (0, 0, c)),
        out_shape=jax.ShapeDtypeStruct((8, 72, 512), F32),
        scratch_shapes=[pltpu.VMEM((528, tile), F32)],
        compiler_params=params(1),
        name="backward",
    )(*args)


def update_kernel(place_ref, sent_ref, image_ref, own_ref, other_ref, many_ref, scratch_ref):
    half, chip = place_ref[0], place_ref[1]
    total = sent_ref[0]
    for source in range(1, 8):
        total = total + sent_ref[source]
    row = lax.broadcasted_iota(jnp.int32, total.shape, 0) + (64 * chip - HALO)
    value = jnp.maximum(image_ref[...] - 0.5 * total, 0.0)
    scratch_ref[...] = jnp.where((row >= 0) & (row < 512), value, 0.0)
    own_ref[...] = scratch_ref[pl.ds(pl.multiple_of(32 * half, 32), 40)]
    other_ref[...] = scratch_ref[pl.ds(pl.multiple_of(32 - 32 * half, 32), 40)]
    core = scratch_ref[HALO : HALO + 64]
    for target in range(8):
        many_ref[target] = core


def update(place, sent, image):
    window = jax.ShapeDtypeStruct((40, 512), F32)
    return pl.pallas_call(
        update_kernel,
        in_specs=[SMEM, VMEM, VMEM],
        out_specs=[VMEM] * 3,
        out_shape=[window, window, jax.ShapeDtypeStruct((8, 64, 512), F32)],
        scratch_shapes=[pltpu.VMEM((72, 512), F32)],
        compiler_params=params(),
        name="update",
    )(place, sent, image)


def total_kernel(place_ref, sent_ref, own_ref, other_ref, scratch_ref):
    half = place_ref[0]
    total = sent_ref[0]
    for source in range(1, 8):
        total = total + sent_ref[source]
    scratch_ref[...] = total
    own_ref[...] = scratch_ref[pl.ds(pl.multiple_of(32 * half, 32), 40)]
    other_ref[...] = scratch_ref[pl.ds(pl.multiple_of(32 - 32 * half, 32), 40)]


def total_windows(place, sent):
    window = jax.ShapeDtypeStruct((40, 512), F32)
    return pl.pallas_call(
        total_kernel,
        in_specs=[SMEM, VMEM],
        out_specs=[VMEM] * 2,
        out_shape=[window, window],
        scratch_shapes=[pltpu.VMEM((72, 512), F32)],
        compiler_params=params(),
        name="total_windows",
    )(place, sent)


def lanes_of(shape):
    return lax.broadcasted_iota(jnp.int32, shape, len(shape) - 1)


def to_facets_kernel(place_ref, own_ref, theirs_ref, out_ref, full_ref):
    half = place_ref[0]
    full_ref[0] = jnp.zeros((40, 128), F32)
    full_ref[9] = jnp.zeros((40, 128), F32)
    for i in range(4):
        full_ref[1 + 4 * half + i] = own_ref[:, 128 * i : 128 * i + 128]
        full_ref[5 - 4 * half + i] = theirs_ref[:, 128 * i : 128 * i + 128]
    lane = lanes_of((40, 128))
    for facet in range(8):
        out_ref[facet, :40] = full_ref[facet + 1]
        out_ref[facet, 40:] = jnp.where(
            lane < HALO,
            full_ref[facet + 2],
            jnp.where(lane >= 128 - HALO, full_ref[facet], 0.0),
        )


def to_facets(place, own, other):
    theirs = swapped(other)
    packed = pl.pallas_call(
        to_facets_kernel,
        in_specs=[SMEM, VMEM, VMEM],
        out_specs=VMEM,
        out_shape=jax.ShapeDtypeStruct((8, 80, 128), F32),
        scratch_shapes=[pltpu.VMEM((10, 40, 128), F32)],
        compiler_params=params(),
        name="to_facets",
    )(place, own, theirs)
    return lax.all_to_all(packed, "chan", 0, 0, tiled=True)


def to_strip_kernel(place_ref, sent_ref, own_ref, other_ref, full_ref):
    half = place_ref[0]
    lane = lanes_of((40, 128))
    for facet in range(8):
        value = sent_ref[facet, :40]
        if facet > 0:
            value = value + jnp.where(lane < HALO, sent_ref[facet - 1, 40:], 0.0)
        if facet < 7:
            value = value + jnp.where(lane >= 128 - HALO, sent_ref[facet + 1, 40:], 0.0)
        full_ref[facet] = value
    for i in range(4):
        own_ref[i] = full_ref[4 * half + i]
        other_ref[i] = full_ref[4 - 4 * half + i]


def join_kernel(place_ref, own_ref, theirs_ref, out_ref):
    half = place_ref[0]
    out_ref[...] = jnp.zeros((72, 512), F32)
    for ref, start in ((own_ref, 32 * half), (theirs_ref, 32 - 32 * half)):
        rows = pl.ds(pl.multiple_of(start, 32), 40)
        for i in range(4):
            out_ref[rows, 128 * i : 128 * i + 128] += ref[i]


def to_strip(place, partial):
    sent = lax.all_to_all(partial, "chan", 0, 0, tiled=True)
    piece = jax.ShapeDtypeStruct((4, 40, 128), F32)
    own, other = pl.pallas_call(
        to_strip_kernel,
        in_specs=[SMEM, VMEM],
        out_specs=[VMEM] * 2,
        out_shape=[piece, piece],
        scratch_shapes=[pltpu.VMEM((8, 40, 128), F32)],
        compiler_params=params(),
        name="to_strip",
    )(place, sent)
    return pl.pallas_call(
        join_kernel,
        in_specs=[SMEM, VMEM, VMEM],
        out_specs=VMEM,
        out_shape=jax.ShapeDtypeStruct((72, 512), F32),
        compiler_params=params(),
        name="join",
    )(place, own, swapped(other))


def synthesis_of(coef_ref, dual_ref, out_ref, rows_ref):
    lane = lanes_of((40, 128))

    @pl.loop(0, 8)
    def channel(ch):
        for d in range(7):
            rows_ref[d] = jnp.zeros((40, 128), F32)
        fields = [dual_ref[q, ch] for q in range(NBASIS)]

        def add(row, col, weight):
            value = weight(0) * fields[0]
            for q in range(1, NBASIS):
                value = value + weight(q) * fields[q]
            rows_ref[SHIFTS.index(col), HALO + row : HALO + row + 32] += value

        add(0, 0, lambda q: coef_ref[q, 4] + coef_ref[q, 13] + coef_ref[q, 22])
        for level, step in enumerate(STEPS):
            for a in (-1, 0, 1):
                for e in (-1, 0, 1):
                    if a or e:
                        place = 9 * level + 3 * (a + 1) + e + 1
                        add(a * step, e * step, lambda q, place=place: coef_ref[q, place])
        main = rows_ref[0]
        edge = jnp.zeros((40, 128), F32)
        for d, col in enumerate(SHIFTS):
            if col:
                turned = pltpu.roll(rows_ref[d], col % 128, 1)
                inside = (lane >= col) if col > 0 else (lane < 128 + col)
                main = main + jnp.where(inside, turned, 0.0)
                edge = edge + jnp.where(inside, 0.0, turned)
        out_ref[ch, :40] = main
        out_ref[ch, 40:] = edge


def shifted_columns(field_ref, turned_ref):
    lane = lanes_of((40, 128))

    @pl.loop(0, 8)
    def channel(ch):
        main = field_ref[ch, :40]
        edge = field_ref[ch, 40:]
        for d, col in enumerate(SHIFTS):
            if col:
                inside = (lane < 128 - col) if col > 0 else (lane >= -col)
                turned_ref[d, ch] = jnp.where(
                    inside, pltpu.roll(main, -col % 128, 1), pltpu.roll(edge, -col % 128, 1)
                )
            else:
                turned_ref[d, ch] = main


def shrink_all(taps_ref, level_ref, radius_ref, dual_ref, turned_ref, out_ref):
    @pl.loop(0, NBASIS)
    def basis(q):
        for level, step in enumerate(STEPS):

            @pl.when(level_ref[q] == level + 1)
            def at_level():
                low, mid, high = (SHIFTS.index(s) for s in (-step, 0, step))
                squares = jnp.zeros((32, 128), F32)
                for ch in range(8):
                    across = (
                        taps_ref[q, 3] * turned_ref[low, ch]
                        + taps_ref[q, 4] * turned_ref[mid, ch]
                        + taps_ref[q, 5] * turned_ref[high, ch]
                    )
                    value = (
                        taps_ref[q, 0] * across[HALO - step : HALO - step + 32]
                        + taps_ref[q, 1] * across[HALO : HALO + 32]
                        + taps_ref[q, 2] * across[HALO + step : HALO + step + 32]
                    )
                    raised = dual_ref[q, ch] + 0.5 * value
                    out_ref[q, ch] = raised
                    squares = squares + raised * raised
                limit = radius_ref[q]
                scale = limit / jnp.maximum(jnp.sqrt(squares), limit)
                for ch in range(8):
                    out_ref[q, ch] = out_ref[q, ch] * scale


def synthesis_kernel(coef_ref, dual_ref, out_ref, rows_ref):
    synthesis_of(coef_ref, dual_ref, out_ref, rows_ref)


ROWS = pltpu.VMEM((7, 40, 128), F32)
TURNED = pltpu.VMEM((7, 8, 40, 128), F32)
FIELD = pltpu.VMEM((8, 80, 128), F32)


def synthesis(coef, dual):
    return pl.pallas_call(
        synthesis_kernel,
        in_specs=[SMEM, VMEM],
        out_specs=VMEM,
        out_shape=jax.ShapeDtypeStruct((8, 80, 128), F32),
        scratch_shapes=[ROWS],
        compiler_params=params(),
        name="synthesis",
    )(coef, dual)


def middle_kernel(coef_ref, taps_ref, level_ref, radius_ref, dual_ref, before_ref, now_ref,
                  dual_out, part_out, right_out, left_out, field_ref, turned_ref, rows_ref):
    field_ref[...] = 2.0 * now_ref[...] - before_ref[...]
    shifted_columns(field_ref, turned_ref)
    shrink_all(taps_ref, level_ref, radius_ref, dual_ref, turned_ref, dual_out)
    synthesis_of(coef_ref, dual_out, part_out, rows_ref)
    lane = lanes_of((40, 128))
    for ch in range(8):
        main, edge = part_out[ch, :40], part_out[ch, 40:]
        right_out[ch] = jnp.where(lane >= 128 - HALO, main, edge)
        left_out[ch] = jnp.where(lane < HALO, main, edge)


def middle(coef, taps, levels, radius, dual, before, now):
    side = jax.ShapeDtypeStruct((8, 40, 128), F32)
    return pl.pallas_call(
        middle_kernel,
        in_specs=[SMEM] * 4 + [VMEM] * 3,
        out_specs=[VMEM] * 4,
        out_shape=[
            jax.ShapeDtypeStruct((NBASIS, 8, 32, 128), F32),
            jax.ShapeDtypeStruct((8, 80, 128), F32),
            side,
            side,
        ],
        scratch_shapes=[FIELD, TURNED, ROWS],
        compiler_params=params(),
        name="middle",
    )(coef, taps, levels, radius, dual, before, now)


def last_kernel(place_ref, taps_ref, level_ref, radius_ref, dual_ref, now_ref, part_ref, above_ref,
                below_ref, gradient_ref, image_out, dual_out, field_ref, turned_ref):
    chip_row, facet = place_ref[2], place_ref[3]
    lane = lanes_of((40, 128))
    row = lax.broadcasted_iota(jnp.int32, (40, 128), 0) + (32 * chip_row - HALO)
    in_rows = (row >= 0) & (row < 512)
    in_edge = ((lane < HALO) & (facet < 7)) | ((lane >= 128 - HALO) & (facet > 0))
    for ch in range(8):
        for start, keep in ((0, in_rows), (40, in_rows & in_edge)):
            which = start // 40
            field_ref[ch, start : start + 40] = (
                part_ref[ch, start : start + 40] + gradient_ref[ch, start : start + 40]
            )
            field_ref[ch, start : start + 8] += above_ref[ch, which]
            field_ref[ch, start + 32 : start + 40] += below_ref[ch, which]
            now = now_ref[ch, start : start + 40]
            value = jnp.maximum(now - 0.5 * field_ref[ch, start : start + 40], 0.0)
            value = jnp.where(keep, value, 0.0)
            if start == 0:
                image_out[ch] = value[HALO : HALO + 32]
            field_ref[ch, start : start + 40] = 2.0 * value - now
    shifted_columns(field_ref, turned_ref)
    shrink_all(taps_ref, level_ref, radius_ref, dual_ref, turned_ref, dual_out)


def last(place, taps, levels, radius, dual, now, part, above, below, gradient):
    return pl.pallas_call(
        last_kernel,
        in_specs=[SMEM] * 4 + [VMEM] * 6,
        out_specs=[VMEM] * 2,
        out_shape=[
            jax.ShapeDtypeStruct((8, 32, 128), F32),
            jax.ShapeDtypeStruct((NBASIS, 8, 32, 128), F32),
        ],
        scratch_shapes=[FIELD, TURNED],
        compiler_params=params(),
        name="last",
    )(place, taps, levels, radius, dual, now, part, above, below, gradient)


def swapped(value):
    return lax.ppermute(value, "core", [(0, 1), (1, 0)])


def neighbours(value, axis, count, step):
    return lax.ppermute(
        value, axis, [(i, i + step) for i in range(count) if 0 <= i + step < count]
    )


def half_of(value, half, size, dim):
    return lax.dynamic_slice_in_dim(value, half * size, size, dim)


def per_device(
    sky_image,
    dual_coefs,
    phase_screen,
    grid_rows,
    grid_weight,
    visibilities,
    filters,
    level_counts,
    radius,
):
    half = lax.axis_index("core")
    chip = lax.axis_index("y") * 4 + lax.axis_index("x")
    facet = lax.axis_index("chan")
    place = jnp.stack([half, chip, chip * 2 + half, facet]).astype(jnp.int32)
    taps = filters.reshape(NBASIS, 6)
    outer = (filters[:, 0, :, None] * filters[:, 1, None, :]).reshape(NBASIS, 1, 9)
    is_level = (level_counts[:, None] == jnp.arange(1, 4)[None, :]).astype(F32)
    coef = (is_level[:, :, None] * outer).reshape(NBASIS, 27)

    strip = lax.all_to_all(sky_image, "chan", 0, 0, tiled=True)
    own = half_of(strip, half, 4, 0)
    theirs = swapped(half_of(strip, 1 - half, 4, 0))
    first = jnp.where(half == 0, own, theirs)
    second = jnp.where(half == 0, theirs, own)
    strip = jnp.stack([first, second]).transpose(0, 2, 1, 3).reshape(64, 512)
    image = lax.all_to_all(
        jnp.broadcast_to(strip[None], (8, 64, 512)), CHIPS, 0, 0, tiled=True
    ).reshape(512, 512)

    phase = phase_screen[0, 0]
    phase_own = half_of(phase, half, 512, 1)
    phase_other = swapped(half_of(phase, 1 - half, 512, 1))
    weight_own = grid_weight[0, 0]
    weight_other = swapped(weight_own)
    data_own = visibilities[0, 0].reshape(128, 256)
    data_both = jnp.stack([data_own, swapped(data_own)])
    rows_own = grid_rows[0, 0]
    rows_other = swapped(rows_own.astype(F32)).astype(jnp.int32)
    left, right = tables(jnp.stack([rows_own, rows_other]))
    cos, sin = screens(phase_own, phase_other)
    grid = gridding(place, weight_own, weight_other)

    extra = to_strip(place, synthesis(coef, dual_coefs))
    seen = forward(image, cos, sin, left, grid)
    window = lax.dynamic_slice_in_dim(jnp.pad(image, ((HALO, HALO), (0, 0))), 64 * chip, 72, 0)
    before = to_facets(
        place, half_of_rows(window, half), half_of_rows(window, 1 - half)
    )
    sent = backward(place, seen, swapped(seen), data_both, grid, right, cos, sin, extra)
    sent = lax.all_to_all(sent, CHIPS, 0, 0, tiled=True)
    own, other, many = update(place, sent, window)

    image = lax.all_to_all(many, CHIPS, 0, 0, tiled=True).reshape(512, 512)
    now = to_facets(place, own, other)
    seen = forward(image, cos, sin, left, grid)
    dual, part, to_right, to_left = middle(
        coef, taps, level_counts, radius, dual_coefs, before, now
    )
    sent = backward(place, seen, swapped(seen), data_both, grid, right, cos, sin)
    sent = lax.all_to_all(sent, CHIPS, 0, 0, tiled=True)
    from_left = neighbours(to_right, "chan", 8, 1)
    from_right = neighbours(to_left, "chan", 8, -1)
    lane = lanes_of((8, 40, 128))
    main = part[:, :40] + jnp.where(lane < HALO, from_left, 0.0)
    main = main + jnp.where(lane >= 128 - HALO, from_right, 0.0)
    edge = part[:, 40:] + jnp.where(lane >= 128 - HALO, from_left, 0.0)
    edge = edge + jnp.where(lane < HALO, from_right, 0.0)
    both = jnp.stack([main, edge], axis=1)
    above = neighbours(both[:, :, 32:], ("y", "x", "core"), 16, 1)
    below = neighbours(both[:, :, :8], ("y", "x", "core"), 16, -1)
    gradient = to_facets(place, *total_windows(place, sent))
    return tuple(
        last(
            place, taps, level_counts, radius, dual, now, both.reshape(8, 80, 128), above, below, gradient
        )
    )


def half_of_rows(window, half):
    return lax.dynamic_slice_in_dim(window, 32 * half, 40, 0)


def solution(mesh):
    fine = Mesh(mesh.devices.reshape(8, 2, 4, 2), ("chan", "y", "x", "core"))
    rows = ("y", "x", "core")
    placed = (
        P(None, rows, "chan"),
        P(None, None, rows, "chan"),
        P("chan", rows, None, None),
        P("chan", rows, None),
        P("chan", rows, None, None),
        P("chan", rows, None, None, None),
        P(),
        P(),
        P(),
    )
    return jax.shard_map(
        per_device,
        mesh=fine,
        in_specs=placed,
        out_specs=(P(None, rows, "chan"), P(None, None, rows, "chan")),
        check_vma=False,
    )
```

time: 764 us -> 201 us (0.26); the launches traced: 752 us -> 198 us
  matrix products: 347 us -> 0 us
  other arithmetic: 180 us -> 1.49 us
  Pallas kernels: 0 us -> 56.1 us
  between operations: 54.6 us -> 1.05 us
  local copies, waits for them, and re-layouts: 42.1 us -> 14.7 us
  waiting for transfers between devices: 25.1 us -> 50.2 us
  starting transfers between devices: 90 us -> 74.5 us
  blocking collectives: 13.8 us -> 0 us
    dot_general x40 -> x0, matrix products: 347 us -> none  [product(): jnp.einsum(form, left, right, precision=FULL_PRECISION, preferred_element...]
    add x24 -> x1, other arithmetic: 120 us -> 0.01 us  [per_device(): is_level = (level_counts[:, None] == jnp.arange(1, 4)[None, :]).astype(F32)]
    pallas_call x0 -> x17, Pallas kernels: none -> 56.1 us  [the longest x2 10.3 us: forward(): pl.pallas_call(forward_kernel, grid=(2, 512 // tile), in_specs=[pl.BlockS...]
    unnamed x18 -> x0, other arithmetic: 43.1 us -> none
    ppermute x16 -> x15, starting transfers between devices: 60.4 us -> 17.6 us  [the longest x4 16 us: neighbours(): lax.ppermute(value, axis, [(i, i + step) for i in range(count) if 0 <= i...]
    all_to_all x5 -> x9, waiting for transfers between devices: 0.01 us -> 41.2 us  [the longest x2 13.6 us: per_device(): sent = lax.all_to_all(sent, CHIPS, 0, 0, tiled=True)]
    all_to_all x5 -> x9, starting transfers between devices: 29.5 us -> 56.8 us  [the longest x3 20.7 us: to_facets(): return lax.all_to_all(packed, 'chan', 0, 0, tiled=True)]
    ppermute x16 -> x15, waiting for transfers between devices: 25.1 us -> 8.99 us  [the longest x11 7.14 us: swapped(): return lax.ppermute(value, 'core', [(0, 1), (1, 0)])]
  transfers between devices with their start and end apart: 23 -> 24, of which waited for: 9 -> 13; matrix products, arithmetic and copies ran while one was open for 22% -> 3% of each run, Pallas kernels for 0% -> 24%
where the time goes in v1:
time: 201 us; the launch traced here: 198 us
  starting transfers between devices  74.5 us (37%)
  Pallas kernels  56.1 us (28%)
  waiting for transfers between devices  50.2 us (25%)
  local copies, waits for them, and re-layouts  14.7 us (7%)
    all_to_all x3, starting transfers between devices, to_facets(): return lax.all_to_all(packed, 'chan', 0, 0, tiled=True)  20.7 us
    ppermute x4, starting transfers between devices, neighbours(): lax.ppermute(value, axis, [(i, i + step) for i in range(count) if 0 <= i...  16 us
    all_to_all x2, waiting for transfers between devices, per_device(): sent = lax.all_to_all(sent, CHIPS, 0, 0, tiled=True)  13.6 us
    all_to_all x1, waiting for transfers between devices, per_device(): image = lax.all_to_all(many, CHIPS, 0, 0, tiled=True).reshape(512, 512)  10.6 us
    pallas_call x2, Pallas kernels, forward(): pl.pallas_call(forward_kernel, grid=(2, 512 // tile), in_specs=[pl.BlockS...  10.3 us
    unnamed x58, local copies, waits for them, and re-layouts  10.2 us
    pallas_call x2, Pallas kernels, backward(): pl.pallas_call(backward_kernel, grid=(512 // tile,), in_specs=specs, out_...  10 us
    all_to_all x1, waiting for transfers between devices, per_device(): lax.all_to_all(jnp.broadcast_to(strip[None], (8, 64, 512)), CHIPS, 0, 0,...  9.86 us
  transfers between devices with their start and end apart: 24, of which 13 were waited for; matrix products, arithmetic and copies ran while one was open for 3% of the time, Pallas kernels for 24%

profile of v1, /device:TPU:24, one launch (start us, length us, event | category | flops | bytes accessed | tf_op | source)
XLA Modules:
  0.0 198.0 jit_solution(336614839758286276)
XLA Ops:
  0.6 8.3 %all-to-all-start = ((f32[8,32,128]{2,1,0:T(8,128)}), f32[8,32,128]{2,1,0:T(8,128)S(1)}, u32[]{:S(2)}, u32[]{:S(2)}) async-start(f32[8,32,128]{2,1,0:T(8,128)} %param.10), calls=%async_computation | async-start | bytes 262144 | tf_op jit(solution)/shard_map/all_to_all | solution.py:608
  8.9 2.7 %dynamic-slice_bitcast_fusion = (f32[512,512]{1,0:T(8,128)}, f32[512,512]{1,0:T(8,128)S(1)}) fusion(f32[1,1,512,1024]{3,2,1,0:T(8,128)} %param.12, s32[]{:T(128)S(6)} %select_n.64, s32[]{:T(128)S(6)} %select_n.63), kind=kLoop, calls=%fused_computation | loop fusion | bytes 4194312 | tf_op jit(solution)/shard_map/dynamic_slice | solution.py:585
  12.2 2.1 %all-to-all-done = f32[8,32,128]{2,1,0:T(8,128)S(1)} async-done(((f32[8,32,128]{2,1,0:T(8,128)}), f32[8,32,128]{2,1,0:T(8,128)S(1)}, u32[]{:S(2)}, u32[]{:S(2)}) %all-to-all-start) | async-done | bytes 131104 | tf_op jit(solution)/shard_map/all_to_all | solution.py:608
  17.1 5.9 %all-to-all-start.1 = ((f32[8,64,512]{2,1,0:T(8,128)}), f32[8,64,512]{2,1,0:T(8,128)S(1)}, u32[]{:S(2)}, u32[]{:S(2)}) async-start(f32[8,64,512]{2,1,0:T(8,128)} %broadcast_in_dim.24), calls=%async_computation.1 | async-start | bytes 2097152 | tf_op jit(solution)/shard_map/all_to_all | solution.py:614
  23.5 3.4 %synthesis.1 = f32[8,80,128]{2,1,0:T(8,128)S(1)} custom-call(f32[9,27]{1,0:T(8,128)S(1)} %mul.76.coef_ref, f32[9,8,32,128]{3,2,1,0:T(8,128)S(1)} %copy-done.8), custom_call_target="tpu_custom_call" | custom-call | tf_op jit(solution)/shard_map/synthesis/pallas_call | solution.py:492
  27.7 9.9 %all-to-all-done.1 = f32[8,64,512]{2,1,0:T(8,128)S(1)} async-done(((f32[8,64,512]{2,1,0:T(8,128)}), f32[8,64,512]{2,1,0:T(8,128)S(1)}, u32[]{:S(2)}, u32[]{:S(2)}) %all-to-all-start.1) | async-done | bytes 1048608 | tf_op jit(solution)/shard_map/all_to_all | solution.py:614
  37.6 7.2 %all-to-all-start.3 = ((f32[8,80,128]{2,1,0:T(8,128)}), f32[8,80,128]{2,1,0:T(8,128)}, u32[]{:S(2)}, u32[]{:S(2)}) async-start(f32[8,80,128]{2,1,0:T(8,128)} %copy-done.20), calls=%async_computation.3 | async-start | bytes 655360 | tf_op jit(solution)/shard_map/all_to_all | solution.py:381
  45.1 1.8 tables.1
  47.7 6.4 %screens.1 = (f32[2,512,512]{2,1,0:T(8,128)S(1)}, f32[2,512,512]{2,1,0:T(8,128)}) custom-call(f32[512,512]{1,0:T(8,128)S(1)} %get-tuple-element.33.own_ref, f32[512,512]{1,0:T(8,128)} %collective-permute-done.2.other_ref), custom_call_target="tpu_custom_call" | custom-call | tf_op jit(solution)/shard_map/screens/pallas_call | solution.py:76
  54.1 7.1 %gridding.1.grid_ref = bf16[2,2,2,512,256]{4,3,2,1,0:T(8,128)(2,1)S(1)} custom-call(s32[4]{0:T(128)S(1)} %pad_add_fusion.place_ref, f32[1024,256]{1,0:T(8,128)} %bitcast.15.own_ref, f32[1024,256]{1,0:T(8,128)} %collective-permute-done.4.other_ref, bf16[2,2,512,1024]{3,2,1,0:T(8,128)(2,1)} %constant.68.clone.table_ref), custom_call_target="tpu_custom_call" | custom-call | tf_op jit(solution)/shard_map/gridding/pallas_call | solution.py:145
  62.6 5.1 %forward.2.mine_ref = f32[2,128,256]{2,1,0:T(8,128)S(1)} custom-call(f32[512,512]{1,0:T(8,128)S(1)} %bitcast.46, f32[2,512,512]{2,1,0:T(8,128)S(1)} %get-tuple-element.17.cos_ref, f32[2,512,512]{2,1,0:T(8,128)S(1)} %copy-done.5, bf16[2,256,512]{2,1,0:T(8,128)(2,1)S(1)} %get-tuple-element.19.left_ref, bf16[2,2,2,512,256]{4,3,2,1,0:T(8,128)(2,1)} %copy-done), custom_call_target="tpu_custom_call" | custom-call | tf_op jit(solution)/shard_map/forward/pallas_call | solution.py:185
  71.6 4.7 %backward.2 = f32[8,72,512]{2,1,0:T(8,128)S(1)} custom-call(s32[4]{0:T(128)S(1)} %pad_add_fusion.place_ref, f32[2,128,256]{2,1,0:T(8,128)S(1)} %forward.2.mine_ref, f32[2,128,256]{2,1,0:T(8,128)} %collective-permute-done.5.theirs_ref, f32[2,128,256]{2,1,0:T(8,128)S(1)} %pad_maximum_fusion.1.data_ref, bf16[2,2,2,512,256]{4,3,2,1,0:T(8,128)(2,1)S(1)} %copy-done.1, ...), custom_call_target="tpu_custom_call" | custom-call | tf_op jit(solution)/shard_map/backward/pallas_call | solution.py:258
  77.2 4.9 %all-to-all-start.4 = ((f32[8,72,512]{2,1,0:T(8,128)}), f32[8,72,512]{2,1,0:T(8,128)S(1)}, u32[]{:S(2)}, u32[]{:S(2)}) async-start(f32[8,72,512]{2,1,0:T(8,128)} %copy-done.7), calls=%async_computation.4 | async-start | bytes 2359296 | tf_op jit(solution)/shard_map/all_to_all | solution.py:638
  84.9 13.5 %all-to-all-done.4.sent_ref = f32[8,72,512]{2,1,0:T(8,128)S(1)} async-done(((f32[8,72,512]{2,1,0:T(8,128)}), f32[8,72,512]{2,1,0:T(8,128)S(1)}, u32[]{:S(2)}, u32[]{:S(2)}) %all-to-all-start.4) | async-done | bytes 1179680 | tf_op jit(solution)/shard_map/all_to_all | solution.py:638
  98.4 7.2 %all-to-all-start.2 = ((f32[8,80,128]{2,1,0:T(8,128)}), f32[8,80,128]{2,1,0:T(8,128)S(1)}, u32[]{:S(2)}, u32[]{:S(2)}) async-start(f32[8,80,128]{2,1,0:T(8,128)} %to_facets.3), calls=%async_computation.2 | async-start | bytes 655360 | tf_op jit(solution)/shard_map/all_to_all | solution.py:353
  107.3 5.0 %all-to-all-done.2.before_ref = f32[8,80,128]{2,1,0:T(8,128)S(1)} async-done(((f32[8,80,128]{2,1,0:T(8,128)}), f32[8,80,128]{2,1,0:T(8,128)S(1)}, u32[]{:S(2)}, u32[]{:S(2)}) %all-to-all-start.2) | async-done | bytes 327712 | tf_op jit(solution)/shard_map/all_to_all | solution.py:353
  113.1 5.1 %all-to-all-start.6 = ((f32[8,64,512]{2,1,0:T(8,128)}), f32[8,64,512]{2,1,0:T(8,128)S(1)}, u32[]{:S(2)}, u32[]{:S(2)}) async-start(f32[8,64,512]{2,1,0:T(8,128)} %copy-done.23), calls=%async_computation.6 | async-start | bytes 2097152 | tf_op jit(solution)/shard_map/all_to_all | solution.py:641
  120.8 10.6 %all-to-all-done.6 = f32[8,64,512]{2,1,0:T(8,128)S(1)} async-done(((f32[8,64,512]{2,1,0:T(8,128)}), f32[8,64,512]{2,1,0:T(8,128)S(1)}, u32[]{:S(2)}, u32[]{:S(2)}) %all-to-all-start.6) | async-done | bytes 1048608 | tf_op jit(solution)/shard_map/all_to_all | solution.py:641
  131.4 6.3 %all-to-all-start.5 = ((f32[8,80,128]{2,1,0:T(8,128)}), f32[8,80,128]{2,1,0:T(8,128)S(1)}, u32[]{:S(2)}, u32[]{:S(2)}) async-start(f32[8,80,128]{2,1,0:T(8,128)} %copy-done.19), calls=%async_computation.5 | async-start | bytes 655360 | tf_op jit(solution)/shard_map/all_to_all | solution.py:353
  137.8 1.6 copy-done.6
  140.4 5.1 %forward.3.mine_ref = f32[2,128,256]{2,1,0:T(8,128)S(1)} custom-call(f32[512,512]{1,0:T(8,128)S(1)} %bitcast.49, f32[2,512,512]{2,1,0:T(8,128)S(1)} %copy-done.4, f32[2,512,512]{2,1,0:T(8,128)S(1)} %copy-done.6, bf16[2,256,512]{2,1,0:T(8,128)(2,1)S(1)} %copy-done.16, bf16[2,2,2,512,256]{4,3,2,1,0:T(8,128)(2,1)} %copy-done), custom_call_target="tpu_custom_call" | custom-call | tf_op jit(solution)/shard_map/forward/pallas_call | solution.py:185
  145.6 1.5 collective-permute-done.13.theirs_ref
  147.2 5.4 %backward.3 = f32[8,72,512]{2,1,0:T(8,128)} custom-call(s32[4]{0:T(128)S(1)} %pad_add_fusion.place_ref, f32[2,128,256]{2,1,0:T(8,128)S(1)} %forward.3.mine_ref, f32[2,128,256]{2,1,0:T(8,128)S(1)} %collective-permute-done.13.theirs_ref, f32[2,128,256]{2,1,0:T(8,128)S(1)} %copy-done.11, bf16[2,2,2,512,256]{4,3,2,1,0:T(8,128)(2,1)S(1)} %copy-done.2, ...), custom_call_target="tpu_custom_call" | custom-call | tf_op jit(solution)/shard_map/backward/pallas_call | solution.py:258
  152.5 4.6 %all-to-all-start.7 = ((f32[8,72,512]{2,1,0:T(8,128)}), f32[8,72,512]{2,1,0:T(8,128)S(1)}, u32[]{:S(2)}, u32[]{:S(2)}) async-start(f32[8,72,512]{2,1,0:T(8,128)} %backward.3), calls=%async_computation.7 | async-start | bytes 2359296 | tf_op jit(solution)/shard_map/all_to_all | solution.py:648
  157.4 6.8 %middle.1 = (f32[9,8,32,128]{3,2,1,0:T(8,128)S(1)}, f32[8,80,128]{2,1,0:T(8,128)S(1)}, f32[8,40,128]{2,1,0:T(8,128)}, f32[8,40,128]{2,1,0:T(8,128)}) custom-call(f32[9,27]{1,0:T(8,128)S(1)} %mul.76.coef_ref, f32[9,6]{1,0:T(8,128)S(1)} %reshape.77.taps_ref, s32[9]{0:T(128)S(1)} %copy-done.24, f32[9]{0:T(128)S(1)} %copy-done.25, ...), custom_call_target="tpu_custom_call" | custom-call | tf_op jit(solution)/shard_map/middle/pallas_call | solution.py:518
  165.2 2.7 %collective-permute-start.10 = (f32[8,40,128]{2,1,0:T(8,128)}, f32[8,40,128]{2,1,0:T(8,128)S(1)}, u32[]{:S(2)}, u32[]{:S(2)}) collective-permute-start(f32[8,40,128]{2,1,0:T(8,128)} %get-tuple-element.28), channel_id=1, source_target_pairs={{16,0},{32,16},{48,32},{64,48},{80,64},{96,80},{112,96},{17,1},{33... | collective-permute-start | bytes 491528 | tf_op jit(solution)/shard_map/ppermute | solution.py:579
  167.8 5.6 %collective-permute-start.9 = (f32[8,40,128]{2,1,0:T(8,128)}, f32[8,40,128]{2,1,0:T(8,128)S(1)}, u32[]{:S(2)}, u32[]{:S(2)}) collective-permute-start(f32[8,40,128]{2,1,0:T(8,128)} %get-tuple-element.27), channel_id=1, source_target_pairs={{0,16},{16,32},{32,48},{48,64},{64,80},{80,96},{96,112},{1,17},{17... | collective-permute-start | bytes 491528 | tf_op jit(solution)/shard_map/ppermute | solution.py:579
  176.8 7.2 %all-to-all-start.8 = ((f32[8,80,128]{2,1,0:T(8,128)}), f32[8,80,128]{2,1,0:T(8,128)S(1)}, u32[]{:S(2)}, u32[]{:S(2)}) async-start(f32[8,80,128]{2,1,0:T(8,128)} %to_facets.5), calls=%async_computation.8 | async-start | bytes 655360 | tf_op jit(solution)/shard_map/all_to_all | solution.py:353
  184.1 2.1 %collective-permute-start.11 = (f32[8,2,8,128]{3,2,1,0:T(8,128)S(1)}, f32[8,2,8,128]{3,2,1,0:T(8,128)S(1)}, u32[]{:S(2)}, u32[]{:S(2)}) collective-permute-start(f32[8,2,8,128]{3,2,1,0:T(8,128)S(1)} %get-tuple-element.39), channel_id=1, source_target_pairs={{0,1},{1,2},{2,3},{3,4},{4,5},{5,6},{6,7},{7,8},{8,9},{9,10},{10,1... | collective-permute-start | bytes 196616 | tf_op jit(solution)/shard_map/ppermute | solution.py:579
  186.1 5.8 %collective-permute-start.12 = (f32[8,2,8,128]{3,2,1,0:T(8,128)S(1)}, f32[8,2,8,128]{3,2,1,0:T(8,128)S(1)}, u32[]{:S(2)}, u32[]{:S(2)}) collective-permute-start(f32[8,2,8,128]{3,2,1,0:T(8,128)S(1)} %get-tuple-element.38), channel_id=1, source_target_pairs={{1,0},{2,1},{3,2},{4,3},{5,4},{6,5},{7,6},{8,7},{9,8},{10,9},{11,1... | collective-permute-start | bytes 196616 | tf_op jit(solution)/shard_map/ppermute | solution.py:579
  191.9 1.8 collective-permute-done.12.below_ref
  193.8 4.2 %last.1 = (f32[8,32,128]{2,1,0:T(8,128)}, f32[9,8,32,128]{3,2,1,0:T(8,128)}) custom-call(s32[4]{0:T(128)S(1)} %pad_add_fusion.place_ref, f32[9,6]{1,0:T(8,128)S(1)} %reshape.77.taps_ref, s32[9]{0:T(128)S(1)} %copy-done.24, f32[9]{0:T(128)S(1)} %copy-done.25, f32[9,8,32,128]{3,2,1,0:T(8,128)S(1)} %copy-done.22, f32[8,80,128]{2,1,0:T(8,128)S(1)} %all-to-all-done.5.now_ref, ...), custom_call_target="tpu_custom_call" | custom-call | tf_op jit(solution)/shard_map/last/pallas_call | solution.py:560
  (120 shorter events, 25.3 us)
Async XLA Ops:
  0.6 13.7 %all-to-all-start = ((f32[8,32,128]{2,1,0:T(8,128)}), f32[8,32,128]{2,1,0:T(8,128)S(1)}, u32[]{:S(2)}, u32[]{:S(2)}) async-start(f32[8,32,128]{2,1,0:T(8,128)} %param.10), calls=%async_computation | async-start | bytes 262144 | tf_op jit(solution)/shard_map/all_to_all | solution.py:608
  11.6 36.1 %collective-permute-start.2 = (f32[512,512]{1,0:T(8,128)}, f32[512,512]{1,0:T(8,128)}, u32[]{:S(2)}, u32[]{:S(2)}) collective-permute-start(f32[512,512]{1,0:T(8,128)} %get-tuple-element.32), channel_id=1, source_target_pairs={{0,1},{1,0},{2,3},{3,2},{4,5},{5,4},{6,7},{7,6},{8,9},{9,8},{10,11... | collective-permute-start | bytes 3145736 | tf_op jit(solution)/shard_map/ppermute | solution.py:575
  11.6 42.5 %collective-permute-start.4 = (f32[1024,256]{1,0:T(8,128)}, f32[1024,256]{1,0:T(8,128)}, u32[]{:S(2)}, u32[]{:S(2)}) collective-permute-start(f32[1024,256]{1,0:T(8,128)} %bitcast.15.own_ref), channel_id=1, source_target_pairs={{0,1},{1,0},{2,3},{3,2},{4,5},{5,4},{6,7},{7,6},{8,9},{9,8},{10,11... | collective-permute-start | bytes 3145736 | tf_op jit(solution)/shard_map/ppermute | solution.py:575
  12.1 15.6 %collective-permute-start.3 = (f32[64]{0:T(128)S(1)}, f32[64]{0:T(128)S(1)}, u32[]{:S(2)}, u32[]{:S(2)}) collective-permute-start(f32[64]{0:T(128)S(1)} %convert_bitcast_fusion.1), channel_id=1, source_target_pairs={{0,1},{1,0},{2,3},{3,2},{4,5},{5,4},{6,7},{7,6},{8,9},{9,8},{10,11... | collective-permute-start | bytes 776 | tf_op jit(solution)/shard_map/ppermute | solution.py:575
  14.3 1.5 collective-permute-start
  17.1 20.4 %all-to-all-start.1 = ((f32[8,64,512]{2,1,0:T(8,128)}), f32[8,64,512]{2,1,0:T(8,128)S(1)}, u32[]{:S(2)}, u32[]{:S(2)}) async-start(f32[8,64,512]{2,1,0:T(8,128)} %broadcast_in_dim.24), calls=%async_computation.1 | async-start | bytes 2097152 | tf_op jit(solution)/shard_map/all_to_all | solution.py:614
  37.6 30.7 %all-to-all-start.3 = ((f32[8,80,128]{2,1,0:T(8,128)}), f32[8,80,128]{2,1,0:T(8,128)}, u32[]{:S(2)}, u32[]{:S(2)}) async-start(f32[8,80,128]{2,1,0:T(8,128)} %copy-done.20), calls=%async_computation.3 | async-start | bytes 655360 | tf_op jit(solution)/shard_map/all_to_all | solution.py:381
  47.7 14.9 %copy-start.15 = (bf16[2,256,512]{2,1,0:T(8,128)(2,1)}, bf16[2,256,512]{2,1,0:T(8,128)(2,1)S(1)}, u32[]{:S(2)}) copy-start(bf16[2,256,512]{2,1,0:T(8,128)(2,1)S(1)} %get-tuple-element.19.left_ref) | copy-start | bytes 1572868
  54.1 8.5 %copy-start.3 = (f32[2,512,512]{2,1,0:T(8,128)}, f32[2,512,512]{2,1,0:T(8,128)S(1)}, u32[]{:S(2)}) copy-start(f32[2,512,512]{2,1,0:T(8,128)S(1)} %get-tuple-element.17.cos_ref) | copy-start | bytes 6291460
  54.1 8.5 %copy-start.5 = (f32[2,512,512]{2,1,0:T(8,128)S(1)}, f32[2,512,512]{2,1,0:T(8,128)}, u32[]{:S(2)}) copy-start(f32[2,512,512]{2,1,0:T(8,128)} %get-tuple-element.18.sin_ref) | copy-start | bytes 6291460
  62.6 9.0 %copy-start.1 = (bf16[2,2,2,512,256]{4,3,2,1,0:T(8,128)(2,1)S(1)}, bf16[2,2,2,512,256]{4,3,2,1,0:T(8,128)(2,1)}, u32[]{:S(2)}) copy-start(bf16[2,2,2,512,256]{4,3,2,1,0:T(8,128)(2,1)} %copy-done) | copy-start | bytes 6291460
  67.7 3.7 %collective-permute-start.5 = (f32[2,128,256]{2,1,0:T(8,128)S(1)}, f32[2,128,256]{2,1,0:T(8,128)}, u32[]{:S(2)}, u32[]{:S(2)}) collective-permute-start(f32[2,128,256]{2,1,0:T(8,128)S(1)} %forward.2.mine_ref), channel_id=1, source_target_pairs={{0,1},{1,0},{2,3},{3,2},{4,5},{5,4},{6,7},{7,6},{8,9},{9,8},{10,11... | collective-permute-start | bytes 786440 | tf_op jit(solution)/shard_map/ppermute | solution.py:575
  67.8 2.1 %collective-permute-start.6 = (f32[128,256]{1,0:T(8,128)}, f32[128,256]{1,0:T(8,128)}, u32[]{:S(2)}, u32[]{:S(2)}) collective-permute-start(f32[128,256]{1,0:T(8,128)} %bitcast.17), channel_id=1, source_target_pairs={{0,1},{1,0},{2,3},{3,2},{4,5},{5,4},{6,7},{7,6},{8,9},{9,8},{10,11... | collective-permute-start | bytes 393224 | tf_op jit(solution)/shard_map/ppermute | solution.py:575
  69.4 1.5 collective-permute-start.7
  77.2 21.2 %all-to-all-start.4 = ((f32[8,72,512]{2,1,0:T(8,128)}), f32[8,72,512]{2,1,0:T(8,128)S(1)}, u32[]{:S(2)}, u32[]{:S(2)}) async-start(f32[8,72,512]{2,1,0:T(8,128)} %copy-done.7), calls=%async_computation.4 | async-start | bytes 2359296 | tf_op jit(solution)/shard_map/all_to_all | solution.py:638
  82.2 1.4 collective-permute-start.1
  98.4 13.9 %all-to-all-start.2 = ((f32[8,80,128]{2,1,0:T(8,128)}), f32[8,80,128]{2,1,0:T(8,128)S(1)}, u32[]{:S(2)}, u32[]{:S(2)}) async-start(f32[8,80,128]{2,1,0:T(8,128)} %to_facets.3), calls=%async_computation.2 | async-start | bytes 655360 | tf_op jit(solution)/shard_map/all_to_all | solution.py:353
  113.1 24.7 %copy-start.4 = (f32[2,512,512]{2,1,0:T(8,128)S(1)}, f32[2,512,512]{2,1,0:T(8,128)}, u32[]{:S(2)}) copy-start(f32[2,512,512]{2,1,0:T(8,128)} %copy-done.3) | copy-start | bytes 6291460
  113.1 18.3 %all-to-all-start.6 = ((f32[8,64,512]{2,1,0:T(8,128)}), f32[8,64,512]{2,1,0:T(8,128)S(1)}, u32[]{:S(2)}, u32[]{:S(2)}) async-start(f32[8,64,512]{2,1,0:T(8,128)} %copy-done.23), calls=%async_computation.6 | async-start | bytes 2097152 | tf_op jit(solution)/shard_map/all_to_all | solution.py:641
  118.2 1.3 collective-permute-start.8
  131.4 21.1 %all-to-all-start.5 = ((f32[8,80,128]{2,1,0:T(8,128)}), f32[8,80,128]{2,1,0:T(8,128)S(1)}, u32[]{:S(2)}, u32[]{:S(2)}) async-start(f32[8,80,128]{2,1,0:T(8,128)} %copy-done.19), calls=%async_computation.5 | async-start | bytes 655360 | tf_op jit(solution)/shard_map/all_to_all | solution.py:353
  140.4 6.8 %copy-start.11 = (f32[2,128,256]{2,1,0:T(8,128)S(1)}, f32[2,128,256]{2,1,0:T(8,128)}, u32[]{:S(2)}) copy-start(f32[2,128,256]{2,1,0:T(8,128)} %copy-done.10) | copy-start | bytes 786436
  140.4 6.8 %copy-start.14 = (bf16[2,512,256]{2,1,0:T(8,128)(2,1)S(1)}, bf16[2,512,256]{2,1,0:T(8,128)(2,1)}, u32[]{:S(2)}) copy-start(bf16[2,512,256]{2,1,0:T(8,128)(2,1)} %copy-done.12) | copy-start | bytes 1572868
  145.5 1.6 collective-permute-start.13
  152.5 21.0 %all-to-all-start.7 = ((f32[8,72,512]{2,1,0:T(8,128)}), f32[8,72,512]{2,1,0:T(8,128)S(1)}, u32[]{:S(2)}, u32[]{:S(2)}) async-start(f32[8,72,512]{2,1,0:T(8,128)} %backward.3), calls=%async_computation.7 | async-start | bytes 2359296 | tf_op jit(solution)/shard_map/all_to_all | solution.py:648
  165.2 18.8 %collective-permute-start.10 = (f32[8,40,128]{2,1,0:T(8,128)}, f32[8,40,128]{2,1,0:T(8,128)S(1)}, u32[]{:S(2)}, u32[]{:S(2)}) collective-permute-start(f32[8,40,128]{2,1,0:T(8,128)} %get-tuple-element.28), channel_id=1, source_target_pairs={{16,0},{32,16},{48,32},{64,48},{80,64},{96,80},{112,96},{17,1},{33... | collective-permute-start | bytes 491528 | tf_op jit(solution)/shard_map/ppermute | solution.py:579
  167.8 16.1 %collective-permute-start.9 = (f32[8,40,128]{2,1,0:T(8,128)}, f32[8,40,128]{2,1,0:T(8,128)S(1)}, u32[]{:S(2)}, u32[]{:S(2)}) collective-permute-start(f32[8,40,128]{2,1,0:T(8,128)} %get-tuple-element.27), channel_id=1, source_target_pairs={{0,16},{16,32},{32,48},{48,64},{64,80},{80,96},{96,112},{1,17},{17... | collective-permute-start | bytes 491528 | tf_op jit(solution)/shard_map/ppermute | solution.py:579
  174.1 1.4 collective-permute-start.14
  176.8 17.0 %all-to-all-start.8 = ((f32[8,80,128]{2,1,0:T(8,128)}), f32[8,80,128]{2,1,0:T(8,128)S(1)}, u32[]{:S(2)}, u32[]{:S(2)}) async-start(f32[8,80,128]{2,1,0:T(8,128)} %to_facets.5), calls=%async_computation.8 | async-start | bytes 655360 | tf_op jit(solution)/shard_map/all_to_all | solution.py:353
  184.0 9.8 %copy-start.22 = (f32[9,8,32,128]{3,2,1,0:T(8,128)S(1)}, f32[9,8,32,128]{3,2,1,0:T(8,128)}, u32[]{:S(2)}) copy-start(f32[9,8,32,128]{3,2,1,0:T(8,128)} %copy-done.21) | copy-start | bytes 3538948
  184.1 7.9 %collective-permute-start.11 = (f32[8,2,8,128]{3,2,1,0:T(8,128)S(1)}, f32[8,2,8,128]{3,2,1,0:T(8,128)S(1)}, u32[]{:S(2)}, u32[]{:S(2)}) collective-permute-start(f32[8,2,8,128]{3,2,1,0:T(8,128)S(1)} %get-tuple-element.39), channel_id=1, source_target_pairs={{0,1},{1,2},{2,3},{3,4},{4,5},{5,6},{6,7},{7,8},{8,9},{9,10},{10,1... | collective-permute-start | bytes 196616 | tf_op jit(solution)/shard_map/ppermute | solution.py:579
  186.1 7.6 %collective-permute-start.12 = (f32[8,2,8,128]{3,2,1,0:T(8,128)S(1)}, f32[8,2,8,128]{3,2,1,0:T(8,128)S(1)}, u32[]{:S(2)}, u32[]{:S(2)}) collective-permute-start(f32[8,2,8,128]{3,2,1,0:T(8,128)S(1)} %get-tuple-element.38), channel_id=1, source_target_pairs={{1,0},{2,1},{3,2},{4,3},{5,4},{6,5},{7,6},{8,7},{9,8},{10,9},{11,1... | collective-permute-start | bytes 196616 | tf_op jit(solution)/shard_map/ppermute | solution.py:579
  (20 other events, 54.3 us)

commit v2 on v1

v2 whole, which is shorter than its diff:
```python
import functools
import math

import jax
import jax.numpy as jnp
import ml_dtypes
import numpy as np
from jax import lax
from jax.experimental import pallas as pl
from jax.experimental.pallas import tpu as pltpu
from jax.sharding import Mesh
from jax.sharding import PartitionSpec as P

NBASIS = 9
HALO = 4
F32 = jnp.float32
BF16 = jnp.bfloat16
CHIPS = ("y", "x")
STEPS = (1, 2, 4)
SHIFTS = (0, -1, 1, -2, 2, -4, 4)
MIB = 1024 * 1024
SMEM = pl.BlockSpec(memory_space=pltpu.SMEM)
VMEM = pl.BlockSpec(memory_space=pltpu.VMEM)
ANY = pl.BlockSpec(memory_space=pltpu.HBM)


def params(size=16):
    return pltpu.CompilerParams(vmem_limit_bytes=size * MIB)


def where_am_i():
    half = lax.axis_index("core")
    chip = lax.axis_index("y") * 4 + lax.axis_index("x")
    return half, chip, 2 * chip + half, lax.axis_index("chan")


def cost(us):
    return pl.CostEstimate(flops=0, bytes_accessed=int(us * 3.0e6), transcendentals=0)


def sent_out(*shape):
    return pltpu.HBM(shape, F32)


def kept(shape, kind=F32):
    return pltpu.VMEM(shape, kind)


def in_hbm(value):
    return pltpu.with_memory_space_constraint(value, pltpu.HBM)


def parts(value):
    high = value.astype(BF16)
    return high, (value - high.astype(F32)).astype(BF16)


def dot(left, right):
    return jnp.dot(left, right, preferred_element_type=F32)


def dot_t(left, right):
    return lax.dot_general(left, right, (((1,), (1,)), ((), ())), preferred_element_type=F32)


def sincos(angle):
    y = 0.5 * angle
    z = y * y
    s = F32(2.6050929582509915e-06)
    for a in (-0.00019809011067269285, 0.008333050086782038, -0.16666657944392363, 0.9999999956966753):
        s = s * z + F32(a)
    s = s * y
    c = F32(-2.6050510628158867e-07)
    for a in (
        2.476010151557824e-05,
        -0.0013888360127752544,
        0.041666636147634536,
        -0.4999999935511792,
        0.9999999997790222,
    ):
        c = c * z + F32(a)
    return 2.0 * s * c, 1.0 - 2.0 * s * s


def rounded(value):
    return ((value * 32767.0 + 32768.5).astype(jnp.int32) - 32768).astype(jnp.int16)


def widened(value):
    return value.astype(jnp.int32).astype(F32)


def screens_kernel(other_ref, phase_hbm, out_ref, own_ref, sems):
    cols = pl.ds(pl.multiple_of(512 * lax.axis_index("core"), 512), 512)
    copies = [
        pltpu.make_async_copy(
            phase_hbm.at[pl.ds(128 * i, 128), cols], own_ref.at[pl.ds(128 * i, 128)], sems.at[i]
        )
        for i in range(4)
    ]
    for copy in copies:
        copy.start()

    def fill(b, ref, start):
        at = pl.ds(pl.multiple_of(start, 32), 32)
        s, c = sincos(ref[at])
        for part in range(2):
            cols = slice(256 * part, 256 * part + 256)
            out_ref[b, part, 0, at] = rounded(c[:, cols])
            out_ref[b, part, 1, at] = rounded(s[:, cols])

    pl.loop(0, 512, step=32)(functools.partial(fill, 1, other_ref))
    for i in range(4):
        copies[i].wait()
        pl.loop(128 * i, 128 * i + 128, step=32)(functools.partial(fill, 0, own_ref))


def screens(phase, other):
    return pl.pallas_call(
        screens_kernel,
        in_specs=[VMEM, ANY],
        out_specs=VMEM,
        out_shape=kept((2, 2, 2, 512, 256), jnp.int16),
        scratch_shapes=[pltpu.VMEM((512, 512), F32), pltpu.SemaphoreType.DMA((4,))],
        compiler_params=params(),
        cost_estimate=cost(4),
        name="screens",
    )(other, in_hbm(phase))


def tables_kernel(gcol_ref, grow_ref, left_ref, right_ref):
    size = 512
    for b in range(2):
        for turned, g_ref, out_ref in ((0, gcol_ref, left_ref), (1, grow_ref, right_ref)):
            shape = (size, 128) if turned else (128, size)
            n = lax.broadcasted_iota(jnp.int32, shape, 0 if turned else 1)
            picked = lax.broadcasted_iota(jnp.int32, shape, 1 if turned else 0)
            index = (g_ref[b] * n) & (size - 1)
            index = jnp.where(index >= size // 2, index - size, index)
            s, c = sincos(index.astype(F32) * F32(2.0 * math.pi / size))
            high, low = parts(jnp.where(picked < 64, c, -s) * F32(1.0 / math.sqrt(size)))
            if turned:
                out_ref[b, :, :128] = high
                out_ref[b, :, 128:] = low
            else:
                out_ref[b, :128, :] = high
                out_ref[b, 128:, :] = low


def tables(rows_both):
    doubled = jnp.concatenate([rows_both, rows_both], axis=1)
    return pl.pallas_call(
        tables_kernel,
        in_specs=[VMEM, VMEM],
        out_specs=[VMEM, VMEM],
        out_shape=[
            pltpu.HBM((2, 256, 512), BF16),
            pltpu.HBM((2, 512, 256), BF16),
        ],
        compiler_params=params(),
        cost_estimate=cost(2),
        name="tables",
    )(doubled[:, :, None], doubled[:, None, :])


def gridding_kernel(own_ref, other_ref, table_ref, out_ref):
    half = lax.axis_index("core")
    odd = lax.broadcasted_iota(jnp.int32, own_ref.shape, 0) & half
    sign = jnp.where(odd == 1, F32(-1.0), F32(1.0))
    for b, ref in enumerate((own_ref, other_ref)):
        high, low = parts(ref[...] * sign)
        for part in range(2):
            value = dot(table_ref[part, 0], high)
            value = value + dot(table_ref[part, 0], low)
            value = value + dot(table_ref[part, 1], high)
            for cols in range(2):
                kept_high, kept_low = parts(value[256 * cols : 256 * cols + 256])
                out_ref[b, cols, part, 0] = kept_high
                out_ref[b, cols, part, 1] = kept_low


def column_table():
    angle = (np.arange(512)[:, None] * np.arange(1024)[None, :] % 1024) * (2.0 * np.pi / 1024)
    out = np.zeros((2, 2, 512, 1024), ml_dtypes.bfloat16)
    for part, value in enumerate((np.cos(angle) / 32.0, -np.sin(angle) / 32.0)):
        high = value.astype(ml_dtypes.bfloat16)
        out[part, 0] = high
        out[part, 1] = (value - high.astype(np.float64)).astype(ml_dtypes.bfloat16)
    return out


def gridding(own, other):
    return pl.pallas_call(
        gridding_kernel,
        in_specs=[VMEM, VMEM, VMEM],
        out_specs=VMEM,
        out_shape=pltpu.HBM((2, 2, 2, 2, 256, 256), BF16),
        compiler_params=params(),
        cost_estimate=cost(7),
        name="gridding",
    )(own, other, column_table())


def thrice(left, high, low, form):
    count = left.shape[0] // 2
    both = form(left, high)
    return both[:count] + both[count:] + form(left[:count], low)


def fetch(table_hbm, grid_hbm, table_ref, grid_ref, sems, order):
    copies = {}
    for i, key in enumerate(order):
        source, target = (table_hbm, table_ref) if len(key) == 1 else (grid_hbm, grid_ref)
        copies[key] = pltpu.make_async_copy(source.at[key], target.at[key], sems.at[i])
        copies[key].start()
    return copies


FETCHED = [
    pltpu.VMEM((2, 2, 2, 2, 256, 256), BF16),
    pltpu.SemaphoreType.DMA((6,)),
]


def forward_kernel(image_ref, trig_ref, left_hbm, grid_hbm, out_ref, copy_ref, left_ref, grid_ref, sems):
    order = [(0,), (0, 0), (0, 1), (1,), (1, 0), (1, 1)]
    copies = fetch(left_hbm, grid_hbm, left_ref, grid_ref, sems, order)
    for b in range(2):
        total = None
        copies[(b,)].wait()
        left = left_ref[b]
        for part in range(2):
            image = image_ref[:, 256 * part : 256 * part + 256] * F32(1.0 / 32767.0)
            from_real = thrice(left, *parts(widened(trig_ref[b, part, 0]) * image), dot)
            from_imag = thrice(left, *parts(widened(trig_ref[b, part, 1]) * image), dot)
            spectrum = jnp.concatenate(
                [from_real[:64] - from_imag[64:], from_imag[:64] + from_real[64:]], axis=0
            )
            spectrum = jnp.concatenate(parts(spectrum), axis=0)
            copies[(b, part)].wait()
            by_real = thrice(spectrum, grid_ref[b, part, 0, 0], grid_ref[b, part, 0, 1], dot)
            by_imag = thrice(spectrum, grid_ref[b, part, 1, 0], grid_ref[b, part, 1, 1], dot)
            seen = jnp.concatenate(
                [by_real[:64] - by_imag[64:], by_imag[:64] + by_real[64:]], axis=0
            )
            total = seen if total is None else total + seen
        out_ref[b] = total
        copy_ref[b] = total


def forward(image, trig, left, grid):
    return pl.pallas_call(
        forward_kernel,
        in_specs=[VMEM, VMEM, ANY, ANY],
        out_specs=[VMEM] * 2,
        out_shape=[jax.ShapeDtypeStruct((2, 128, 256), F32)] * 2,
        scratch_shapes=[pltpu.VMEM((2, 256, 512), BF16)] + FETCHED,
        compiler_params=params(20),
        cost_estimate=cost(4),
        name="forward",
    )(image, trig, in_hbm(left), in_hbm(grid))


def backward_kernel(mine_ref, theirs_ref, data_ref, trig_ref, *rest):
    extra_ref = rest[0] if len(rest) == 8 else None
    right_hbm, grid_hbm, out_ref, total_ref, right_ref, grid_ref, sems = rest[-7:]
    order = [(0, 0), (0,), (1, 0), (1,), (0, 1), (1, 1)]
    copies = fetch(right_hbm, grid_hbm, right_ref, grid_ref, sems, order)
    total_ref[0:8] = jnp.zeros((8, 512), F32)
    total_ref[520:528] = jnp.zeros((8, 512), F32)
    misfits = [
        jnp.concatenate(parts(mine_ref[b] + theirs_ref[1 - b] - data_ref[b]), axis=0) for b in range(2)
    ]
    for half in range(2):
        cols = slice(256 * half, 256 * half + 256)
        total = None
        for b in range(2):
            copies[(b, half)].wait()
            by_real = thrice(misfits[b], grid_ref[b, half, 0, 0], grid_ref[b, half, 0, 1], dot_t)
            by_imag = thrice(misfits[b], grid_ref[b, half, 1, 0], grid_ref[b, half, 1, 1], dot_t)
            real = by_real[:64] + by_imag[64:]
            imag = by_real[64:] - by_imag[:64]
            spread = jnp.concatenate(
                [jnp.concatenate([real, imag], axis=1), jnp.concatenate([imag, -real], axis=1)],
                axis=0,
            )
            high, low = parts(spread * F32(1.0 / 32767.0))
            if half == 0:
                copies[(b,)].wait()
            right = right_ref[b]
            pulled = dot(right, jnp.concatenate([high, high], axis=0)) + dot(right[:, :128], low)
            part = widened(trig_ref[b, half, 0]) * pulled[:, :256]
            part = part + widened(trig_ref[b, half, 1]) * pulled[:, 256:]
            total = part if total is None else total + part
        total_ref[8:520, cols] = total
        for chip in range(8):
            out_ref[chip, :, cols] = total_ref[64 * chip + 4 : 64 * chip + 76, cols]
    if extra_ref is not None:
        chip = where_am_i()[1]
        out_ref[chip] += extra_ref[...]

        @pl.when(chip > 0)
        def above():
            out_ref[chip - 1, 64:72] += extra_ref[0:8]

        @pl.when(chip < 7)
        def below():
            out_ref[chip + 1, 0:8] += extra_ref[64:72]


def backward(mine, theirs, data, grid, right, trig, extra=None):
    args = [mine, theirs, data, trig] + ([] if extra is None else [extra])
    return pl.pallas_call(
        backward_kernel,
        in_specs=[VMEM] * len(args) + [ANY] * 2,
        out_specs=VMEM,
        out_shape=sent_out(8, 72, 512),
        scratch_shapes=[pltpu.VMEM((528, 512), F32), pltpu.VMEM((2, 512, 256), BF16)] + FETCHED,
        compiler_params=params(20),
        cost_estimate=cost(5),
        name="backward",
    )(*args, in_hbm(right), in_hbm(grid))


def update_kernel(sent_ref, image_ref, own_ref, other_ref, many_ref, scratch_ref):
    half, chip = where_am_i()[:2]
    total = sent_ref[0]
    for source in range(1, 8):
        total = total + sent_ref[source]
    row = lax.broadcasted_iota(jnp.int32, total.shape, 0) + (64 * chip - HALO)
    value = jnp.maximum(image_ref[...] - 0.5 * total, 0.0)
    scratch_ref[...] = jnp.where((row >= 0) & (row < 512), value, 0.0)
    for window_ref, start in ((own_ref, 32 * half), (other_ref, 32 - 32 * half)):
        rows = pl.ds(pl.multiple_of(start, 32), 40)
        window_ref[0] = scratch_ref[rows]
        window_ref[1] = image_ref[rows]
    core = scratch_ref[HALO : HALO + 64]
    for target in range(8):
        many_ref[target] = core


def update(sent, image):
    window = jax.ShapeDtypeStruct((2, 40, 512), F32)
    return pl.pallas_call(
        update_kernel,
        in_specs=[VMEM, VMEM],
        out_specs=[VMEM] * 3,
        out_shape=[window, sent_out(2, 40, 512), sent_out(8, 64, 512)],
        scratch_shapes=[pltpu.VMEM((72, 512), F32)],
        compiler_params=params(),
        cost_estimate=cost(1),
        name="update",
    )(sent, image)


def total_kernel(sent_ref, own_ref, other_ref, scratch_ref):
    half = lax.axis_index("core")
    total = sent_ref[0]
    for source in range(1, 8):
        total = total + sent_ref[source]
    scratch_ref[...] = total
    own_ref[...] = scratch_ref[pl.ds(pl.multiple_of(32 * half, 32), 40)]
    other_ref[...] = scratch_ref[pl.ds(pl.multiple_of(32 - 32 * half, 32), 40)]


def total_windows(sent):
    window = jax.ShapeDtypeStruct((40, 512), F32)
    return pl.pallas_call(
        total_kernel,
        in_specs=[VMEM],
        out_specs=[VMEM] * 2,
        out_shape=[window, sent_out(40, 512)],
        scratch_shapes=[pltpu.VMEM((72, 512), F32)],
        compiler_params=params(),
        cost_estimate=cost(1),
        name="total_windows",
    )(sent)


def lanes_of(shape):
    return lax.broadcasted_iota(jnp.int32, shape, len(shape) - 1)


def packed_edge(edge):
    lane = lanes_of((8, 128))
    out = jnp.zeros((8, 128), F32)
    for g in range(5):
        turned = pltpu.roll(edge[8 * g : 8 * g + 8], 8 * g + HALO, 1)
        out = jnp.where((lane >= 8 * g) & (lane < 8 * g + 8), turned, out)
    return out


def unpacked_edge(packed):
    lane = lanes_of((40, 128))
    turned = [pltpu.roll(packed, 128 - HALO - 8 * g, 1) for g in range(5)]
    inside = (lane < HALO) | (lane >= 128 - HALO)
    return jnp.where(inside, jnp.concatenate(turned, axis=0), 0.0)


def to_facets_kernel(own_ref, theirs_ref, out_ref, full_ref):
    half = lax.axis_index("core")
    full_ref[0] = jnp.zeros((40, 128), F32)
    full_ref[9] = jnp.zeros((40, 128), F32)
    for i in range(4):
        full_ref[1 + 4 * half + i] = own_ref[:, 128 * i : 128 * i + 128]
        full_ref[5 - 4 * half + i] = theirs_ref[:, 128 * i : 128 * i + 128]
    lane = lanes_of((40, 128))
    for facet in range(8):
        out_ref[facet, :40] = full_ref[facet + 1]
        out_ref[facet, 40:] = packed_edge(
            jnp.where(lane < HALO, full_ref[facet + 2], full_ref[facet])
        )


def to_facets(own, other):
    theirs = swapped(other)
    return pl.pallas_call(
        to_facets_kernel,
        in_specs=[VMEM, VMEM],
        out_specs=VMEM,
        out_shape=sent_out(8, 48, 128),
        scratch_shapes=[pltpu.VMEM((10, 40, 128), F32)],
        compiler_params=params(),
        cost_estimate=cost(1),
        name="to_facets",
    )(own, theirs)


def pair_kernel(own_ref, theirs_ref, out_ref, full_ref):
    half = lax.axis_index("core")
    for which in range(2):
        full_ref[which, 0] = jnp.zeros((40, 128), F32)
        full_ref[which, 9] = jnp.zeros((40, 128), F32)
        for i in range(4):
            full_ref[which, 1 + 4 * half + i] = own_ref[which, :, 128 * i : 128 * i + 128]
            full_ref[which, 5 - 4 * half + i] = theirs_ref[which, :, 128 * i : 128 * i + 128]
    lane = lanes_of((40, 128))
    row = lax.broadcasted_iota(jnp.int32, (8, 128), 0)
    for facet in range(8):
        out_ref[facet, :40] = full_ref[0, facet + 1]
        for which in range(2):
            out_ref[facet, 40 + 8 * which : 48 + 8 * which] = packed_edge(
                jnp.where(lane < HALO, full_ref[which, facet + 2], full_ref[which, facet])
            )
        out_ref[facet, 56:64] = jnp.where(
            row < HALO, full_ref[1, facet + 1, 0:8], full_ref[1, facet + 1, 32:40]
        )


def pair_to_facets(own, other):
    theirs = swapped(other)
    return pl.pallas_call(
        pair_kernel,
        in_specs=[VMEM, VMEM],
        out_specs=VMEM,
        out_shape=sent_out(8, 64, 128),
        scratch_shapes=[pltpu.VMEM((2, 10, 40, 128), F32)],
        compiler_params=params(),
        cost_estimate=cost(1),
        name="pair_to_facets",
    )(own, theirs)


def split_kernel(sent_ref, image_own, image_other, term_own, term_other, full_ref):
    half = lax.axis_index("core")
    lane = lanes_of((40, 128))
    edges = [unpacked_edge(sent_ref[facet, 72:80]) for facet in range(8)]
    for facet in range(8):
        value = sent_ref[facet, 32:72]
        if facet > 0:
            value = value + jnp.where(lane < HALO, edges[facet - 1], 0.0)
        if facet < 7:
            value = value + jnp.where(lane >= 128 - HALO, edges[facet + 1], 0.0)
        full_ref[facet] = value
    for i in range(4):
        cols = slice(128 * i, 128 * i + 128)
        image_own[:, cols] = sent_ref[4 * half + i, 0:32]
        image_other[:, cols] = sent_ref[4 - 4 * half + i, 0:32]
        term_own[:, cols] = full_ref[4 * half + i]
        term_other[:, cols] = full_ref[4 - 4 * half + i]


def split(sent):
    return pl.pallas_call(
        split_kernel,
        in_specs=[VMEM],
        out_specs=[VMEM] * 4,
        out_shape=[
            jax.ShapeDtypeStruct((32, 512), F32),
            sent_out(32, 512),
            jax.ShapeDtypeStruct((40, 512), F32),
            sent_out(40, 512),
        ],
        scratch_shapes=[pltpu.VMEM((8, 40, 128), F32)],
        compiler_params=params(),
        cost_estimate=cost(1),
        name="split",
    )(sent)


def spread_kernel(own_ref, theirs_ref, out_ref):
    half = lax.axis_index("core")
    for ref, start in ((own_ref, 32 * half), (theirs_ref, 32 - 32 * half)):
        rows = pl.ds(pl.multiple_of(start, 32), 32)
        value = ref[...]
        for target in range(8):
            out_ref[target, rows] = value


def spread(own, theirs):
    return pl.pallas_call(
        spread_kernel,
        in_specs=[VMEM, VMEM],
        out_specs=VMEM,
        out_shape=sent_out(8, 64, 512),
        compiler_params=params(),
        cost_estimate=cost(1),
        name="spread",
    )(own, theirs)


def join_kernel(own_ref, theirs_ref, out_ref):
    half = lax.axis_index("core")
    out_ref[...] = jnp.zeros((72, 512), F32)
    for ref, start in ((own_ref, 32 * half), (theirs_ref, 32 - 32 * half)):
        rows = pl.ds(pl.multiple_of(start, 32), 40)
        out_ref[rows] += ref[...]


def join(own, theirs):
    return pl.pallas_call(
        join_kernel,
        in_specs=[VMEM, VMEM],
        out_specs=VMEM,
        out_shape=jax.ShapeDtypeStruct((72, 512), F32),
        compiler_params=params(),
        cost_estimate=cost(1),
        name="join",
    )(own, theirs)


def spread_rows(scal_ref, q, step, ch, field, padded_ref, total_ref):
    padded_ref[ch, 8:40] = field
    low, mid, high = HALO + step, HALO, HALO - step
    value = (
        scal_ref[q, 0] * padded_ref[ch, low : low + 40]
        + scal_ref[q, 1] * padded_ref[ch, mid : mid + 40]
        + scal_ref[q, 2] * padded_ref[ch, high : high + 40]
    )
    for e in range(3):
        total_ref[SHIFTS.index((e - 1) * step), ch] += scal_ref[q, 3 + e] * value


def clear(padded_ref, total_ref):
    for ch in range(8):
        padded_ref[ch, 0:8] = jnp.zeros((8, 128), F32)
        padded_ref[ch, 40:48] = jnp.zeros((8, 128), F32)
        for d in range(7):
            total_ref[d, ch] = jnp.zeros((40, 128), F32)


def shift_all(total_ref, ch):
    lane = lanes_of((40, 128))
    main = total_ref[0, ch]
    edge = jnp.zeros((40, 128), F32)
    for d, col in enumerate(SHIFTS):
        if col:
            turned = pltpu.roll(total_ref[d, ch], col % 128, 1)
            inside = (lane >= col) if col > 0 else (lane < 128 + col)
            main = main + jnp.where(inside, turned, 0.0)
            edge = edge + jnp.where(inside, 0.0, turned)
    return main, edge


def shifted_columns(field_ref, turned_ref):
    lane = lanes_of((40, 128))

    @pl.loop(0, 8)
    def channel(ch):
        main = field_ref[ch, :40]
        edge = field_ref[ch, 40:]
        for d, col in enumerate(SHIFTS):
            if col:
                inside = (lane < 128 - col) if col > 0 else (lane >= -col)
                turned_ref[d, ch] = jnp.where(
                    inside, pltpu.roll(main, -col % 128, 1), pltpu.roll(edge, -col % 128, 1)
                )
            else:
                turned_ref[d, ch] = main


def each_level(scal_ref, q, work):
    for level, step in enumerate(STEPS):
        pl.when(scal_ref[q, 7] == F32(level + 1))(functools.partial(work, step))


def shrink(scal_ref, q, at, dual_ref, turned_ref, out_ref, after=None):
    def at_level(step):
        low, mid, high = (SHIFTS.index(s) for s in (-step, 0, step))
        squares = jnp.zeros((32, 128), F32)
        for ch in range(8):
            across = (
                scal_ref[q, 3] * turned_ref[low, ch]
                + scal_ref[q, 4] * turned_ref[mid, ch]
                + scal_ref[q, 5] * turned_ref[high, ch]
            )
            value = (
                scal_ref[q, 0] * across[HALO - step : HALO - step + 32]
                + scal_ref[q, 1] * across[HALO : HALO + 32]
                + scal_ref[q, 2] * across[HALO + step : HALO + step + 32]
            )
            raised = dual_ref[at, ch] + 0.5 * value
            out_ref[at, ch] = raised
            squares = squares + raised * raised
        limit = scal_ref[q, 6]
        scale = limit / jnp.maximum(jnp.sqrt(squares), limit)
        for ch in range(8):
            value = out_ref[at, ch] * scale
            out_ref[at, ch] = value
            if after is not None:
                after(step, ch, value)

    each_level(scal_ref, q, at_level)


class Scalars:
    def __init__(self, filters_ref, level_ref):
        self.filters_ref = filters_ref
        self.level_ref = level_ref

    def __getitem__(self, at):
        q, column = at
        if column == 7:
            return self.level_ref[q].astype(F32)
        return self.filters_ref[q, column // 3, column % 3]


def start_kernel(filters_ref, level_ref, image_ref, dual_ref, out_ref, padded_ref, total_ref):
    step_index = pl.program_id(0)
    scal_ref = Scalars(filters_ref, level_ref)

    @pl.when(step_index == 0)
    def first():
        clear(padded_ref, total_ref)

    @pl.loop(0, 3)
    def basis(i):
        q = 3 * step_index + i

        def at_level(step):
            for ch in range(8):
                spread_rows(scal_ref, q, step, ch, dual_ref[i, ch], padded_ref, total_ref)

        each_level(scal_ref, q, at_level)

    @pl.when(step_index == 2)
    def final():
        for ch in range(8):
            main, edge = shift_all(total_ref, ch)
            out_ref[ch, 0:32] = image_ref[ch]
            out_ref[ch, 32:72] = main
            out_ref[ch, 72:80] = packed_edge(edge)


TURNED = pltpu.VMEM((7, 8, 40, 128), F32)
FIELD = pltpu.VMEM((8, 80, 128), F32)
PADDED = pltpu.VMEM((8, 48, 128), F32)
THIRD = pl.BlockSpec((3, 8, 32, 128), lambda i: (i, 0, 0, 0))


def whole(*shape):
    return pl.BlockSpec(shape, lambda i: (0,) * len(shape))


def start(filters, levels, image, dual):
    return pl.pallas_call(
        start_kernel,
        grid=(3,),
        in_specs=[SMEM, SMEM, whole(8, 32, 128), THIRD],
        out_specs=whole(8, 80, 128),
        out_shape=sent_out(8, 80, 128),
        scratch_shapes=[PADDED, TURNED],
        compiler_params=params(),
        cost_estimate=cost(4),
        name="start",
    )(filters, levels, in_hbm(image), in_hbm(dual))


def middle_kernel(scal_ref, before_ref, pair_ref, dual_ref, dual_out, part_out, right_out, left_out,
                  now_out, field_ref, turned_ref, padded_ref, total_ref):
    step_index = pl.program_id(0)

    @pl.when(step_index == 0)
    def first():
        for ch in range(8):
            main = pair_ref[ch, :40]
            now_out[ch, :40] = main
            now = 2.0 * main
            field_ref[ch, 4:36] = now[4:36] - before_ref[ch]
            outer = pair_ref[ch, 56:64]
            field_ref[ch, 0:4] = now[0:4] - outer[0:4]
            field_ref[ch, 36:40] = now[36:40] - outer[4:8]
            edge = unpacked_edge(pair_ref[ch, 40:48])
            now_out[ch, 40:] = edge
            field_ref[ch, 40:] = 2.0 * edge - unpacked_edge(pair_ref[ch, 48:56])
        shifted_columns(field_ref, turned_ref)
        clear(padded_ref, total_ref)

    @pl.loop(0, 3)
    def basis(i):
        q = 3 * step_index + i

        def after(step, ch, value):
            spread_rows(scal_ref, q, step, ch, value, padded_ref, total_ref)

        shrink(scal_ref, q, i, dual_ref, turned_ref, dual_out, after)

    @pl.when(step_index == 2)
    def final():
        lane = lanes_of((40, 128))
        for ch in range(8):
            main, edge = shift_all(total_ref, ch)
            part_out[ch, :40] = main
            part_out[ch, 40:] = edge
            right_out[ch] = jnp.where(lane >= 128 - HALO, main, edge)
            left_out[ch] = jnp.where(lane < HALO, main, edge)


def middle(scal, dual, before, pair):
    side = jax.ShapeDtypeStruct((8, 40, 128), F32)
    field = sent_out(8, 80, 128)
    return pl.pallas_call(
        middle_kernel,
        grid=(3,),
        in_specs=[SMEM, whole(8, 32, 128), whole(8, 64, 128), THIRD],
        out_specs=[THIRD, whole(8, 80, 128)] + [whole(8, 40, 128)] * 2 + [whole(8, 80, 128)],
        out_shape=[sent_out(NBASIS, 8, 32, 128), field, side, side, field],
        scratch_shapes=[FIELD, TURNED, PADDED, TURNED],
        compiler_params=params(20),
        cost_estimate=cost(6),
        name="middle",
    )(scal, in_hbm(before), in_hbm(pair), in_hbm(dual))


def last_kernel(scal_ref, now_ref, part_ref, above_ref, below_ref, gradient_ref, dual_ref,
                image_out, dual_out, field_ref, turned_ref):
    step_index = pl.program_id(0)

    @pl.when(step_index == 0)
    def first():
        chip_row, facet = where_am_i()[2:]
        lane = lanes_of((40, 128))
        row = lax.broadcasted_iota(jnp.int32, (40, 128), 0) + (32 * chip_row - HALO)
        in_rows = (row >= 0) & (row < 512)
        in_edge = ((lane < HALO) & (facet < 7)) | ((lane >= 128 - HALO) & (facet > 0))
        for ch in range(8):
            for start, keep in ((0, in_rows), (40, in_rows & in_edge)):
                which = start // 40
                gradient = unpacked_edge(gradient_ref[ch, 40:]) if which else gradient_ref[ch, :40]
                field_ref[ch, start : start + 40] = part_ref[ch, start : start + 40] + gradient
                field_ref[ch, start : start + 8] += above_ref[ch, which]
                field_ref[ch, start + 32 : start + 40] += below_ref[ch, which]
                now = now_ref[ch, start : start + 40]
                value = jnp.maximum(now - 0.5 * field_ref[ch, start : start + 40], 0.0)
                value = jnp.where(keep, value, 0.0)
                if start == 0:
                    image_out[ch] = value[HALO : HALO + 32]
                field_ref[ch, start : start + 40] = 2.0 * value - now
        shifted_columns(field_ref, turned_ref)

    @pl.loop(0, 3)
    def basis(i):
        shrink(scal_ref, 3 * step_index + i, i, dual_ref, turned_ref, dual_out)


def last(scal, dual, now, part, above, below, gradient):
    field, side = whole(8, 80, 128), whole(8, 2, 8, 128)
    return pl.pallas_call(
        last_kernel,
        grid=(3,),
        in_specs=[SMEM, field, field, side, side, whole(8, 48, 128), THIRD],
        out_specs=[whole(8, 32, 128), THIRD],
        out_shape=[
            jax.ShapeDtypeStruct((8, 32, 128), F32),
            jax.ShapeDtypeStruct((NBASIS, 8, 32, 128), F32),
        ],
        scratch_shapes=[FIELD, TURNED],
        compiler_params=params(20),
        cost_estimate=cost(4),
        name="last",
    )(scal, now, part, above, below, gradient, dual)


def swapped(value):
    return lax.ppermute(value, "core", [(0, 1), (1, 0)])


def neighbours(value, axis, count, step):
    return lax.ppermute(
        value, axis, [(i, i + step) for i in range(count) if 0 <= i + step < count]
    )


def half_of(value, half, size, dim):
    return lax.dynamic_slice_in_dim(value, half * size, size, dim)


def per_device(
    sky_image,
    dual_coefs,
    phase_screen,
    grid_rows,
    grid_weight,
    visibilities,
    filters,
    level_counts,
    radius,
):
    half, chip = where_am_i()[:2]
    scal = jnp.concatenate(
        [filters.reshape(NBASIS, 6), radius[:, None], level_counts[:, None].astype(F32)], axis=1
    )

    packed, phase = lax.optimization_barrier(
        (start(filters, level_counts, sky_image, dual_coefs), phase_screen[0, 0])
    )
    sent = lax.all_to_all(packed, "chan", 0, 0, tiled=True)

    phase_other = swapped(half_of(phase, 1 - half, 512, 1))
    weight_own = grid_weight[0, 0]
    weight_other = swapped(weight_own)
    data_own = visibilities[0, 0].reshape(128, 256)
    data = jnp.stack([data_own, swapped(data_own)])
    rows_own = grid_rows[0, 0]
    rows_other = swapped(rows_own.astype(F32)).astype(jnp.int32)
    left, right = tables(jnp.stack([rows_own, rows_other]))
    trig = screens(phase, phase_other)
    sent, left, right, trig = lax.optimization_barrier((sent, left, right, trig))

    own, other, term_own, term_other = split(sent)
    image = lax.all_to_all(spread(own, swapped(other)), CHIPS, 0, 0, tiled=True)
    extra = join(term_own, swapped(term_other))
    grid = gridding(weight_own, weight_other)
    image, extra, data = lax.optimization_barrier((image, extra, data))
    image = image.reshape(512, 512)

    seen, seen_copy = forward(image, trig, left, grid)
    window = lax.dynamic_slice_in_dim(jnp.pad(image, ((HALO, HALO), (0, 0))), 64 * chip, 72, 0)
    sent = backward(seen_copy, swapped(seen), data, grid, right, trig, extra)
    sent = lax.all_to_all(sent, CHIPS, 0, 0, tiled=True)
    own, other, many = update(sent, window)

    image = lax.all_to_all(many, CHIPS, 0, 0, tiled=True)
    packed = pair_to_facets(own, other)
    image, packed = lax.optimization_barrier((image, packed))
    image = image.reshape(512, 512)
    pair = lax.all_to_all(packed, "chan", 0, 0, tiled=True)
    seen, seen_copy = forward(image, trig, left, grid)
    dual, part, to_right, to_left, now = middle(scal, dual_coefs, sky_image, pair)
    sent = backward(seen_copy, swapped(seen), data, grid, right, trig)
    sent = lax.all_to_all(sent, CHIPS, 0, 0, tiled=True)
    from_left = neighbours(to_right, "chan", 8, 1)
    from_right = neighbours(to_left, "chan", 8, -1)
    packed = to_facets(*total_windows(sent))
    from_left, from_right = lax.optimization_barrier((from_left, from_right, packed))[:2]
    lane = lanes_of((8, 40, 128))
    main = part[:, :40] + jnp.where(lane < HALO, from_left, 0.0)
    main = main + jnp.where(lane >= 128 - HALO, from_right, 0.0)
    edge = part[:, 40:] + jnp.where(lane >= 128 - HALO, from_left, 0.0)
    edge = edge + jnp.where(lane < HALO, from_right, 0.0)
    both = jnp.stack([main, edge], axis=1)
    above = neighbours(both[:, :, 32:], ("y", "x", "core"), 16, 1)
    below = neighbours(both[:, :, :8], ("y", "x", "core"), 16, -1)
    gradient = lax.all_to_all(packed, "chan", 0, 0, tiled=True)
    return tuple(last(scal, dual, now, both.reshape(8, 80, 128), above, below, gradient))


def solution(mesh):
    fine = Mesh(mesh.devices.reshape(8, 2, 4, 2), ("chan", "y", "x", "core"))
    rows = ("y", "x", "core")
    placed = (
        P(None, rows, "chan"),
        P(None, None, rows, "chan"),
        P("chan", rows, None, None),
        P("chan", rows, None),
        P("chan", rows, None, None),
        P("chan", rows, None, None, None),
        P(),
        P(),
        P(),
    )
    return jax.shard_map(
        per_device,
        mesh=fine,
        in_specs=placed,
        out_specs=(P(None, rows, "chan"), P(None, None, rows, "chan")),
        check_vma=False,
    )
```

time: 201 us -> 172 us (0.86)
  starting transfers between devices: 74.5 us -> 56.6 us
  local copies, waits for them, and re-layouts: 14.7 us -> 9.94 us
  waiting for transfers between devices: 50.2 us -> 47.8 us
    all_to_all x7 -> x5, starting transfers between devices: 47.2 us -> 32.7 us  [the longest x1 8.28 us: per_device(): sent = lax.all_to_all(packed, 'chan', 0, 0, tiled=True)]
    all_to_all x7 -> x5, waiting for transfers between devices: 27.6 us -> 17 us  [the longest x1 11 us: per_device(): image = lax.all_to_all(many, CHIPS, 0, 0, tiled=True)]
    all_to_all x2, waiting for transfers between devices: 13.6 us -> 18.2 us  [per_device(): sent = lax.all_to_all(sent, CHIPS, 0, 0, tiled=True)]
    ppermute x4, starting transfers between devices: 16 us -> 12 us  [neighbours(): lax.ppermute(value, axis, [(i, i + step) for i in range(count) if 0 <= i...]
    ppermute x4, waiting for transfers between devices: 1.85 us -> 5.73 us  [neighbours(): lax.ppermute(value, axis, [(i, i + step) for i in range(count) if 0 <= i...]
    unnamed x58 -> x36, local copies, waits for them, and re-layouts: 10.2 us -> 7.43 us
    pallas_call x16, Pallas kernels: 54.4 us -> 52.2 us  [the longest x2 12.2 us: backward(): pl.pallas_call(backward_kernel, in_specs=[VMEM] * len(args) + [ANY] * 2,...]
    ppermute x11 -> x10, waiting for transfers between devices: 7.14 us -> 6.92 us  [swapped(): return lax.ppermute(value, 'core', [(0, 1), (1, 0)])]
  transfers between devices with their start and end apart: 24 -> 21, of which waited for: 13 -> 11; matrix products, arithmetic and copies ran while one was open for 3% -> 0% of each run, Pallas kernels for 24% -> 17%
where the time goes in v2:
time: 172 us; the launch traced here: 170 us
  starting transfers between devices  56.6 us (33%)
  Pallas kernels  54.8 us (32%)
  waiting for transfers between devices  47.8 us (28%)
  local copies, waits for them, and re-layouts  9.94 us (6%)
    all_to_all x2, waiting for transfers between devices, per_device(): sent = lax.all_to_all(sent, CHIPS, 0, 0, tiled=True)  18.2 us
    pallas_call x2, Pallas kernels, backward(): pl.pallas_call(backward_kernel, in_specs=[VMEM] * len(args) + [ANY] * 2,...  12.2 us
    ppermute x4, starting transfers between devices, neighbours(): lax.ppermute(value, axis, [(i, i + step) for i in range(count) if 0 <= i...  12 us
    all_to_all x1, waiting for transfers between devices, per_device(): image = lax.all_to_all(many, CHIPS, 0, 0, tiled=True)  11 us
    all_to_all x2, starting transfers between devices, per_device(): sent = lax.all_to_all(sent, CHIPS, 0, 0, tiled=True)  10.6 us
    pallas_call x2, Pallas kernels, forward(): pl.pallas_call(forward_kernel, in_specs=[VMEM, VMEM, ANY, ANY], out_specs...  9.22 us
    all_to_all x1, starting transfers between devices, per_device(): sent = lax.all_to_all(packed, 'chan', 0, 0, tiled=True)  8.28 us
    unnamed x36, local copies, waits for them, and re-layouts  7.43 us
  transfers between devices with their start and end apart: 21, of which 11 were waited for; matrix products, arithmetic and copies ran while one was open for 0% of the time, Pallas kernels for 17%

profile of v2, /device:TPU:24, one launch (start us, length us, event | category | flops | bytes accessed | tf_op | source)
XLA Modules:
  0.0 170.4 jit_solution(12032722251336696731)
XLA Ops:
  2.1 4.2 %start.1 = f32[8,80,128]{2,1,0:T(8,128)} custom-call(f32[9,2,3]{2,1,0:T(2,128)S(1)} %copy.26.filters_ref, s32[9]{0:T(128)S(1)} %copy-done.11, f32[8,32,128]{2,1,0:T(8,128)} %before_ref.1, f32[9,8,32,128]{3,2,1,0:T(8,128)} %dual_ref.3), custom_call_target="tpu_custom_call" | custom-call | bytes 12000000 | tf_op jit(solution)/shard_map/start/pallas_call | solution.py:676
  8.2 8.3 %all-to-all-start = ((f32[8,80,128]{2,1,0:T(8,128)}), f32[8,80,128]{2,1,0:T(8,128)S(1)}, u32[]{:S(2)}, u32[]{:S(2)}) async-start(f32[8,80,128]{2,1,0:T(8,128)} %start.1), calls=%async_computation | async-start | bytes 655360 | tf_op jit(solution)/shard_map/all_to_all | solution.py:827
  16.8 2.6 %tables.1 = (bf16[2,256,512]{2,1,0:T(8,128)(2,1)}, bf16[2,512,256]{2,1,0:T(8,128)(2,1)}) custom-call(s32[2,128,1]{2,1,0:T(8,128)S(1)} %copy.24.gcol_ref, s32[2,1,128]{2,1,0:T(1,128)S(1)} %bitcast.29), custom_call_target="tpu_custom_call" | custom-call | bytes 6000000 | tf_op jit(solution)/shard_map/tables/pallas_call | solution.py:152
  19.4 2.8 %screens.1.trig_ref = s16[2,2,2,512,256]{4,3,2,1,0:T(8,128)(2,1)S(1)} custom-call(f32[512,512]{1,0:T(8,128)S(1)} %collective-permute-done.1.other_ref, f32[512,1024]{1,0:T(8,128)} %bitcast.31), custom_call_target="tpu_custom_call" | custom-call | bytes 12000000 | tf_op jit(solution)/shard_map/screens/pallas_call | solution.py:119
  25.0 1.5 collective-permute-done.2.theirs_ref
  27.5 5.9 %all-to-all-start.1 = ((f32[8,64,512]{2,1,0:T(8,128)}), f32[8,64,512]{2,1,0:T(8,128)S(1)}, u32[]{:S(2)}, u32[]{:S(2)}) async-start(f32[8,64,512]{2,1,0:T(8,128)} %spread.1), calls=%async_computation.1 | async-start | bytes 2097152 | tf_op jit(solution)/shard_map/all_to_all | solution.py:841
  34.8 2.2 %copy-done = bf16[2,2,512,1024]{3,2,1,0:T(8,128)(2,1)S(1)} copy-done((bf16[2,2,512,1024]{3,2,1,0:T(8,128)(2,1)S(1)}, bf16[2,2,512,1024]{3,2,1,0:T(8,128)(2,1)}, u32[]{:S(2)}) %copy-start) | copy-done | bytes 4194328
  36.9 6.4 %gridding.1.grid_hbm.rest_2_.rest_1_ = bf16[2,2,2,2,256,256]{5,4,3,2,1,0:T(8,128)(2,1)} custom-call(f32[1024,256]{1,0:T(8,128)} %bitcast.12.own_ref, f32[1024,256]{1,0:T(8,128)} %collective-permute-done.5.other_ref, bf16[2,2,512,1024]{3,2,1,0:T(8,128)(2,1)S(1)} %copy-done), custom_call_target="tpu_custom_call" | custom-call | bytes 21000000 | tf_op jit(solution)/shard_map/gridding/pallas_call | solution.py:193
  43.3 4.6 %all-to-all-done.1 = f32[8,64,512]{2,1,0:T(8,128)S(1)} async-done(((f32[8,64,512]{2,1,0:T(8,128)}), f32[8,64,512]{2,1,0:T(8,128)S(1)}, u32[]{:S(2)}, u32[]{:S(2)}) %all-to-all-start.1) | async-done | bytes 1048608 | tf_op jit(solution)/shard_map/all_to_all | solution.py:841
  47.9 4.3 %forward.2 = (f32[2,128,256]{2,1,0:T(8,128)S(1)}, f32[2,128,256]{2,1,0:T(8,128)S(1)}) custom-call(f32[512,512]{1,0:T(8,128)S(1)} %bitcast.25, s16[2,2,2,512,256]{4,3,2,1,0:T(8,128)(2,1)S(1)} %screens.1.trig_ref, bf16[2,256,512]{2,1,0:T(8,128)(2,1)} %get-tuple-element.46.left_hbm, bf16[2,2,2,2,256,256]{5,4,3,2,1,0:T(8,128)(2,1)} %gridding.1.grid_hbm.rest_2_.rest_1_), custom_call_target="tpu_custom_call" | custom-call | bytes 12000000 | tf_op jit(solution)/shard_map/forward/pallas_call | solution.py:252
  52.5 1.5 collective-permute-done.6.theirs_ref
  54.0 6.1 %backward.2 = f32[8,72,512]{2,1,0:T(8,128)} custom-call(f32[2,128,256]{2,1,0:T(8,128)S(1)} %get-tuple-element.47.mine_ref, f32[2,128,256]{2,1,0:T(8,128)S(1)} %collective-permute-done.6.theirs_ref, f32[2,128,256]{2,1,0:T(8,128)S(1)} %pad_maximum_fusion.1.data_ref, s16[2,2,2,512,256]{4,3,2,1,0:T(8,128)(2,1)S(1)} %screens.1.trig_ref, ...), custom_call_target="tpu_custom_call" | custom-call | bytes 15000000 | tf_op jit(solution)/shard_map/backward/pallas_call | solution.py:313
  60.1 5.6 %all-to-all-start.2 = ((f32[8,72,512]{2,1,0:T(8,128)}), f32[8,72,512]{2,1,0:T(8,128)}, u32[]{:S(2)}, u32[]{:S(2)}) async-start(f32[8,72,512]{2,1,0:T(8,128)} %backward.2), calls=%async_computation.2 | async-start | bytes 2359296 | tf_op jit(solution)/shard_map/all_to_all | solution.py:850
  65.8 16.3 %all-to-all-done.2.sent_ref = f32[8,72,512]{2,1,0:T(8,128)} async-done(((f32[8,72,512]{2,1,0:T(8,128)}), f32[8,72,512]{2,1,0:T(8,128)}, u32[]{:S(2)}, u32[]{:S(2)}) %all-to-all-start.2) | async-done | bytes 1179680 | tf_op jit(solution)/shard_map/all_to_all | solution.py:850
  82.1 2.4 %update.1 = (f32[2,40,512]{2,1,0:T(8,128)S(1)}, f32[2,40,512]{2,1,0:T(8,128)}, f32[8,64,512]{2,1,0:T(8,128)}) custom-call(f32[8,72,512]{2,1,0:T(8,128)} %all-to-all-done.2.sent_ref, f32[72,512]{1,0:T(8,128)S(1)} %pad_dynamic-slice_fusion.image_ref), custom_call_target="tpu_custom_call" | custom-call | bytes 3000000 | tf_op jit(solution)/shard_map/update/pallas_call | solution.py:344
  85.2 5.0 %all-to-all-start.3 = ((f32[8,64,512]{2,1,0:T(8,128)}), f32[8,64,512]{2,1,0:T(8,128)S(1)}, u32[]{:S(2)}, u32[]{:S(2)}) async-start(f32[8,64,512]{2,1,0:T(8,128)} %get-tuple-element.52), calls=%async_computation.3 | async-start | bytes 2097152 | tf_op jit(solution)/shard_map/all_to_all | solution.py:853
  90.1 1.6 collective-permute-done.7.theirs_ref
  93.6 11.0 %all-to-all-done.3 = f32[8,64,512]{2,1,0:T(8,128)S(1)} async-done(((f32[8,64,512]{2,1,0:T(8,128)}), f32[8,64,512]{2,1,0:T(8,128)S(1)}, u32[]{:S(2)}, u32[]{:S(2)}) %all-to-all-start.3) | async-done | bytes 1048608 | tf_op jit(solution)/shard_map/all_to_all | solution.py:853
  104.6 5.0 %forward.3 = (f32[2,128,256]{2,1,0:T(8,128)}, f32[2,128,256]{2,1,0:T(8,128)S(1)}) custom-call(f32[512,512]{1,0:T(8,128)S(1)} %bitcast.27, s16[2,2,2,512,256]{4,3,2,1,0:T(8,128)(2,1)S(1)} %screens.1.trig_ref, bf16[2,256,512]{2,1,0:T(8,128)(2,1)} %get-tuple-element.46.left_hbm, bf16[2,2,2,2,256,256]{5,4,3,2,1,0:T(8,128)(2,1)} %gridding.1.grid_hbm.rest_2_.rest_1_), custom_call_target="tpu_custom_call" | custom-call | bytes 12000000 | tf_op jit(solution)/shard_map/forward/pallas_call | solution.py:252
  110.2 6.2 %all-to-all-start.4 = ((f32[8,64,128]{2,1,0:T(8,128)}), f32[8,64,128]{2,1,0:T(8,128)S(1)}, u32[]{:S(2)}, u32[]{:S(2)}) async-start(f32[8,64,128]{2,1,0:T(8,128)} %pair_to_facets.1), calls=%async_computation.4 | async-start | bytes 524288 | tf_op jit(solution)/shard_map/all_to_all | solution.py:857
  117.4 6.1 %backward.3 = f32[8,72,512]{2,1,0:T(8,128)} custom-call(f32[2,128,256]{2,1,0:T(8,128)S(1)} %copy-done.4, f32[2,128,256]{2,1,0:T(8,128)S(1)} %collective-permute-done.10.theirs_ref, f32[2,128,256]{2,1,0:T(8,128)S(1)} %pad_maximum_fusion.1.data_ref, s16[2,2,2,512,256]{4,3,2,1,0:T(8,128)(2,1)S(1)} %screens.1.trig_ref, ...), custom_call_target="tpu_custom_call" | custom-call | bytes 15000000 | tf_op jit(solution)/shard_map/backward/pallas_call | solution.py:313
  124.2 5.0 %all-to-all-start.5 = ((f32[8,72,512]{2,1,0:T(8,128)}), f32[8,72,512]{2,1,0:T(8,128)S(1)}, u32[]{:S(2)}, u32[]{:S(2)}) async-start(f32[8,72,512]{2,1,0:T(8,128)} %backward.3), calls=%async_computation.5 | async-start | bytes 2359296 | tf_op jit(solution)/shard_map/all_to_all | solution.py:861
  129.6 6.3 %middle.1 = (f32[9,8,32,128]{3,2,1,0:T(8,128)}, f32[8,80,128]{2,1,0:T(8,128)}, f32[8,40,128]{2,1,0:T(8,128)S(1)}, f32[8,40,128]{2,1,0:T(8,128)S(1)}, f32[8,80,128]{2,1,0:T(8,128)}) custom-call(f32[9,8]{1,0:T(8,128)S(1)} %pad_maximum_fusion.2.scal_ref, f32[8,32,128]{2,1,0:T(8,128)} %before_ref.1, f32[8,64,128]{2,1,0:T(8,128)} %copy-done.13, ...), custom_call_target="tpu_custom_call" | custom-call | bytes 18000000 | tf_op jit(solution)/shard_map/middle/pallas_call | solution.py:732
  135.9 4.6 %collective-permute-start.8 = (f32[8,40,128]{2,1,0:T(8,128)S(1)}, f32[8,40,128]{2,1,0:T(8,128)S(1)}, u32[]{:S(2)}, u32[]{:S(2)}) collective-permute-start(f32[8,40,128]{2,1,0:T(8,128)S(1)} %get-tuple-element.58), channel_id=1, source_target_pairs={{0,16},{16,32},{32,48},{48,64},{64,80},{80,96},{96,112},{1,17},{17... | collective-permute-start | bytes 491528 | tf_op jit(solution)/shard_map/ppermute | solution.py:799
  140.6 2.8 %collective-permute-start.9 = (f32[8,40,128]{2,1,0:T(8,128)S(1)}, f32[8,40,128]{2,1,0:T(8,128)S(1)}, u32[]{:S(2)}, u32[]{:S(2)}) collective-permute-start(f32[8,40,128]{2,1,0:T(8,128)S(1)} %get-tuple-element.59), channel_id=1, source_target_pairs={{16,0},{32,16},{48,32},{64,48},{80,64},{96,80},{112,96},{17,1},{33... | collective-permute-start | bytes 491528 | tf_op jit(solution)/shard_map/ppermute | solution.py:799
  143.4 1.9 %all-to-all-done.5.sent_ref = f32[8,72,512]{2,1,0:T(8,128)S(1)} async-done(((f32[8,72,512]{2,1,0:T(8,128)}), f32[8,72,512]{2,1,0:T(8,128)S(1)}, u32[]{:S(2)}, u32[]{:S(2)}) %all-to-all-start.5) | async-done | bytes 1179680 | tf_op jit(solution)/shard_map/all_to_all | solution.py:861
  146.0 1.5 collective-permute-done.11.theirs_ref
  148.3 7.3 %all-to-all-start.6 = ((f32[8,48,128]{2,1,0:T(8,128)}), f32[8,48,128]{2,1,0:T(8,128)S(1)}, u32[]{:S(2)}, u32[]{:S(2)}) async-start(f32[8,48,128]{2,1,0:T(8,128)} %to_facets.1), calls=%async_computation.6 | async-start | bytes 393216 | tf_op jit(solution)/shard_map/all_to_all | solution.py:874
  155.8 2.6 %collective-permute-start.13 = (f32[8,2,8,128]{3,2,1,0:T(8,128)S(1)}, f32[8,2,8,128]{3,2,1,0:T(8,128)S(1)}, u32[]{:S(2)}, u32[]{:S(2)}) collective-permute-start(f32[8,2,8,128]{3,2,1,0:T(8,128)S(1)} %get-tuple-element.70), channel_id=1, source_target_pairs={{1,0},{2,1},{3,2},{4,3},{5,4},{6,5},{7,6},{8,7},{9,8},{10,9},{11,1... | collective-permute-start | bytes 196616 | tf_op jit(solution)/shard_map/ppermute | solution.py:799
  158.3 1.9 %collective-permute-start.12 = (f32[8,2,8,128]{3,2,1,0:T(8,128)S(1)}, f32[8,2,8,128]{3,2,1,0:T(8,128)S(1)}, u32[]{:S(2)}, u32[]{:S(2)}) collective-permute-start(f32[8,2,8,128]{3,2,1,0:T(8,128)S(1)} %get-tuple-element.71), channel_id=1, source_target_pairs={{0,1},{1,2},{2,3},{3,4},{4,5},{5,6},{6,7},{7,8},{8,9},{9,10},{10,1... | collective-permute-start | bytes 196616 | tf_op jit(solution)/shard_map/ppermute | solution.py:799
  160.3 5.7 %collective-permute-done.12.above_ref = f32[8,2,8,128]{3,2,1,0:T(8,128)S(1)} collective-permute-done((f32[8,2,8,128]{3,2,1,0:T(8,128)S(1)}, f32[8,2,8,128]{3,2,1,0:T(8,128)S(1)}, u32[]{:S(2)}, u32[]{:S(2)}) %collective-permute-start.12) | collective-permute-done | bytes 65568 | tf_op jit(solution)/shard_map/ppermute | solution.py:799
  166.0 4.4 %last.1 = (f32[8,32,128]{2,1,0:T(8,128)}, f32[9,8,32,128]{3,2,1,0:T(8,128)}) custom-call(f32[9,8]{1,0:T(8,128)S(1)} %pad_maximum_fusion.2.scal_ref, f32[8,80,128]{2,1,0:T(8,128)S(1)} %copy-done.2, f32[8,80,128]{2,1,0:T(8,128)S(1)} %bitcast.28, f32[8,2,8,128]{3,2,1,0:T(8,128)S(1)} %collective-permute-done.12.above_ref, ...), custom_call_target="tpu_custom_call" | custom-call | bytes 12000000 | tf_op jit(solution)/shard_map/last/pallas_call | solution.py:778
  (81 shorter events, 16.0 us)
Async XLA Ops:
  2.1 5.5 %copy-start.7 = (f32[9,2,3]{2,1,0:T(2,128)}, f32[9,2,3]{2,1,0:T(2,128)S(1)}, u32[]{:S(2)}) copy-start(f32[9,2,3]{2,1,0:T(2,128)S(1)} %copy.26.filters_ref) | copy-start | bytes 652
  6.3 1.4 copy-start.16
  7.6 11.8 %collective-permute-start.1 = (f32[512,512]{1,0:T(8,128)S(1)}, f32[512,512]{1,0:T(8,128)S(1)}, u32[]{:S(2)}, u32[]{:S(2)}) collective-permute-start(f32[512,512]{1,0:T(8,128)S(1)} %constant_dynamic-slice_fusion), channel_id=1, source_target_pairs={{0,1},{1,0},{2,3},{3,2},{4,5},{5,4},{6,7},{7,6},{8,9},{9,8},{10,11... | collective-permute-start | bytes 3145736 | tf_op jit(solution)/shard_map/ppermute | solution.py:795
  7.7 8.8 %collective-permute-start = (f32[64]{0:T(128)S(1)}, f32[64]{0:T(128)S(1)}, u32[]{:S(2)}, u32[]{:S(2)}) collective-permute-start(f32[64]{0:T(128)S(1)} %convert_bitcast_fusion.1), channel_id=1, source_target_pairs={{0,1},{1,0},{2,3},{3,2},{4,5},{5,4},{6,7},{7,6},{8,9},{9,8},{10,11... | collective-permute-start | bytes 776 | tf_op jit(solution)/shard_map/ppermute | solution.py:795
  8.2 15.4 %all-to-all-start = ((f32[8,80,128]{2,1,0:T(8,128)}), f32[8,80,128]{2,1,0:T(8,128)S(1)}, u32[]{:S(2)}, u32[]{:S(2)}) async-start(f32[8,80,128]{2,1,0:T(8,128)} %start.1), calls=%async_computation | async-start | bytes 655360 | tf_op jit(solution)/shard_map/all_to_all | solution.py:827
  16.5 18.3 %collective-permute-start.5 = (f32[1024,256]{1,0:T(8,128)}, f32[1024,256]{1,0:T(8,128)}, u32[]{:S(2)}, u32[]{:S(2)}) collective-permute-start(f32[1024,256]{1,0:T(8,128)} %bitcast.12.own_ref), channel_id=1, source_target_pairs={{0,1},{1,0},{2,3},{3,2},{4,5},{5,4},{6,7},{7,6},{8,9},{9,8},{10,11... | collective-permute-start | bytes 3145736 | tf_op jit(solution)/shard_map/ppermute | solution.py:795
  25.0 1.5 collective-permute-start.2
  27.5 5.9 %copy-start.15 = (f32[1,1,2,64,256]{4,3,2,1,0:T(8,128)S(1)}, f32[1,1,2,64,256]{4,3,2,1,0:T(8,128)}, u32[]{:S(2)}) copy-start(f32[1,1,2,64,256]{4,3,2,1,0:T(8,128)} %param.15) | copy-start | bytes 393220
  27.5 20.5 %all-to-all-start.1 = ((f32[8,64,512]{2,1,0:T(8,128)}), f32[8,64,512]{2,1,0:T(8,128)S(1)}, u32[]{:S(2)}, u32[]{:S(2)}) async-start(f32[8,64,512]{2,1,0:T(8,128)} %spread.1), calls=%async_computation.1 | async-start | bytes 2097152 | tf_op jit(solution)/shard_map/all_to_all | solution.py:841
  33.4 1.3 collective-permute-start.4
  33.4 9.9 %collective-permute-start.3 = (f32[40,512]{1,0:T(8,128)}, f32[40,512]{1,0:T(8,128)S(1)}, u32[]{:S(2)}, u32[]{:S(2)}) collective-permute-start(f32[40,512]{1,0:T(8,128)} %get-tuple-element.43), channel_id=1, source_target_pairs={{0,1},{1,0},{2,3},{3,2},{4,5},{5,4},{6,7},{7,6},{8,9},{9,8},{10,11... | collective-permute-start | bytes 245768 | tf_op jit(solution)/shard_map/ppermute | solution.py:795
  34.8 2.2 %copy-start = (bf16[2,2,512,1024]{3,2,1,0:T(8,128)(2,1)S(1)}, bf16[2,2,512,1024]{3,2,1,0:T(8,128)(2,1)}, u32[]{:S(2)}) copy-start(bf16[2,2,512,1024]{3,2,1,0:T(8,128)(2,1)} %constant.33.clone.table_ref) | copy-start | bytes 12582916
  36.9 6.4 %copy-start.10 = (f32[40,512]{1,0:T(8,128)S(1)}, f32[40,512]{1,0:T(8,128)}, u32[]{:S(2)}) copy-start(f32[40,512]{1,0:T(8,128)} %copy-done.9) | copy-start | bytes 245764
  52.2 1.8 %collective-permute-start.6 = (f32[2,128,256]{2,1,0:T(8,128)S(1)}, f32[2,128,256]{2,1,0:T(8,128)S(1)}, u32[]{:S(2)}, u32[]{:S(2)}) collective-permute-start(f32[2,128,256]{2,1,0:T(8,128)S(1)} %get-tuple-element.48), channel_id=1, source_target_pairs={{0,1},{1,0},{2,3},{3,2},{4,5},{5,4},{6,7},{7,6},{8,9},{9,8},{10,11... | collective-permute-start | bytes 786440 | tf_op jit(solution)/shard_map/ppermute | solution.py:795
  60.1 21.9 %all-to-all-start.2 = ((f32[8,72,512]{2,1,0:T(8,128)}), f32[8,72,512]{2,1,0:T(8,128)}, u32[]{:S(2)}, u32[]{:S(2)}) async-start(f32[8,72,512]{2,1,0:T(8,128)} %backward.2), calls=%async_computation.2 | async-start | bytes 2359296 | tf_op jit(solution)/shard_map/all_to_all | solution.py:850
  85.2 19.4 %all-to-all-start.3 = ((f32[8,64,512]{2,1,0:T(8,128)}), f32[8,64,512]{2,1,0:T(8,128)S(1)}, u32[]{:S(2)}, u32[]{:S(2)}) async-start(f32[8,64,512]{2,1,0:T(8,128)} %get-tuple-element.52), calls=%async_computation.3 | async-start | bytes 2097152 | tf_op jit(solution)/shard_map/all_to_all | solution.py:853
  90.1 1.6 collective-permute-start.7
  110.2 6.2 %collective-permute-start.10 = (f32[2,128,256]{2,1,0:T(8,128)}, f32[2,128,256]{2,1,0:T(8,128)S(1)}, u32[]{:S(2)}, u32[]{:S(2)}) collective-permute-start(f32[2,128,256]{2,1,0:T(8,128)} %get-tuple-element.62), channel_id=1, source_target_pairs={{0,1},{1,0},{2,3},{3,2},{4,5},{5,4},{6,7},{7,6},{8,9},{9,8},{10,11... | collective-permute-start | bytes 786440 | tf_op jit(solution)/shard_map/ppermute | solution.py:795
  110.2 13.3 %all-to-all-start.4 = ((f32[8,64,128]{2,1,0:T(8,128)}), f32[8,64,128]{2,1,0:T(8,128)S(1)}, u32[]{:S(2)}, u32[]{:S(2)}) async-start(f32[8,64,128]{2,1,0:T(8,128)} %pair_to_facets.1), calls=%async_computation.4 | async-start | bytes 524288 | tf_op jit(solution)/shard_map/all_to_all | solution.py:857
  123.5 5.7 %copy-start.8 = (f32[9,2,3]{2,1,0:T(2,128)S(1)}, f32[9,2,3]{2,1,0:T(2,128)}, u32[]{:S(2)}) copy-start(f32[9,2,3]{2,1,0:T(2,128)} %copy-done.7) | copy-start | bytes 652
  123.5 5.8 %copy-start.12 = (s32[9]{0:T(128)S(1)}, s32[9]{0:T(128)}, u32[]{:S(2)}) copy-start(s32[9]{0:T(128)} %level_ref.1) | copy-start | bytes 112
  123.5 5.9 %copy-start.17 = (f32[9]{0:T(128)S(1)}, f32[9]{0:T(128)}, u32[]{:S(2)}) copy-start(f32[9]{0:T(128)} %param.18) | copy-start | bytes 112
  124.2 21.1 %all-to-all-start.5 = ((f32[8,72,512]{2,1,0:T(8,128)}), f32[8,72,512]{2,1,0:T(8,128)S(1)}, u32[]{:S(2)}, u32[]{:S(2)}) async-start(f32[8,72,512]{2,1,0:T(8,128)} %backward.3), calls=%async_computation.5 | async-start | bytes 2359296 | tf_op jit(solution)/shard_map/all_to_all | solution.py:861
  135.9 19.8 %copy-start.14 = (f32[8,80,128]{2,1,0:T(8,128)S(1)}, f32[8,80,128]{2,1,0:T(8,128)}, u32[]{:S(2)}) copy-start(f32[8,80,128]{2,1,0:T(8,128)} %get-tuple-element.57) | copy-start | bytes 983044
  135.9 19.8 %collective-permute-start.8 = (f32[8,40,128]{2,1,0:T(8,128)S(1)}, f32[8,40,128]{2,1,0:T(8,128)S(1)}, u32[]{:S(2)}, u32[]{:S(2)}) collective-permute-start(f32[8,40,128]{2,1,0:T(8,128)S(1)} %get-tuple-element.58), channel_id=1, source_target_pairs={{0,16},{16,32},{32,48},{48,64},{64,80},{80,96},{96,112},{1,17},{17... | collective-permute-start | bytes 491528 | tf_op jit(solution)/shard_map/ppermute | solution.py:799
  140.6 15.1 %collective-permute-start.9 = (f32[8,40,128]{2,1,0:T(8,128)S(1)}, f32[8,40,128]{2,1,0:T(8,128)S(1)}, u32[]{:S(2)}, u32[]{:S(2)}) collective-permute-start(f32[8,40,128]{2,1,0:T(8,128)S(1)} %get-tuple-element.59), channel_id=1, source_target_pairs={{16,0},{32,16},{48,32},{64,48},{80,64},{96,80},{112,96},{17,1},{33... | collective-permute-start | bytes 491528 | tf_op jit(solution)/shard_map/ppermute | solution.py:799
  146.0 1.5 collective-permute-start.11
  148.3 17.7 %copy-start.1 = (f32[9,8,32,128]{3,2,1,0:T(8,128)S(1)}, f32[9,8,32,128]{3,2,1,0:T(8,128)}, u32[]{:S(2)}) copy-start(f32[9,8,32,128]{3,2,1,0:T(8,128)} %get-tuple-element.67.dual_ref) | copy-start | bytes 3538948
  148.3 17.7 %copy-start.2 = (f32[8,80,128]{2,1,0:T(8,128)S(1)}, f32[8,80,128]{2,1,0:T(8,128)}, u32[]{:S(2)}) copy-start(f32[8,80,128]{2,1,0:T(8,128)} %get-tuple-element.56.now_ref) | copy-start | bytes 983044
  148.3 17.7 %all-to-all-start.6 = ((f32[8,48,128]{2,1,0:T(8,128)}), f32[8,48,128]{2,1,0:T(8,128)S(1)}, u32[]{:S(2)}, u32[]{:S(2)}) async-start(f32[8,48,128]{2,1,0:T(8,128)} %to_facets.1), calls=%async_computation.6 | async-start | bytes 393216 | tf_op jit(solution)/shard_map/all_to_all | solution.py:874
  155.8 4.5 %collective-permute-start.13 = (f32[8,2,8,128]{3,2,1,0:T(8,128)S(1)}, f32[8,2,8,128]{3,2,1,0:T(8,128)S(1)}, u32[]{:S(2)}, u32[]{:S(2)}) collective-permute-start(f32[8,2,8,128]{3,2,1,0:T(8,128)S(1)} %get-tuple-element.70), channel_id=1, source_target_pairs={{1,0},{2,1},{3,2},{4,3},{5,4},{6,5},{7,6},{8,7},{9,8},{10,9},{11,1... | collective-permute-start | bytes 196616 | tf_op jit(solution)/shard_map/ppermute | solution.py:799
  158.3 7.7 %collective-permute-start.12 = (f32[8,2,8,128]{3,2,1,0:T(8,128)S(1)}, f32[8,2,8,128]{3,2,1,0:T(8,128)S(1)}, u32[]{:S(2)}, u32[]{:S(2)}) collective-permute-start(f32[8,2,8,128]{3,2,1,0:T(8,128)S(1)} %get-tuple-element.71), channel_id=1, source_target_pairs={{0,1},{1,2},{2,3},{3,4},{4,5},{5,6},{6,7},{7,8},{8,9},{9,10},{10,1... | collective-permute-start | bytes 196616 | tf_op jit(solution)/shard_map/ppermute | solution.py:799
  (7 other events, 5.2 us)

commit v3 on v2

--- a/solution.py
+++ b/solution.py
@@ -13,9 +13,9 @@
 
 NBASIS = 9
 HALO = 4
+CHIPS = ("y", "x")
 F32 = jnp.float32
 BF16 = jnp.bfloat16
-CHIPS = ("y", "x")
 STEPS = (1, 2, 4)
 SHIFTS = (0, -1, 1, -2, 2, -4, 4)
 MIB = 1024 * 1024
@@ -48,6 +48,11 @@
 
 def in_hbm(value):
     return pltpu.with_memory_space_constraint(value, pltpu.HBM)
+
+
+def chip_of(other_y, ahead):
+    y = lax.axis_index("y")
+    return 4 * ((1 - y) if other_y else y) + ((lax.axis_index("x") + ahead) & 3)
 
 
 def parts(value):
@@ -222,15 +227,24 @@
 ]
 
 
-def forward_kernel(image_ref, trig_ref, left_hbm, grid_hbm, out_ref, copy_ref, left_ref, grid_ref, sems):
+def forward_kernel(*refs, windows):
+    pieces, (trig_ref, left_hbm, grid_hbm, out_ref, copy_ref) = refs[: -9 - windows], refs[-9 - windows : -4 - windows]
+    image_ref, left_ref, grid_ref, sems = refs[-4:]
     order = [(0,), (0, 0), (0, 1), (1,), (1, 0), (1, 1)]
     copies = fetch(left_hbm, grid_hbm, left_ref, grid_ref, sems, order)
+    for i, ref in enumerate(pieces):
+        start = pl.multiple_of(64 * chip_of(i // 4, i % 4) + 8, 8)
+        image_ref[pl.ds(start, 64)] = ref[...]
+    if windows:
+        image_ref[0:8] = jnp.zeros((8, 512), F32)
+        image_ref[520:528] = jnp.zeros((8, 512), F32)
+        refs[-5][...] = image_ref[pl.ds(pl.multiple_of(64 * chip_of(0, 0), 64), 80)][4:76]
     for b in range(2):
         total = None
         copies[(b,)].wait()
         left = left_ref[b]
         for part in range(2):
-            image = image_ref[:, 256 * part : 256 * part + 256] * F32(1.0 / 32767.0)
+            image = image_ref[8:520, 256 * part : 256 * part + 256] * F32(1.0 / 32767.0)
             from_real = thrice(left, *parts(widened(trig_ref[b, part, 0]) * image), dot)
             from_imag = thrice(left, *parts(widened(trig_ref[b, part, 1]) * image), dot)
             spectrum = jnp.concatenate(
@@ -248,26 +262,30 @@
         copy_ref[b] = total
 
 
-def forward(image, trig, left, grid):
-    return pl.pallas_call(
-        forward_kernel,
-        in_specs=[VMEM, VMEM, ANY, ANY],
-        out_specs=[VMEM] * 2,
-        out_shape=[jax.ShapeDtypeStruct((2, 128, 256), F32)] * 2,
-        scratch_shapes=[pltpu.VMEM((2, 256, 512), BF16)] + FETCHED,
+def forward(pieces, trig, left, grid, windows):
+    shapes = [jax.ShapeDtypeStruct((2, 128, 256), F32)] * 2
+    if windows:
+        shapes = shapes + [jax.ShapeDtypeStruct((72, 512), F32)]
+    return pl.pallas_call(
+        functools.partial(forward_kernel, windows=windows),
+        in_specs=[VMEM] * (len(pieces) + 1) + [ANY] * 2,
+        out_specs=[VMEM] * len(shapes),
+        out_shape=shapes,
+        scratch_shapes=[pltpu.VMEM((528, 512), F32), pltpu.VMEM((2, 256, 512), BF16)] + FETCHED,
         compiler_params=params(20),
-        cost_estimate=cost(4),
+        cost_estimate=cost(5),
         name="forward",
-    )(image, trig, in_hbm(left), in_hbm(grid))
+    )(*pieces, trig, in_hbm(left), in_hbm(grid))
 
 
 def backward_kernel(mine_ref, theirs_ref, data_ref, trig_ref, *rest):
     extra_ref = rest[0] if len(rest) == 8 else None
-    right_hbm, grid_hbm, out_ref, total_ref, right_ref, grid_ref, sems = rest[-7:]
+    right_hbm, grid_hbm, out_ref = rest[-7:-4]
+    total_ref, right_ref, grid_ref, sems = rest[-4:]
     order = [(0, 0), (0,), (1, 0), (1,), (0, 1), (1, 1)]
     copies = fetch(right_hbm, grid_hbm, right_ref, grid_ref, sems, order)
     total_ref[0:8] = jnp.zeros((8, 512), F32)
-    total_ref[520:528] = jnp.zeros((8, 512), F32)
+    total_ref[512:520] = jnp.zeros((8, 512), F32)
     misfits = [
         jnp.concatenate(parts(mine_ref[b] + theirs_ref[1 - b] - data_ref[b]), axis=0) for b in range(2)
     ]
@@ -292,20 +310,12 @@
             part = widened(trig_ref[b, half, 0]) * pulled[:, :256]
             part = part + widened(trig_ref[b, half, 1]) * pulled[:, 256:]
             total = part if total is None else total + part
-        total_ref[8:520, cols] = total
-        for chip in range(8):
-            out_ref[chip, :, cols] = total_ref[64 * chip + 4 : 64 * chip + 76, cols]
+        total_ref[4:516, cols] = total
     if extra_ref is not None:
-        chip = where_am_i()[1]
-        out_ref[chip] += extra_ref[...]
-
-        @pl.when(chip > 0)
-        def above():
-            out_ref[chip - 1, 64:72] += extra_ref[0:8]
-
-        @pl.when(chip < 7)
-        def below():
-            out_ref[chip + 1, 0:8] += extra_ref[64:72]
+        rows = pl.ds(pl.multiple_of(64 * chip_of(0, 0), 64), 72)
+        total_ref[rows] += extra_ref[...]
+    for chip in range(8):
+        out_ref[chip] = total_ref[64 * chip : 64 * chip + 72]
 
 
 def backward(mine, theirs, data, grid, right, trig, extra=None):
@@ -315,14 +325,14 @@
         in_specs=[VMEM] * len(args) + [ANY] * 2,
         out_specs=VMEM,
         out_shape=sent_out(8, 72, 512),
-        scratch_shapes=[pltpu.VMEM((528, 512), F32), pltpu.VMEM((2, 512, 256), BF16)] + FETCHED,
+        scratch_shapes=[pltpu.VMEM((520, 512), F32), pltpu.VMEM((2, 512, 256), BF16)] + FETCHED,
         compiler_params=params(20),
         cost_estimate=cost(5),
         name="backward",
     )(*args, in_hbm(right), in_hbm(grid))
 
 
-def update_kernel(sent_ref, image_ref, own_ref, other_ref, many_ref, scratch_ref):
+def update_kernel(sent_ref, image_ref, own_ref, other_ref, core_ref, scratch_ref):
     half, chip = where_am_i()[:2]
     total = sent_ref[0]
     for source in range(1, 8):
@@ -334,18 +344,16 @@
         rows = pl.ds(pl.multiple_of(start, 32), 40)
         window_ref[0] = scratch_ref[rows]
         window_ref[1] = image_ref[rows]
-    core = scratch_ref[HALO : HALO + 64]
-    for target in range(8):
-        many_ref[target] = core
+    core_ref[...] = scratch_ref[HALO : HALO + 64]
 
 
 def update(sent, image):
     window = jax.ShapeDtypeStruct((2, 40, 512), F32)
     return pl.pallas_call(
         update_kernel,
-        in_specs=[VMEM, VMEM],
+        in_specs=[VMEM] * 2,
         out_specs=[VMEM] * 3,
-        out_shape=[window, sent_out(2, 40, 512), sent_out(8, 64, 512)],
+        out_shape=[window, window, jax.ShapeDtypeStruct((64, 512), F32)],
         scratch_shapes=[pltpu.VMEM((72, 512), F32)],
         compiler_params=params(),
         cost_estimate=cost(1),
@@ -369,7 +377,7 @@
         total_kernel,
         in_specs=[VMEM],
         out_specs=[VMEM] * 2,
-        out_shape=[window, sent_out(40, 512)],
+        out_shape=[window, window],
         scratch_shapes=[pltpu.VMEM((72, 512), F32)],
         compiler_params=params(),
         cost_estimate=cost(1),
@@ -447,8 +455,7 @@
         )
 
 
-def pair_to_facets(own, other):
-    theirs = swapped(other)
+def pair_to_facets(own, theirs):
     return pl.pallas_call(
         pair_kernel,
         in_specs=[VMEM, VMEM],
@@ -488,7 +495,7 @@
         out_shape=[
             jax.ShapeDtypeStruct((32, 512), F32),
             sent_out(32, 512),
-            jax.ShapeDtypeStruct((40, 512), F32),
+            sent_out(40, 512),
             sent_out(40, 512),
         ],
         scratch_shapes=[pltpu.VMEM((8, 40, 128), F32)],
@@ -498,24 +505,21 @@
     )(sent)
 
 
-def spread_kernel(own_ref, theirs_ref, out_ref):
+def rows_kernel(own_ref, theirs_ref, out_ref):
     half = lax.axis_index("core")
     for ref, start in ((own_ref, 32 * half), (theirs_ref, 32 - 32 * half)):
-        rows = pl.ds(pl.multiple_of(start, 32), 32)
-        value = ref[...]
-        for target in range(8):
-            out_ref[target, rows] = value
-
-
-def spread(own, theirs):
-    return pl.pallas_call(
-        spread_kernel,
+        out_ref[pl.ds(pl.multiple_of(start, 32), 32)] = ref[...]
+
+
+def join_rows(own, theirs):
+    return pl.pallas_call(
+        rows_kernel,
         in_specs=[VMEM, VMEM],
         out_specs=VMEM,
-        out_shape=sent_out(8, 64, 512),
+        out_shape=jax.ShapeDtypeStruct((64, 512), F32),
         compiler_params=params(),
         cost_estimate=cost(1),
-        name="spread",
+        name="join_rows",
     )(own, theirs)
 
 
@@ -536,7 +540,7 @@
         compiler_params=params(),
         cost_estimate=cost(1),
         name="join",
-    )(own, theirs)
+    )(in_hbm(own), theirs)
 
 
 def spread_rows(scal_ref, q, step, ch, field, padded_ref, total_ref):
@@ -632,7 +636,7 @@
         q, column = at
         if column == 7:
             return self.level_ref[q].astype(F32)
-        return self.filters_ref[q, column // 3, column % 3]
+        return self.filters_ref[column % 3, column // 3, q]
 
 
 def start_kernel(filters_ref, level_ref, image_ref, dual_ref, out_ref, padded_ref, total_ref):
@@ -683,7 +687,7 @@
         compiler_params=params(),
         cost_estimate=cost(4),
         name="start",
-    )(filters, levels, in_hbm(image), in_hbm(dual))
+    )(filters, in_hbm(levels), in_hbm(image), in_hbm(dual))
 
 
 def middle_kernel(scal_ref, before_ref, pair_ref, dual_ref, dual_out, part_out, right_out, left_out,
@@ -737,9 +741,9 @@
         out_shape=[sent_out(NBASIS, 8, 32, 128), field, side, side, field],
         scratch_shapes=[FIELD, TURNED, PADDED, TURNED],
         compiler_params=params(20),
-        cost_estimate=cost(6),
+        cost_estimate=cost(7),
         name="middle",
-    )(scal, in_hbm(before), in_hbm(pair), in_hbm(dual))
+    )(scal, in_hbm(before), pair, in_hbm(dual))
 
 
 def last_kernel(scal_ref, now_ref, part_ref, above_ref, below_ref, gradient_ref, dual_ref,
@@ -795,6 +799,22 @@
     return lax.ppermute(value, "core", [(0, 1), (1, 0)])
 
 
+def gathered(value):
+    return gathered_x(value) + gathered_x(across_y(value))
+
+
+def across_y(value):
+    return lax.ppermute(value, "y", [(0, 1), (1, 0)])
+
+
+def along_x(value, step):
+    return lax.ppermute(value, "x", [(i, (i + step) % 4) for i in range(4)])
+
+
+def gathered_x(value):
+    return [value] + [along_x(value, -ahead) for ahead in (1, 2, 3)]
+
+
 def neighbours(value, axis, count, step):
     return lax.ppermute(
         value, axis, [(i, i + step) for i in range(count) if 0 <= i + step < count]
@@ -816,13 +836,13 @@
     level_counts,
     radius,
 ):
-    half, chip = where_am_i()[:2]
+    half = lax.axis_index("core")
     scal = jnp.concatenate(
         [filters.reshape(NBASIS, 6), radius[:, None], level_counts[:, None].astype(F32)], axis=1
     )
 
     packed, phase = lax.optimization_barrier(
-        (start(filters, level_counts, sky_image, dual_coefs), phase_screen[0, 0])
+        (start(filters.transpose(2, 1, 0), level_counts, sky_image, dual_coefs), phase_screen[0, 0])
     )
     sent = lax.all_to_all(packed, "chan", 0, 0, tiled=True)
 
@@ -835,33 +855,32 @@
     rows_other = swapped(rows_own.astype(F32)).astype(jnp.int32)
     left, right = tables(jnp.stack([rows_own, rows_other]))
     trig = screens(phase, phase_other)
-    sent, left, right, trig = lax.optimization_barrier((sent, left, right, trig))
+    grid = gridding(weight_own, weight_other)
+    sent, grid = lax.optimization_barrier((sent, grid))
 
     own, other, term_own, term_other = split(sent)
-    image = lax.all_to_all(spread(own, swapped(other)), CHIPS, 0, 0, tiled=True)
+    strip = join_rows(own, swapped(other))
+    pieces = gathered(strip)
     extra = join(term_own, swapped(term_other))
-    grid = gridding(weight_own, weight_other)
-    image, extra, data = lax.optimization_barrier((image, extra, data))
-    image = image.reshape(512, 512)
-
-    seen, seen_copy = forward(image, trig, left, grid)
-    window = lax.dynamic_slice_in_dim(jnp.pad(image, ((HALO, HALO), (0, 0))), 64 * chip, 72, 0)
+    pieces, extra, data, right = lax.optimization_barrier((pieces, extra, data, right))
+
+    seen, seen_copy, window = forward(pieces, trig, left, grid, True)
     sent = backward(seen_copy, swapped(seen), data, grid, right, trig, extra)
     sent = lax.all_to_all(sent, CHIPS, 0, 0, tiled=True)
-    own, other, many = update(sent, window)
-
-    image = lax.all_to_all(many, CHIPS, 0, 0, tiled=True)
-    packed = pair_to_facets(own, other)
-    image, packed = lax.optimization_barrier((image, packed))
-    image = image.reshape(512, 512)
+    own, other, core = update(sent, window)
+
+    pieces = gathered(core)
+    packed = pair_to_facets(own, swapped(other))
+    packed, pieces[4] = lax.optimization_barrier((packed, pieces[4]))
     pair = lax.all_to_all(packed, "chan", 0, 0, tiled=True)
-    seen, seen_copy = forward(image, trig, left, grid)
+    seen, seen_copy = forward(pieces, trig, left, grid, False)
     dual, part, to_right, to_left, now = middle(scal, dual_coefs, sky_image, pair)
     sent = backward(seen_copy, swapped(seen), data, grid, right, trig)
     sent = lax.all_to_all(sent, CHIPS, 0, 0, tiled=True)
+    windows = total_windows(sent)
     from_left = neighbours(to_right, "chan", 8, 1)
     from_right = neighbours(to_left, "chan", 8, -1)
-    packed = to_facets(*total_windows(sent))
+    packed = to_facets(*windows)
     from_left, from_right = lax.optimization_barrier((from_left, from_right, packed))[:2]
     lane = lanes_of((8, 40, 128))
     main = part[:, :40] + jnp.where(lane < HALO, from_left, 0.0)

time: 172 us -> 164 us (0.953)
  waiting for transfers between devices: 47.8 us -> 16.9 us
  blocking collectives: 0 us -> 21.4 us
  starting transfers between devices: 56.6 us -> 63.1 us
  Pallas kernels: 54.8 us -> 51.6 us
  local copies, waits for them, and re-layouts: 9.94 us -> 7.06 us
    all_to_all x0 -> x1, blocking collectives: none -> 21.4 us  [per_device(): sent = lax.all_to_all(sent, CHIPS, 0, 0, tiled=True)]
    ppermute x0 -> x14, starting transfers between devices: none -> 19.2 us  [the longest x12 16.8 us: along_x(): return lax.ppermute(value, 'x', [(i, (i + step) % 4) for i in range(4)])]
    all_to_all x2 -> x1, waiting for transfers between devices: 18.2 us -> 1.22 us  [per_device(): sent = lax.all_to_all(sent, CHIPS, 0, 0, tiled=True)]
    all_to_all x2 -> x0, waiting for transfers between devices: 15.6 us -> none  [the longest x1 11 us: per_device(): image = lax.all_to_all(many, CHIPS, 0, 0, tiled=True)]
    all_to_all x2 -> x0, starting transfers between devices: 10.9 us -> none  [the longest x1 5.89 us: per_device(): image = lax.all_to_all(spread(own, swapped(other)), CHIPS, 0, 0, tiled=True)]
    ppermute x0 -> x14, waiting for transfers between devices: none -> 9.55 us  [the longest x12 7.77 us: along_x(): return lax.ppermute(value, 'x', [(i, (i + step) % 4) for i in range(4)])]
    all_to_all x2 -> x1, starting transfers between devices: 10.6 us -> 4.37 us  [per_device(): sent = lax.all_to_all(sent, CHIPS, 0, 0, tiled=True)]
    ppermute x4, waiting for transfers between devices: 5.73 us -> 1.85 us  [neighbours(): lax.ppermute(value, axis, [(i, i + step) for i in range(count) if 0 <= i...]
  transfers between devices with their start and end apart: 21 -> 32, of which waited for: 11 -> 13; matrix products, arithmetic and copies ran while one was open for 0% -> 2% of each run, Pallas kernels for 17% -> 19%
where the time goes in v3:
time: 164 us; the launch traced here: 161 us
  starting transfers between devices  63.1 us (38%)
  Pallas kernels  51.6 us (31%)
  blocking collectives  21.4 us (13%)
  waiting for transfers between devices  16.9 us (10%)
  local copies, waits for them, and re-layouts  7.06 us (4%)
    all_to_all x1, blocking collectives, per_device(): sent = lax.all_to_all(sent, CHIPS, 0, 0, tiled=True)  21.4 us
    ppermute x12, starting transfers between devices, along_x(): return lax.ppermute(value, 'x', [(i, (i + step) % 4) for i in range(4)])  16.8 us
    ppermute x4, starting transfers between devices, neighbours(): lax.ppermute(value, axis, [(i, i + step) for i in range(count) if 0 <= i...  15.2 us
    pallas_call x2, Pallas kernels, backward(): pl.pallas_call(backward_kernel, in_specs=[VMEM] * len(args) + [ANY] * 2,...  12.2 us
    pallas_call x2, Pallas kernels, forward(): pl.pallas_call(functools.partial(forward_kernel, windows=windows), in_spe...  9.7 us
    all_to_all x1, starting transfers between devices, per_device(): sent = lax.all_to_all(packed, 'chan', 0, 0, tiled=True)  8.28 us
    ppermute x12, waiting for transfers between devices, along_x(): return lax.ppermute(value, 'x', [(i, (i + step) % 4) for i in range(4)])  7.77 us
    all_to_all x1, starting transfers between devices, per_device(): gradient = lax.all_to_all(packed, 'chan', 0, 0, tiled=True)  7.34 us
  transfers between devices with their start and end apart: 32, of which 13 were waited for; matrix products, arithmetic and copies ran while one was open for 2% of the time, Pallas kernels for 19%

profile of v3, /device:TPU:24, one launch (start us, length us, event | category | flops | bytes accessed | tf_op | source)
XLA Modules:
  0.0 161.4 jit_solution(8384895844257147382)
XLA Ops:
  1.4 4.2 %start.1 = f32[8,80,128]{2,1,0:T(8,128)} custom-call(f32[3,2,9]{2,1,0:T(2,128)S(1)} %bitcast.27, s32[9]{0:T(128)} %level_ref.1, f32[8,32,128]{2,1,0:T(8,128)} %before_ref.1, f32[9,8,32,128]{3,2,1,0:T(8,128)} %dual_ref.3), custom_call_target="tpu_custom_call" | custom-call | bytes 12000000 | tf_op jit(solution)/shard_map/start/pallas_call | solution.py:680
  5.6 2.4 %constant_dynamic-slice_fusion = f32[512,512]{1,0:T(8,128)} fusion(f32[512,1024]{1,0:T(8,128)} %bitcast.29, s32[]{:T(128)S(6)} %select_n.16), kind=kLoop, calls=%fused_computation.17 | loop fusion | bytes 2097156 | tf_op jit(solution)/shard_map/dynamic_slice | solution.py:825
  8.5 8.3 %all-to-all-start = ((f32[8,80,128]{2,1,0:T(8,128)}), f32[8,80,128]{2,1,0:T(8,128)S(1)}, u32[]{:S(2)}, u32[]{:S(2)}) async-start(f32[8,80,128]{2,1,0:T(8,128)} %start.1), calls=%async_computation | async-start | bytes 655360 | tf_op jit(solution)/shard_map/all_to_all | solution.py:847
  16.8 2.2 %copy-done = bf16[2,2,512,1024]{3,2,1,0:T(8,128)(2,1)S(1)} copy-done((bf16[2,2,512,1024]{3,2,1,0:T(8,128)(2,1)S(1)}, bf16[2,2,512,1024]{3,2,1,0:T(8,128)(2,1)}, u32[]{:S(2)}) %copy-start) | copy-done | bytes 4194328
  18.9 6.1 %gridding.1.refs_10_.rest_2_.rest_1_ = bf16[2,2,2,2,256,256]{5,4,3,2,1,0:T(8,128)(2,1)} custom-call(f32[1024,256]{1,0:T(8,128)S(1)} %bitcast.26, f32[1024,256]{1,0:T(8,128)} %collective-permute-done.other_ref, bf16[2,2,512,1024]{3,2,1,0:T(8,128)(2,1)S(1)} %copy-done), custom_call_target="tpu_custom_call" | custom-call | bytes 21000000 | tf_op jit(solution)/shard_map/gridding/pallas_call | solution.py:198
  28.1 2.8 %collective-permute-start.2 = (f32[64,512]{1,0:T(8,128)S(1)}, f32[64,512]{1,0:T(8,128)S(1)}, u32[]{:S(2)}, u32[]{:S(2)}) collective-permute-start(f32[64,512]{1,0:T(8,128)S(1)} %join_rows.1.refs_0_), channel_id=1, source_target_pairs={{0,6},{2,0},{4,2},{6,4},{1,7},{3,1},{5,3},{7,5},{8,14},{10,8},{12,... | collective-permute-start | bytes 393224 | tf_op jit(solution)/shard_map/ppermute | solution.py:811
  33.1 2.8 %collective-permute-start.6 = (f32[64,512]{1,0:T(8,128)}, f32[64,512]{1,0:T(8,128)}, u32[]{:S(2)}, u32[]{:S(2)}) collective-permute-start(f32[64,512]{1,0:T(8,128)} %collective-permute-done.5.refs_4_), channel_id=1, source_target_pairs={{0,6},{2,0},{4,2},{6,4},{1,7},{3,1},{5,3},{7,5},{8,14},{10,8},{12,... | collective-permute-start | bytes 393224 | tf_op jit(solution)/shard_map/ppermute | solution.py:811
  39.0 2.6 %tables.1 = (bf16[2,256,512]{2,1,0:T(8,128)(2,1)}, bf16[2,512,256]{2,1,0:T(8,128)(2,1)}) custom-call(s32[2,128,1]{2,1,0:T(8,128)S(1)} %copy.22.gcol_ref, s32[2,1,128]{2,1,0:T(1,128)S(1)} %bitcast.28), custom_call_target="tpu_custom_call" | custom-call | bytes 6000000 | tf_op jit(solution)/shard_map/tables/pallas_call | solution.py:157
  41.6 2.8 %screens.1.refs_8_.trig_ref = s16[2,2,2,512,256]{4,3,2,1,0:T(8,128)(2,1)S(1)} custom-call(f32[512,512]{1,0:T(8,128)S(1)} %collective-permute-done.12.other_ref, f32[512,1024]{1,0:T(8,128)} %bitcast.30), custom_call_target="tpu_custom_call" | custom-call | bytes 12000000 | tf_op jit(solution)/shard_map/screens/pallas_call | solution.py:124
  47.0 5.5 %forward.2 = (f32[2,128,256]{2,1,0:T(8,128)S(1)}, f32[2,128,256]{2,1,0:T(8,128)S(1)}, f32[72,512]{1,0:T(8,128)S(1)}) custom-call(f32[64,512]{1,0:T(8,128)S(1)} %join_rows.1.refs_0_, f32[64,512]{1,0:T(8,128)S(1)} %copy-done.5, f32[64,512]{1,0:T(8,128)} %collective-permute-done.3.refs_2_, f32[64,512]{1,0:T(8,128)} %collective-permute-done.4.refs_3_, ...), custom_call_target="tpu_custom_call" | custom-call | bytes 15000000 | tf_op jit(solution)/shard_map/forward/pallas_call | solution.py:269
  52.5 1.5 collective-permute-done.13.theirs_ref
  54.0 6.1 %backward.2 = f32[8,72,512]{2,1,0:T(8,128)} custom-call(f32[2,128,256]{2,1,0:T(8,128)S(1)} %get-tuple-element.60.mine_ref, f32[2,128,256]{2,1,0:T(8,128)S(1)} %collective-permute-done.13.theirs_ref, f32[2,128,256]{2,1,0:T(8,128)S(1)} %pad_maximum_fusion.1.data_ref, s16[2,2,2,512,256]{4,3,2,1,0:T(8,128)(2,1)S(1)} %screens.1.refs_8_.trig_ref, ...), custom_call_target="tpu_custom_call" | custom-call | bytes 15000000 | tf_op jit(solution)/shard_map/backward/pallas_call | solution.py:323
  60.2 21.4 %all_to_all.25.sent_ref = f32[8,72,512]{2,1,0:T(8,128)S(1)} all-to-all(f32[8,72,512]{2,1,0:T(8,128)} %backward.2), channel_id=1, replica_groups=mesh['chan'=8,'y'=2,'x'=4,'core'=2] {'y','x'}, dimensions={0} | all-to-all | bytes 2359296 | tf_op jit(solution)/shard_map/all_to_all | solution.py:869
  81.8 1.5 collective-permute-start.15
  84.6 1.6 %collective-permute-start.19 = (f32[64,512]{1,0:T(8,128)S(1)}, f32[64,512]{1,0:T(8,128)S(1)}, u32[]{:S(2)}, u32[]{:S(2)}) collective-permute-start(f32[64,512]{1,0:T(8,128)S(1)} %get-tuple-element.68.refs_0_), channel_id=1, source_target_pairs={{0,4},{2,6},{4,0},{6,2},{1,5},{3,7},{5,1},{7,3},{8,12},{10,14},{12... | collective-permute-start | bytes 393224 | tf_op jit(solution)/shard_map/ppermute | solution.py:811
  87.7 1.8 %collective-permute-start.21 = (f32[64,512]{1,0:T(8,128)S(1)}, f32[64,512]{1,0:T(8,128)S(1)}, u32[]{:S(2)}, u32[]{:S(2)}) collective-permute-start(f32[64,512]{1,0:T(8,128)S(1)} %collective-permute-done.15.refs_4_), channel_id=1, source_target_pairs={{0,6},{2,0},{4,2},{6,4},{1,7},{3,1},{5,3},{7,5},{8,14},{10,8},{12,... | collective-permute-start | bytes 393224 | tf_op jit(solution)/shard_map/ppermute | solution.py:811
  89.7 1.6 %collective-permute-start.22 = (f32[64,512]{1,0:T(8,128)S(1)}, f32[64,512]{1,0:T(8,128)S(1)}, u32[]{:S(2)}, u32[]{:S(2)}) collective-permute-start(f32[64,512]{1,0:T(8,128)S(1)} %collective-permute-done.15.refs_4_), channel_id=1, source_target_pairs={{0,4},{2,6},{4,0},{6,2},{1,5},{3,7},{5,1},{7,3},{8,12},{10,14},{12... | collective-permute-start | bytes 393224 | tf_op jit(solution)/shard_map/ppermute | solution.py:811
  91.3 1.5 collective-permute-start.23
  93.8 3.0 %collective-permute-done.20.refs_3_ = f32[64,512]{1,0:T(8,128)S(1)} collective-permute-done((f32[64,512]{1,0:T(8,128)S(1)}, f32[64,512]{1,0:T(8,128)S(1)}, u32[]{:S(2)}, u32[]{:S(2)}) %collective-permute-start.20) | collective-permute-done | bytes 131104 | tf_op jit(solution)/shard_map/ppermute | solution.py:811
  98.1 1.7 %collective-permute-done.23.refs_7_ = f32[64,512]{1,0:T(8,128)S(1)} collective-permute-done((f32[64,512]{1,0:T(8,128)S(1)}, f32[64,512]{1,0:T(8,128)S(1)}, u32[]{:S(2)}, u32[]{:S(2)}) %collective-permute-start.23) | collective-permute-done | bytes 131104 | tf_op jit(solution)/shard_map/ppermute | solution.py:811
  99.8 4.2 %forward.3 = (f32[2,128,256]{2,1,0:T(8,128)S(1)}, f32[2,128,256]{2,1,0:T(8,128)S(1)}) custom-call(f32[64,512]{1,0:T(8,128)S(1)} %get-tuple-element.68.refs_0_, f32[64,512]{1,0:T(8,128)S(1)} %collective-permute-done.18.refs_1_, f32[64,512]{1,0:T(8,128)S(1)} %collective-permute-done.19.refs_2_, f32[64,512]{1,0:T(8,128)S(1)} %collective-permute-done.20.refs_3_, ...), custom_call_target="tpu_custom_call" | custom-call | bytes 15000000 | tf_op jit(solution)/shard_map/forward/pallas_call | solution.py:269
  104.2 7.2 %all-to-all-start.2 = ((f32[8,64,128]{2,1,0:T(8,128)}), f32[8,64,128]{2,1,0:T(8,128)S(1)}, u32[]{:S(2)}, u32[]{:S(2)}) async-start(f32[8,64,128]{2,1,0:T(8,128)} %pair_to_facets.1), calls=%async_computation.2 | async-start | bytes 524288 | tf_op jit(solution)/shard_map/all_to_all | solution.py:875
  111.4 6.1 %backward.3 = f32[8,72,512]{2,1,0:T(8,128)} custom-call(f32[2,128,256]{2,1,0:T(8,128)S(1)} %get-tuple-element.75.mine_ref, f32[2,128,256]{2,1,0:T(8,128)S(1)} %collective-permute-done.24.theirs_ref, f32[2,128,256]{2,1,0:T(8,128)S(1)} %pad_maximum_fusion.1.data_ref, s16[2,2,2,512,256]{4,3,2,1,0:T(8,128)(2,1)S(1)} %screens.1.refs_8_.trig_ref, ...), custom_call_target="tpu_custom_call" | custom-call | bytes 15000000 | tf_op jit(solution)/shard_map/backward/pallas_call | solution.py:323
  118.1 4.4 %all-to-all-start.3 = ((f32[8,72,512]{2,1,0:T(8,128)}), f32[8,72,512]{2,1,0:T(8,128)S(1)}, u32[]{:S(2)}, u32[]{:S(2)}) async-start(f32[8,72,512]{2,1,0:T(8,128)} %backward.3), calls=%async_computation.3 | async-start | bytes 2359296 | tf_op jit(solution)/shard_map/all_to_all | solution.py:879
  123.0 6.1 %middle.1 = (f32[9,8,32,128]{3,2,1,0:T(8,128)}, f32[8,80,128]{2,1,0:T(8,128)}, f32[8,40,128]{2,1,0:T(8,128)S(1)}, f32[8,40,128]{2,1,0:T(8,128)S(1)}, f32[8,80,128]{2,1,0:T(8,128)}) custom-call(f32[9,8]{1,0:T(8,128)S(1)} %pad_maximum_fusion.2.scal_ref, f32[8,32,128]{2,1,0:T(8,128)} %before_ref.1, f32[8,64,128]{2,1,0:T(8,128)S(1)} %all-to-all-done.2.pair_ref, ...), custom_call_target="tpu_custom_call" | custom-call | bytes 21000000 | tf_op jit(solution)/shard_map/middle/pallas_call | solution.py:736
  129.1 4.8 %collective-permute-start.16 = (f32[8,40,128]{2,1,0:T(8,128)S(1)}, f32[8,40,128]{2,1,0:T(8,128)S(1)}, u32[]{:S(2)}, u32[]{:S(2)}) collective-permute-start(f32[8,40,128]{2,1,0:T(8,128)S(1)} %get-tuple-element.72), channel_id=1, source_target_pairs={{0,16},{16,32},{32,48},{48,64},{64,80},{80,96},{96,112},{1,17},{17... | collective-permute-start | bytes 491528 | tf_op jit(solution)/shard_map/ppermute | solution.py:819
  134.0 2.7 %collective-permute-start.17 = (f32[8,40,128]{2,1,0:T(8,128)S(1)}, f32[8,40,128]{2,1,0:T(8,128)S(1)}, u32[]{:S(2)}, u32[]{:S(2)}) collective-permute-start(f32[8,40,128]{2,1,0:T(8,128)S(1)} %get-tuple-element.73), channel_id=1, source_target_pairs={{16,0},{32,16},{48,32},{64,48},{80,64},{96,80},{112,96},{17,1},{33... | collective-permute-start | bytes 491528 | tf_op jit(solution)/shard_map/ppermute | solution.py:819
  140.1 7.3 %all-to-all-start.4 = ((f32[8,48,128]{2,1,0:T(8,128)}), f32[8,48,128]{2,1,0:T(8,128)S(1)}, u32[]{:S(2)}, u32[]{:S(2)}) async-start(f32[8,48,128]{2,1,0:T(8,128)} %to_facets.1), calls=%async_computation.4 | async-start | bytes 393216 | tf_op jit(solution)/shard_map/all_to_all | solution.py:893
  147.5 1.9 %collective-permute-start.26 = (f32[8,2,8,128]{3,2,1,0:T(8,128)S(1)}, f32[8,2,8,128]{3,2,1,0:T(8,128)S(1)}, u32[]{:S(2)}, u32[]{:S(2)}) collective-permute-start(f32[8,2,8,128]{3,2,1,0:T(8,128)S(1)} %get-tuple-element.85), channel_id=1, source_target_pairs={{0,1},{1,2},{2,3},{3,4},{4,5},{5,6},{6,7},{7,8},{8,9},{9,10},{10,1... | collective-permute-start | bytes 196616 | tf_op jit(solution)/shard_map/ppermute | solution.py:819
  149.5 5.8 %collective-permute-start.27 = (f32[8,2,8,128]{3,2,1,0:T(8,128)S(1)}, f32[8,2,8,128]{3,2,1,0:T(8,128)S(1)}, u32[]{:S(2)}, u32[]{:S(2)}) collective-permute-start(f32[8,2,8,128]{3,2,1,0:T(8,128)S(1)} %get-tuple-element.84), channel_id=1, source_target_pairs={{1,0},{2,1},{3,2},{4,3},{5,4},{6,5},{7,6},{8,7},{9,8},{10,9},{11,1... | collective-permute-start | bytes 196616 | tf_op jit(solution)/shard_map/ppermute | solution.py:819
  155.3 1.8 %collective-permute-done.27.below_ref = f32[8,2,8,128]{3,2,1,0:T(8,128)S(1)} collective-permute-done((f32[8,2,8,128]{3,2,1,0:T(8,128)S(1)}, f32[8,2,8,128]{3,2,1,0:T(8,128)S(1)}, u32[]{:S(2)}, u32[]{:S(2)}) %collective-permute-start.27) | collective-permute-done | bytes 65568 | tf_op jit(solution)/shard_map/ppermute | solution.py:819
  157.1 4.3 %last.1 = (f32[8,32,128]{2,1,0:T(8,128)}, f32[9,8,32,128]{3,2,1,0:T(8,128)}) custom-call(f32[9,8]{1,0:T(8,128)S(1)} %pad_maximum_fusion.2.scal_ref, f32[8,80,128]{2,1,0:T(8,128)S(1)} %copy-done.3, f32[8,80,128]{2,1,0:T(8,128)S(1)} %bitcast.24, f32[8,2,8,128]{3,2,1,0:T(8,128)S(1)} %collective-permute-done.26.above_ref, ...), custom_call_target="tpu_custom_call" | custom-call | bytes 12000000 | tf_op jit(solution)/shard_map/last/pallas_call | solution.py:782
  (97 shorter events, 22.4 us)
Async XLA Ops:
  0.6 16.1 %collective-permute-start = (f32[1024,256]{1,0:T(8,128)}, f32[1024,256]{1,0:T(8,128)}, u32[]{:S(2)}, u32[]{:S(2)}) collective-permute-start(f32[1024,256]{1,0:T(8,128)} %bitcast.25), channel_id=1, source_target_pairs={{0,1},{1,0},{2,3},{3,2},{4,5},{5,4},{6,7},{7,6},{8,9},{9,8},{10,11... | collective-permute-start | bytes 3145736 | tf_op jit(solution)/shard_map/ppermute | solution.py:799
  8.0 23.8 %collective-permute-start.12 = (f32[512,512]{1,0:T(8,128)}, f32[512,512]{1,0:T(8,128)S(1)}, u32[]{:S(2)}, u32[]{:S(2)}) collective-permute-start(f32[512,512]{1,0:T(8,128)} %constant_dynamic-slice_fusion), channel_id=1, source_target_pairs={{0,1},{1,0},{2,3},{3,2},{4,5},{5,4},{6,7},{7,6},{8,9},{9,8},{10,11... | collective-permute-start | bytes 3145736 | tf_op jit(solution)/shard_map/ppermute | solution.py:799
  8.5 16.6 %all-to-all-start = ((f32[8,80,128]{2,1,0:T(8,128)}), f32[8,80,128]{2,1,0:T(8,128)S(1)}, u32[]{:S(2)}, u32[]{:S(2)}) async-start(f32[8,80,128]{2,1,0:T(8,128)} %start.1), calls=%async_computation | async-start | bytes 655360 | tf_op jit(solution)/shard_map/all_to_all | solution.py:847
  25.8 1.5 collective-permute-start.1
  25.8 5.1 %collective-permute-start.11 = (f32[64]{0:T(128)S(1)}, f32[64]{0:T(128)S(1)}, u32[]{:S(2)}, u32[]{:S(2)}) collective-permute-start(f32[64]{0:T(128)S(1)} %convert_bitcast_fusion.1), channel_id=1, source_target_pairs={{0,1},{1,0},{2,3},{3,2},{4,5},{5,4},{6,7},{7,6},{8,9},{9,8},{10,11... | collective-permute-start | bytes 776 | tf_op jit(solution)/shard_map/ppermute | solution.py:799
  26.4 4.6 %collective-permute-start.10 = (f32[128,256]{1,0:T(8,128)S(1)}, f32[128,256]{1,0:T(8,128)S(1)}, u32[]{:S(2)}, u32[]{:S(2)}) collective-permute-start(f32[128,256]{1,0:T(8,128)S(1)} %bitcast.31), channel_id=1, source_target_pairs={{0,1},{1,0},{2,3},{3,2},{4,5},{5,4},{6,7},{7,6},{8,9},{9,8},{10,11... | collective-permute-start | bytes 393224 | tf_op jit(solution)/shard_map/ppermute | solution.py:799
  27.3 5.7 %collective-permute-start.5 = (f32[64,512]{1,0:T(8,128)S(1)}, f32[64,512]{1,0:T(8,128)}, u32[]{:S(2)}, u32[]{:S(2)}) collective-permute-start(f32[64,512]{1,0:T(8,128)S(1)} %join_rows.1.refs_0_), channel_id=1, source_target_pairs={{0,8},{8,0},{1,9},{9,1},{2,10},{10,2},{3,11},{11,3},{4,12},{12,4},... | collective-permute-start | bytes 393224 | tf_op jit(solution)/shard_map/ppermute | solution.py:807
  28.1 9.1 %collective-permute-start.2 = (f32[64,512]{1,0:T(8,128)S(1)}, f32[64,512]{1,0:T(8,128)S(1)}, u32[]{:S(2)}, u32[]{:S(2)}) collective-permute-start(f32[64,512]{1,0:T(8,128)S(1)} %join_rows.1.refs_0_), channel_id=1, source_target_pairs={{0,6},{2,0},{4,2},{6,4},{1,7},{3,1},{5,3},{7,5},{8,14},{10,8},{12,... | collective-permute-start | bytes 393224 | tf_op jit(solution)/shard_map/ppermute | solution.py:811
  30.9 4.9 %collective-permute-start.9 = (f32[40,512]{1,0:T(8,128)}, f32[40,512]{1,0:T(8,128)S(1)}, u32[]{:S(2)}, u32[]{:S(2)}) collective-permute-start(f32[40,512]{1,0:T(8,128)} %get-tuple-element.47), channel_id=1, source_target_pairs={{0,1},{1,0},{2,3},{3,2},{4,5},{5,4},{6,7},{7,6},{8,9},{9,8},{10,11... | collective-permute-start | bytes 245768 | tf_op jit(solution)/shard_map/ppermute | solution.py:799
  31.0 14.4 %collective-permute-start.3 = (f32[64,512]{1,0:T(8,128)S(1)}, f32[64,512]{1,0:T(8,128)}, u32[]{:S(2)}, u32[]{:S(2)}) collective-permute-start(f32[64,512]{1,0:T(8,128)S(1)} %join_rows.1.refs_0_), channel_id=1, source_target_pairs={{0,4},{2,6},{4,0},{6,2},{1,5},{3,7},{5,1},{7,3},{8,12},{10,14},{12... | collective-permute-start | bytes 393224 | tf_op jit(solution)/shard_map/ppermute | solution.py:811
  31.8 13.6 %collective-permute-start.4 = (f32[64,512]{1,0:T(8,128)S(1)}, f32[64,512]{1,0:T(8,128)}, u32[]{:S(2)}, u32[]{:S(2)}) collective-permute-start(f32[64,512]{1,0:T(8,128)S(1)} %join_rows.1.refs_0_), channel_id=1, source_target_pairs={{0,2},{2,4},{4,6},{6,0},{1,3},{3,5},{5,7},{7,1},{8,10},{10,12},{12... | collective-permute-start | bytes 393224 | tf_op jit(solution)/shard_map/ppermute | solution.py:811
  33.1 12.4 %collective-permute-start.6 = (f32[64,512]{1,0:T(8,128)}, f32[64,512]{1,0:T(8,128)}, u32[]{:S(2)}, u32[]{:S(2)}) collective-permute-start(f32[64,512]{1,0:T(8,128)} %collective-permute-done.5.refs_4_), channel_id=1, source_target_pairs={{0,6},{2,0},{4,2},{6,4},{1,7},{3,1},{5,3},{7,5},{8,14},{10,8},{12,... | collective-permute-start | bytes 393224 | tf_op jit(solution)/shard_map/ppermute | solution.py:811
  36.5 9.0 %collective-permute-start.7 = (f32[64,512]{1,0:T(8,128)}, f32[64,512]{1,0:T(8,128)}, u32[]{:S(2)}, u32[]{:S(2)}) collective-permute-start(f32[64,512]{1,0:T(8,128)} %collective-permute-done.5.refs_4_), channel_id=1, source_target_pairs={{0,4},{2,6},{4,0},{6,2},{1,5},{3,7},{5,1},{7,3},{8,12},{10,14},{12... | collective-permute-start | bytes 393224 | tf_op jit(solution)/shard_map/ppermute | solution.py:811
  37.9 9.0 %collective-permute-start.8 = (f32[64,512]{1,0:T(8,128)}, f32[64,512]{1,0:T(8,128)}, u32[]{:S(2)}, u32[]{:S(2)}) collective-permute-start(f32[64,512]{1,0:T(8,128)} %collective-permute-done.5.refs_4_), channel_id=1, source_target_pairs={{0,2},{2,4},{4,6},{6,0},{1,3},{3,5},{5,7},{7,1},{8,10},{10,12},{12... | collective-permute-start | bytes 393224 | tf_op jit(solution)/shard_map/ppermute | solution.py:811
  52.4 1.6 %collective-permute-start.13 = (f32[2,128,256]{2,1,0:T(8,128)S(1)}, f32[2,128,256]{2,1,0:T(8,128)S(1)}, u32[]{:S(2)}, u32[]{:S(2)}) collective-permute-start(f32[2,128,256]{2,1,0:T(8,128)S(1)} %get-tuple-element.61), channel_id=1, source_target_pairs={{0,1},{1,0},{2,3},{3,2},{4,5},{5,4},{6,7},{7,6},{8,9},{9,8},{10,11... | collective-permute-start | bytes 786440 | tf_op jit(solution)/shard_map/ppermute | solution.py:799
  81.7 9.6 %collective-permute-start.14 = (f32[2,40,512]{2,1,0:T(8,128)S(1)}, f32[2,40,512]{2,1,0:T(8,128)S(1)}, u32[]{:S(2)}, u32[]{:S(2)}) collective-permute-start(f32[2,40,512]{2,1,0:T(8,128)S(1)} %get-tuple-element.67), channel_id=1, source_target_pairs={{0,1},{1,0},{2,3},{3,2},{4,5},{5,4},{6,7},{7,6},{8,9},{9,8},{10,11... | collective-permute-start | bytes 491528 | tf_op jit(solution)/shard_map/ppermute | solution.py:799
  81.8 5.9 %collective-permute-start.15 = (f32[64,512]{1,0:T(8,128)S(1)}, f32[64,512]{1,0:T(8,128)S(1)}, u32[]{:S(2)}, u32[]{:S(2)}) collective-permute-start(f32[64,512]{1,0:T(8,128)S(1)} %get-tuple-element.68.refs_0_), channel_id=1, source_target_pairs={{0,8},{8,0},{1,9},{9,1},{2,10},{10,2},{3,11},{11,3},{4,12},{12,4},... | collective-permute-start | bytes 393224 | tf_op jit(solution)/shard_map/ppermute | solution.py:807
  83.3 6.3 %collective-permute-start.18 = (f32[64,512]{1,0:T(8,128)S(1)}, f32[64,512]{1,0:T(8,128)S(1)}, u32[]{:S(2)}, u32[]{:S(2)}) collective-permute-start(f32[64,512]{1,0:T(8,128)S(1)} %get-tuple-element.68.refs_0_), channel_id=1, source_target_pairs={{0,6},{2,0},{4,2},{6,4},{1,7},{3,1},{5,3},{7,5},{8,14},{10,8},{12,... | collective-permute-start | bytes 393224 | tf_op jit(solution)/shard_map/ppermute | solution.py:811
  84.6 9.2 %collective-permute-start.19 = (f32[64,512]{1,0:T(8,128)S(1)}, f32[64,512]{1,0:T(8,128)S(1)}, u32[]{:S(2)}, u32[]{:S(2)}) collective-permute-start(f32[64,512]{1,0:T(8,128)S(1)} %get-tuple-element.68.refs_0_), channel_id=1, source_target_pairs={{0,4},{2,6},{4,0},{6,2},{1,5},{3,7},{5,1},{7,3},{8,12},{10,14},{12... | collective-permute-start | bytes 393224 | tf_op jit(solution)/shard_map/ppermute | solution.py:811
  86.2 10.5 %collective-permute-start.20 = (f32[64,512]{1,0:T(8,128)S(1)}, f32[64,512]{1,0:T(8,128)S(1)}, u32[]{:S(2)}, u32[]{:S(2)}) collective-permute-start(f32[64,512]{1,0:T(8,128)S(1)} %get-tuple-element.68.refs_0_), channel_id=1, source_target_pairs={{0,2},{2,4},{4,6},{6,0},{1,3},{3,5},{5,7},{7,1},{8,10},{10,12},{12... | collective-permute-start | bytes 393224 | tf_op jit(solution)/shard_map/ppermute | solution.py:811
  87.7 9.0 %collective-permute-start.21 = (f32[64,512]{1,0:T(8,128)S(1)}, f32[64,512]{1,0:T(8,128)S(1)}, u32[]{:S(2)}, u32[]{:S(2)}) collective-permute-start(f32[64,512]{1,0:T(8,128)S(1)} %collective-permute-done.15.refs_4_), channel_id=1, source_target_pairs={{0,6},{2,0},{4,2},{6,4},{1,7},{3,1},{5,3},{7,5},{8,14},{10,8},{12,... | collective-permute-start | bytes 393224 | tf_op jit(solution)/shard_map/ppermute | solution.py:811
  89.7 8.4 %collective-permute-start.22 = (f32[64,512]{1,0:T(8,128)S(1)}, f32[64,512]{1,0:T(8,128)S(1)}, u32[]{:S(2)}, u32[]{:S(2)}) collective-permute-start(f32[64,512]{1,0:T(8,128)S(1)} %collective-permute-done.15.refs_4_), channel_id=1, source_target_pairs={{0,4},{2,6},{4,0},{6,2},{1,5},{3,7},{5,1},{7,3},{8,12},{10,14},{12... | collective-permute-start | bytes 393224 | tf_op jit(solution)/shard_map/ppermute | solution.py:811
  91.3 8.5 %collective-permute-start.23 = (f32[64,512]{1,0:T(8,128)S(1)}, f32[64,512]{1,0:T(8,128)S(1)}, u32[]{:S(2)}, u32[]{:S(2)}) collective-permute-start(f32[64,512]{1,0:T(8,128)S(1)} %collective-permute-done.15.refs_4_), channel_id=1, source_target_pairs={{0,2},{2,4},{4,6},{6,0},{1,3},{3,5},{5,7},{7,1},{8,10},{10,12},{12... | collective-permute-start | bytes 393224 | tf_op jit(solution)/shard_map/ppermute | solution.py:811
  104.1 7.3 %collective-permute-start.24 = (f32[2,128,256]{2,1,0:T(8,128)S(1)}, f32[2,128,256]{2,1,0:T(8,128)S(1)}, u32[]{:S(2)}, u32[]{:S(2)}) collective-permute-start(f32[2,128,256]{2,1,0:T(8,128)S(1)} %get-tuple-element.76), channel_id=1, source_target_pairs={{0,1},{1,0},{2,3},{3,2},{4,5},{5,4},{6,7},{7,6},{8,9},{9,8},{10,11... | collective-permute-start | bytes 786440 | tf_op jit(solution)/shard_map/ppermute | solution.py:799
  104.2 14.0 %all-to-all-start.2 = ((f32[8,64,128]{2,1,0:T(8,128)}), f32[8,64,128]{2,1,0:T(8,128)S(1)}, u32[]{:S(2)}, u32[]{:S(2)}) async-start(f32[8,64,128]{2,1,0:T(8,128)} %pair_to_facets.1), calls=%async_computation.2 | async-start | bytes 524288 | tf_op jit(solution)/shard_map/all_to_all | solution.py:875
  118.1 19.7 %all-to-all-start.3 = ((f32[8,72,512]{2,1,0:T(8,128)}), f32[8,72,512]{2,1,0:T(8,128)S(1)}, u32[]{:S(2)}, u32[]{:S(2)}) async-start(f32[8,72,512]{2,1,0:T(8,128)} %backward.3), calls=%async_computation.3 | async-start | bytes 2359296 | tf_op jit(solution)/shard_map/all_to_all | solution.py:879
  129.1 18.3 %collective-permute-start.16 = (f32[8,40,128]{2,1,0:T(8,128)S(1)}, f32[8,40,128]{2,1,0:T(8,128)S(1)}, u32[]{:S(2)}, u32[]{:S(2)}) collective-permute-start(f32[8,40,128]{2,1,0:T(8,128)S(1)} %get-tuple-element.72), channel_id=1, source_target_pairs={{0,16},{16,32},{32,48},{48,64},{64,80},{80,96},{96,112},{1,17},{17... | collective-permute-start | bytes 491528 | tf_op jit(solution)/shard_map/ppermute | solution.py:819
  134.0 13.5 %collective-permute-start.17 = (f32[8,40,128]{2,1,0:T(8,128)S(1)}, f32[8,40,128]{2,1,0:T(8,128)S(1)}, u32[]{:S(2)}, u32[]{:S(2)}) collective-permute-start(f32[8,40,128]{2,1,0:T(8,128)S(1)} %get-tuple-element.73), channel_id=1, source_target_pairs={{16,0},{32,16},{48,32},{64,48},{80,64},{96,80},{112,96},{17,1},{33... | collective-permute-start | bytes 491528 | tf_op jit(solution)/shard_map/ppermute | solution.py:819
  137.9 1.4 collective-permute-start.25
  140.1 17.0 %all-to-all-start.4 = ((f32[8,48,128]{2,1,0:T(8,128)}), f32[8,48,128]{2,1,0:T(8,128)S(1)}, u32[]{:S(2)}, u32[]{:S(2)}) async-start(f32[8,48,128]{2,1,0:T(8,128)} %to_facets.1), calls=%async_computation.4 | async-start | bytes 393216 | tf_op jit(solution)/shard_map/all_to_all | solution.py:893
  147.5 7.7 %collective-permute-start.26 = (f32[8,2,8,128]{3,2,1,0:T(8,128)S(1)}, f32[8,2,8,128]{3,2,1,0:T(8,128)S(1)}, u32[]{:S(2)}, u32[]{:S(2)}) collective-permute-start(f32[8,2,8,128]{3,2,1,0:T(8,128)S(1)} %get-tuple-element.85), channel_id=1, source_target_pairs={{0,1},{1,2},{2,3},{3,4},{4,5},{5,6},{6,7},{7,8},{8,9},{9,10},{10,1... | collective-permute-start | bytes 196616 | tf_op jit(solution)/shard_map/ppermute | solution.py:819
  149.5 7.6 %collective-permute-start.27 = (f32[8,2,8,128]{3,2,1,0:T(8,128)S(1)}, f32[8,2,8,128]{3,2,1,0:T(8,128)S(1)}, u32[]{:S(2)}, u32[]{:S(2)}) collective-permute-start(f32[8,2,8,128]{3,2,1,0:T(8,128)S(1)} %get-tuple-element.84), channel_id=1, source_target_pairs={{1,0},{2,1},{3,2},{4,3},{5,4},{6,5},{7,6},{8,7},{9,8},{10,9},{11,1... | collective-permute-start | bytes 196616 | tf_op jit(solution)/shard_map/ppermute | solution.py:819
  (15 other events, 105.8 us)

commit v4 on v3

--- a/solution.py
+++ b/solution.py
@@ -168,42 +168,73 @@
     )(doubled[:, :, None], doubled[:, None, :])
 
 
-def gridding_kernel(own_ref, other_ref, table_ref, out_ref):
+def gridding_kernel(own_ref, other_ref, table_ref, turn_ref, out_ref, first_ref, second_ref):
     half = lax.axis_index("core")
-    odd = lax.broadcasted_iota(jnp.int32, own_ref.shape, 0) & half
-    sign = jnp.where(odd == 1, F32(-1.0), F32(1.0))
+    sign = jnp.where(half == 1, F32(-1.0), F32(1.0))
+    table = table_ref[...]
     for b, ref in enumerate((own_ref, other_ref)):
-        high, low = parts(ref[...] * sign)
-        for part in range(2):
-            value = dot(table_ref[part, 0], high)
-            value = value + dot(table_ref[part, 0], low)
-            value = value + dot(table_ref[part, 1], high)
-            for cols in range(2):
-                kept_high, kept_low = parts(value[256 * cols : 256 * cols + 256])
-                out_ref[b, cols, part, 0] = kept_high
-                out_ref[b, cols, part, 1] = kept_low
+        turned = []
+        first_ref[...] = ref[:, :128]
+        second_ref[...] = ref[:, 128:]
+        for q in range(4):
+            rows = pl.ds(q, 256, stride=4)
+            high, low = parts(jnp.concatenate([first_ref[rows], second_ref[rows]], axis=1))
+            value = dot(table, high)
+            real = value[0:256] + value[256:512]
+            imag = value[512:768] + value[768:1024]
+            value = dot(table[0:256], low)
+            real = real + value
+            value = dot(table[512:768], low)
+            imag = imag + value
+            if q:
+                cos, sin = turn_ref[:, 2 * q : 2 * q + 1], turn_ref[:, 2 * q + 1 : 2 * q + 2]
+                if q & 1:
+                    cos, sin = cos * sign, sin * sign
+                real, imag = cos * real + sin * imag, cos * imag - sin * real
+            turned.append((real, imag))
+        even = [turned[0][i] + turned[2][i] for i in range(2)]
+        odd = [turned[1][i] + turned[3][i] for i in range(2)]
+        near = [even[i] + odd[i] for i in range(2)]
+        even = [turned[0][i] - turned[2][i] for i in range(2)]
+        odd = [turned[1][i] - turned[3][i] for i in range(2)]
+        far = [even[0] + odd[1], even[1] - odd[0]]
+        for cols, values in enumerate((near, far)):
+            for part in range(2):
+                high, low = parts(values[part])
+                out_ref[b, cols, part, 0] = high
+                out_ref[b, cols, part, 1] = low
 
 
 def column_table():
-    angle = (np.arange(512)[:, None] * np.arange(1024)[None, :] % 1024) * (2.0 * np.pi / 1024)
-    out = np.zeros((2, 2, 512, 1024), ml_dtypes.bfloat16)
+    angle = (np.arange(256)[:, None] * np.arange(256)[None, :] % 256) * (2.0 * np.pi / 256)
+    out = np.zeros((4, 256, 256), ml_dtypes.bfloat16)
     for part, value in enumerate((np.cos(angle) / 32.0, -np.sin(angle) / 32.0)):
         high = value.astype(ml_dtypes.bfloat16)
-        out[part, 0] = high
-        out[part, 1] = (value - high.astype(np.float64)).astype(ml_dtypes.bfloat16)
+        out[2 * part] = high
+        out[2 * part + 1] = (value - high.astype(np.float64)).astype(ml_dtypes.bfloat16)
+    return out.reshape(1024, 256)
+
+
+def turns():
+    out = np.zeros((256, 8), np.float32)
+    for q in range(4):
+        angle = np.arange(256) * q * (2.0 * np.pi / 1024)
+        out[:, 2 * q] = np.cos(angle)
+        out[:, 2 * q + 1] = np.sin(angle)
     return out
 
 
 def gridding(own, other):
     return pl.pallas_call(
         gridding_kernel,
-        in_specs=[VMEM, VMEM, VMEM],
+        in_specs=[VMEM] * 4,
         out_specs=VMEM,
         out_shape=pltpu.HBM((2, 2, 2, 2, 256, 256), BF16),
-        compiler_params=params(),
-        cost_estimate=cost(7),
+        scratch_shapes=[pltpu.VMEM((1024, 128), F32)] * 2,
+        compiler_params=params(),
+        cost_estimate=cost(3),
         name="gridding",
-    )(own, other, column_table())
+    )(own, other, column_table(), turns())
 
 
 def thrice(left, high, low, form):
@@ -279,8 +310,8 @@
 
 
 def backward_kernel(mine_ref, theirs_ref, data_ref, trig_ref, *rest):
-    extra_ref = rest[0] if len(rest) == 8 else None
-    right_hbm, grid_hbm, out_ref = rest[-7:-4]
+    extra_ref = rest[0] if len(rest) == 15 else None
+    right_hbm, grid_hbm, *outs = rest[-7:-4] if extra_ref is None else rest[-14:-4]
     total_ref, right_ref, grid_ref, sems = rest[-4:]
     order = [(0, 0), (0,), (1, 0), (1,), (0, 1), (1, 1)]
     copies = fetch(right_hbm, grid_hbm, right_ref, grid_ref, sems, order)
@@ -314,17 +345,22 @@
     if extra_ref is not None:
         rows = pl.ds(pl.multiple_of(64 * chip_of(0, 0), 64), 72)
         total_ref[rows] += extra_ref[...]
-    for chip in range(8):
-        out_ref[chip] = total_ref[64 * chip : 64 * chip + 72]
+    if extra_ref is None:
+        for chip in range(8):
+            outs[0][chip] = total_ref[64 * chip : 64 * chip + 72]
+    else:
+        for i, ref in enumerate(outs):
+            ref[...] = total_ref[pl.ds(pl.multiple_of(64 * chip_of(i // 4, i % 4), 64), 72)]
 
 
 def backward(mine, theirs, data, grid, right, trig, extra=None):
     args = [mine, theirs, data, trig] + ([] if extra is None else [extra])
+    pieces = [jax.ShapeDtypeStruct((72, 512), F32)] * 8
     return pl.pallas_call(
         backward_kernel,
         in_specs=[VMEM] * len(args) + [ANY] * 2,
-        out_specs=VMEM,
-        out_shape=sent_out(8, 72, 512),
+        out_specs=VMEM if extra is None else [VMEM] * 8,
+        out_shape=sent_out(8, 72, 512) if extra is None else pieces,
         scratch_shapes=[pltpu.VMEM((520, 512), F32), pltpu.VMEM((2, 512, 256), BF16)] + FETCHED,
         compiler_params=params(20),
         cost_estimate=cost(5),
@@ -332,11 +368,17 @@
     )(*args, in_hbm(right), in_hbm(grid))
 
 
-def update_kernel(sent_ref, image_ref, own_ref, other_ref, core_ref, scratch_ref):
+def sum_of(refs):
+    total = refs[0][...]
+    for ref in refs[1:]:
+        total = total + ref[...]
+    return total
+
+
+def update_kernel(*refs):
+    image_ref, own_ref, other_ref, core_ref, scratch_ref = refs[8:]
     half, chip = where_am_i()[:2]
-    total = sent_ref[0]
-    for source in range(1, 8):
-        total = total + sent_ref[source]
+    total = sum_of(refs[:8])
     row = lax.broadcasted_iota(jnp.int32, total.shape, 0) + (64 * chip - HALO)
     value = jnp.maximum(image_ref[...] - 0.5 * total, 0.0)
     scratch_ref[...] = jnp.where((row >= 0) & (row < 512), value, 0.0)
@@ -351,22 +393,19 @@
     window = jax.ShapeDtypeStruct((2, 40, 512), F32)
     return pl.pallas_call(
         update_kernel,
-        in_specs=[VMEM] * 2,
+        in_specs=[VMEM] * 9,
         out_specs=[VMEM] * 3,
         out_shape=[window, window, jax.ShapeDtypeStruct((64, 512), F32)],
         scratch_shapes=[pltpu.VMEM((72, 512), F32)],
         compiler_params=params(),
         cost_estimate=cost(1),
         name="update",
-    )(sent, image)
+    )(*sent, image)
 
 
 def total_kernel(sent_ref, own_ref, other_ref, scratch_ref):
     half = lax.axis_index("core")
-    total = sent_ref[0]
-    for source in range(1, 8):
-        total = total + sent_ref[source]
-    scratch_ref[...] = total
+    scratch_ref[...] = sum_of([sent_ref.at[source] for source in range(8)])
     own_ref[...] = scratch_ref[pl.ds(pl.multiple_of(32 * half, 32), 40)]
     other_ref[...] = scratch_ref[pl.ds(pl.multiple_of(32 - 32 * half, 32), 40)]
 
@@ -803,6 +842,16 @@
     return gathered_x(value) + gathered_x(across_y(value))
 
 
+def to_chips(pieces):
+    arrived = [pieces[0]]
+    for i in range(1, 8):
+        route = [
+            (4 * y + x, 4 * (y ^ (i // 4)) + (x + i) % 4) for y in range(2) for x in range(4)
+        ]
+        arrived.append(lax.ppermute(pieces[i], CHIPS, route))
+    return arrived
+
+
 def across_y(value):
     return lax.ppermute(value, "y", [(0, 1), (1, 0)])
 
@@ -841,32 +890,30 @@
         [filters.reshape(NBASIS, 6), radius[:, None], level_counts[:, None].astype(F32)], axis=1
     )
 
-    packed, phase = lax.optimization_barrier(
-        (start(filters.transpose(2, 1, 0), level_counts, sky_image, dual_coefs), phase_screen[0, 0])
-    )
+    packed = start(filters.transpose(2, 1, 0), level_counts, sky_image, dual_coefs)
     sent = lax.all_to_all(packed, "chan", 0, 0, tiled=True)
 
-    phase_other = swapped(half_of(phase, 1 - half, 512, 1))
     weight_own = grid_weight[0, 0]
-    weight_other = swapped(weight_own)
+    weight_other, phase = lax.optimization_barrier((swapped(weight_own), phase_screen[0, 0]))
+    phase_other = half_of(phase, 1 - half, 512, 1)
     data_own = visibilities[0, 0].reshape(128, 256)
     data = jnp.stack([data_own, swapped(data_own)])
     rows_own = grid_rows[0, 0]
     rows_other = swapped(rows_own.astype(F32)).astype(jnp.int32)
     left, right = tables(jnp.stack([rows_own, rows_other]))
-    trig = screens(phase, phase_other)
     grid = gridding(weight_own, weight_other)
-    sent, grid = lax.optimization_barrier((sent, grid))
+    sent, grid, phase_other = lax.optimization_barrier((sent, grid, phase_other))
+    trig = screens(phase, swapped(phase_other))
 
     own, other, term_own, term_other = split(sent)
     strip = join_rows(own, swapped(other))
     pieces = gathered(strip)
     extra = join(term_own, swapped(term_other))
-    pieces, extra, data, right = lax.optimization_barrier((pieces, extra, data, right))
+    pieces, extra, data = lax.optimization_barrier((pieces, extra, data))
 
     seen, seen_copy, window = forward(pieces, trig, left, grid, True)
     sent = backward(seen_copy, swapped(seen), data, grid, right, trig, extra)
-    sent = lax.all_to_all(sent, CHIPS, 0, 0, tiled=True)
+    sent = to_chips(sent)
     own, other, core = update(sent, window)
 
     pieces = gathered(core)
@@ -876,8 +923,7 @@
     seen, seen_copy = forward(pieces, trig, left, grid, False)
     dual, part, to_right, to_left, now = middle(scal, dual_coefs, sky_image, pair)
     sent = backward(seen_copy, swapped(seen), data, grid, right, trig)
-    sent = lax.all_to_all(sent, CHIPS, 0, 0, tiled=True)
-    windows = total_windows(sent)
+    windows = total_windows(lax.all_to_all(sent, CHIPS, 0, 0, tiled=True))
     from_left = neighbours(to_right, "chan", 8, 1)
     from_right = neighbours(to_left, "chan", 8, -1)
     packed = to_facets(*windows)

time: 164 us -> 159 us (0.970)
  blocking collectives: 21.4 us -> 0 us
  waiting for transfers between devices: 16.9 us -> 36.8 us
  Pallas kernels: 51.6 us -> 47.2 us
  starting transfers between devices: 63.1 us -> 66 us
  local copies, waits for them, and re-layouts: 7.06 us -> 5.05 us
    all_to_all x1 -> x0, blocking collectives: 21.4 us -> none  [per_device(): sent = lax.all_to_all(sent, CHIPS, 0, 0, tiled=True)]
    ppermute x0 -> x7, waiting for transfers between devices: none -> 13.8 us  [to_chips(): arrived.append(lax.ppermute(pieces[i], CHIPS, route))]
    ppermute x0 -> x7, starting transfers between devices: none -> 6.75 us  [to_chips(): arrived.append(lax.ppermute(pieces[i], CHIPS, route))]
    all_to_all x1, waiting for transfers between devices: 0.01 us -> 2.52 us  [per_device(): sent = lax.all_to_all(packed, 'chan', 0, 0, tiled=True)]
    pallas_call x2, Pallas kernels: 6.19 us -> 3.8 us  [the longest x1 3.7 us: gridding(): pl.pallas_call(gridding_kernel, in_specs=[VMEM] * 4, out_specs=VMEM, out_...]
    ppermute x10, waiting for transfers between devices: 3.65 us -> 5.52 us  [swapped(): return lax.ppermute(value, 'core', [(0, 1), (1, 0)])]
    unnamed x30 -> x54, local copies, waits for them, and re-layouts: 4.21 us -> 3.48 us
  transfers between devices with their start and end apart: 32 -> 39, of which waited for: 13 -> 19; matrix products, arithmetic and copies ran while one was open for 2% -> 1% of each run, Pallas kernels for 19% -> 17%
where the time goes in v4:
time: 159 us; the launch traced here: 156 us
  starting transfers between devices  66 us (42%)
  Pallas kernels  47.2 us (30%)
  waiting for transfers between devices  36.8 us (23%)
  local copies, waits for them, and re-layouts  5.05 us (3%)
    ppermute x12, starting transfers between devices, along_x(): return lax.ppermute(value, 'x', [(i, (i + step) % 4) for i in range(4)])  15.2 us
    ppermute x4, starting transfers between devices, neighbours(): lax.ppermute(value, axis, [(i, i + step) for i in range(count) if 0 <= i...  15.2 us
    ppermute x7, waiting for transfers between devices, to_chips(): arrived.append(lax.ppermute(pieces[i], CHIPS, route))  13.8 us
    pallas_call x2, Pallas kernels, backward(): pl.pallas_call(backward_kernel, in_specs=[VMEM] * len(args) + [ANY] * 2,...  11.2 us
    pallas_call x2, Pallas kernels, forward(): pl.pallas_call(functools.partial(forward_kernel, windows=windows), in_spe...  8.49 us
    all_to_all x1, starting transfers between devices, per_device(): sent = lax.all_to_all(packed, 'chan', 0, 0, tiled=True)  8.31 us
    ppermute x12, waiting for transfers between devices, along_x(): return lax.ppermute(value, 'x', [(i, (i + step) % 4) for i in range(4)])  8 us
    all_to_all x1, starting transfers between devices, per_device(): gradient = lax.all_to_all(packed, 'chan', 0, 0, tiled=True)  6.97 us
  transfers between devices with their start and end apart: 39, of which 19 were waited for; matrix products, arithmetic and copies ran while one was open for 1% of the time, Pallas kernels for 17%

profile of v4, /device:TPU:24, one launch (start us, length us, event | category | flops | bytes accessed | tf_op | source)
XLA Modules:
  0.0 156.4 jit_solution(12193190438421732746)
XLA Ops:
  1.5 4.2 %start.1 = f32[8,80,128]{2,1,0:T(8,128)} custom-call(f32[3,2,9]{2,1,0:T(2,128)S(1)} %bitcast.27, s32[9]{0:T(128)} %level_ref.1, f32[8,32,128]{2,1,0:T(8,128)} %before_ref.1, f32[9,8,32,128]{3,2,1,0:T(8,128)} %dual_ref.3), custom_call_target="tpu_custom_call" | custom-call | bytes 12000000 | tf_op jit(solution)/shard_map/start/pallas_call | solution.py:719
  5.8 8.3 %all-to-all-start = ((f32[8,80,128]{2,1,0:T(8,128)}), f32[8,80,128]{2,1,0:T(8,128)S(1)}, u32[]{:S(2)}, u32[]{:S(2)}) async-start(f32[8,80,128]{2,1,0:T(8,128)} %start.1), calls=%async_computation | async-start | bytes 655360 | tf_op jit(solution)/shard_map/all_to_all | solution.py:894
  14.1 3.7 %gridding.1.refs_10_.rest_2_.rest_1_ = bf16[2,2,2,2,256,256]{5,4,3,2,1,0:T(8,128)(2,1)} custom-call(f32[1024,256]{1,0:T(8,128)S(1)} %bitcast.26, f32[1024,256]{1,0:T(8,128)S(1)} %collective-permute-done.other_ref, bf16[1024,256]{1,0:T(8,128)(2,1)S(1)} %copy-done.2, f32[256,8]{1,0:T(8,128)S(1)} %copy-done.18), custom_call_target="tpu_custom_call" | custom-call | bytes 9000000 | tf_op jit(solution)/shard_map/gridding/pallas_call | solution.py:228
  18.9 2.5 %all-to-all-done.sent_ref = f32[8,80,128]{2,1,0:T(8,128)S(1)} async-done(((f32[8,80,128]{2,1,0:T(8,128)}), f32[8,80,128]{2,1,0:T(8,128)S(1)}, u32[]{:S(2)}, u32[]{:S(2)}) %all-to-all-start) | async-done | bytes 327712 | tf_op jit(solution)/shard_map/all_to_all | solution.py:894
  25.4 2.8 %collective-permute-start.2 = (f32[64,512]{1,0:T(8,128)S(1)}, f32[64,512]{1,0:T(8,128)S(1)}, u32[]{:S(2)}, u32[]{:S(2)}) collective-permute-start(f32[64,512]{1,0:T(8,128)S(1)} %join_rows.1.refs_0_), channel_id=1, source_target_pairs={{0,6},{2,0},{4,2},{6,4},{1,7},{3,1},{5,3},{7,5},{8,14},{10,8},{12,... | collective-permute-start | bytes 393224 | tf_op jit(solution)/shard_map/ppermute | solution.py:860
  31.4 2.4 %collective-permute-start.6 = (f32[64,512]{1,0:T(8,128)S(1)}, f32[64,512]{1,0:T(8,128)S(1)}, u32[]{:S(2)}, u32[]{:S(2)}) collective-permute-start(f32[64,512]{1,0:T(8,128)S(1)} %collective-permute-done.5.refs_4_), channel_id=1, source_target_pairs={{0,6},{2,0},{4,2},{6,4},{1,7},{3,1},{5,3},{7,5},{8,14},{10,8},{12,... | collective-permute-start | bytes 393224 | tf_op jit(solution)/shard_map/ppermute | solution.py:860
  35.2 3.1 %collective-permute-start.8 = (f32[64,512]{1,0:T(8,128)S(1)}, f32[64,512]{1,0:T(8,128)S(1)}, u32[]{:S(2)}, u32[]{:S(2)}) collective-permute-start(f32[64,512]{1,0:T(8,128)S(1)} %collective-permute-done.5.refs_4_), channel_id=1, source_target_pairs={{0,2},{2,4},{4,6},{6,0},{1,3},{3,5},{5,7},{7,1},{8,10},{10,12},{12... | collective-permute-start | bytes 393224 | tf_op jit(solution)/shard_map/ppermute | solution.py:860
  38.5 2.6 %tables.1 = (bf16[2,256,512]{2,1,0:T(8,128)(2,1)}, bf16[2,512,256]{2,1,0:T(8,128)(2,1)}) custom-call(s32[2,128,1]{2,1,0:T(8,128)S(1)} %copy.23.gcol_ref, s32[2,1,128]{2,1,0:T(1,128)S(1)} %bitcast.28), custom_call_target="tpu_custom_call" | custom-call | bytes 6000000 | tf_op jit(solution)/shard_map/tables/pallas_call | solution.py:157
  44.7 2.8 %screens.1.refs_8_.trig_ref = s16[2,2,2,512,256]{4,3,2,1,0:T(8,128)(2,1)S(1)} custom-call(f32[512,512]{1,0:T(8,128)S(1)} %collective-permute-done.11.other_ref, f32[512,1024]{1,0:T(8,128)} %bitcast.29), custom_call_target="tpu_custom_call" | custom-call | bytes 12000000 | tf_op jit(solution)/shard_map/screens/pallas_call | solution.py:124
  47.6 4.2 %forward.2 = (f32[2,128,256]{2,1,0:T(8,128)S(1)}, f32[2,128,256]{2,1,0:T(8,128)S(1)}, f32[72,512]{1,0:T(8,128)S(1)}) custom-call(f32[64,512]{1,0:T(8,128)S(1)} %join_rows.1.refs_0_, f32[64,512]{1,0:T(8,128)S(1)} %copy-done.7, f32[64,512]{1,0:T(8,128)S(1)} %copy-done.9, f32[64,512]{1,0:T(8,128)S(1)} %copy-done.11, f32[64,512]{1,0:T(8,128)S(1)} %copy-done.5, ...), custom_call_target="tpu_custom_call" | custom-call | bytes 15000000 | tf_op jit(solution)/shard_map/forward/pallas_call | solution.py:300
  52.0 1.5 collective-permute-done.13.theirs_ref
  53.5 5.1 %backward.2 = (f32[72,512]{1,0:T(8,128)S(1)}, f32[72,512]{1,0:T(8,128)S(1)}, f32[72,512]{1,0:T(8,128)S(1)}, f32[72,512]{1,0:T(8,128)S(1)}, f32[72,512]{1,0:T(8,1...) custom-call(f32[2,128,256]{2,1,0:T(8,128)S(1)} %get-tuple-element.68.mine_ref, ...), custom_call_target="tpu_custom_call" | custom-call | bytes 15000000 | tf_op jit(solution)/shard_map/backward/pallas_call | solution.py:359
  58.7 2.0 %collective-permute-start.15 = (f32[72,512]{1,0:T(8,128)S(1)}, f32[72,512]{1,0:T(8,128)S(1)}, u32[]{:S(2)}, u32[]{:S(2)}) collective-permute-start(f32[72,512]{1,0:T(8,128)S(1)} %get-tuple-element.75), channel_id=1, source_target_pairs={{0,4},{2,6},{4,0},{6,2},{8,12},{10,14},{12,8},{14,10},{1,5},{3,7},... | collective-permute-start | bytes 442376 | tf_op jit(solution)/shard_map/ppermute | solution.py:851
  60.7 1.5 collective-permute-start.16
  64.2 5.5 %collective-permute-done.14.refs_1_ = f32[72,512]{1,0:T(8,128)S(1)} collective-permute-done((f32[72,512]{1,0:T(8,128)S(1)}, f32[72,512]{1,0:T(8,128)S(1)}, u32[]{:S(2)}, u32[]{:S(2)}) %collective-permute-start.14) | collective-permute-done | bytes 147488 | tf_op jit(solution)/shard_map/ppermute | solution.py:851
  70.9 2.8 %collective-permute-done.18.refs_5_ = f32[72,512]{1,0:T(8,128)S(1)} collective-permute-done((f32[72,512]{1,0:T(8,128)S(1)}, f32[72,512]{1,0:T(8,128)S(1)}, u32[]{:S(2)}, u32[]{:S(2)}) %collective-permute-start.18) | collective-permute-done | bytes 147488 | tf_op jit(solution)/shard_map/ppermute | solution.py:851
  73.6 5.3 %collective-permute-done.19.refs_6_ = f32[72,512]{1,0:T(8,128)S(1)} collective-permute-done((f32[72,512]{1,0:T(8,128)S(1)}, f32[72,512]{1,0:T(8,128)S(1)}, u32[]{:S(2)}, u32[]{:S(2)}) %collective-permute-start.19) | collective-permute-done | bytes 147488 | tf_op jit(solution)/shard_map/ppermute | solution.py:851
  82.5 2.8 %collective-permute-done.22.refs_4_ = f32[64,512]{1,0:T(8,128)S(1)} collective-permute-done((f32[64,512]{1,0:T(8,128)S(1)}, f32[64,512]{1,0:T(8,128)S(1)}, u32[]{:S(2)}, u32[]{:S(2)}) %collective-permute-start.22) | collective-permute-done | bytes 131104 | tf_op jit(solution)/shard_map/ppermute | solution.py:856
  89.0 1.9 %collective-permute-done.27.refs_3_ = f32[64,512]{1,0:T(8,128)S(1)} collective-permute-done((f32[64,512]{1,0:T(8,128)S(1)}, f32[64,512]{1,0:T(8,128)S(1)}, u32[]{:S(2)}, u32[]{:S(2)}) %collective-permute-start.27) | collective-permute-done | bytes 131104 | tf_op jit(solution)/shard_map/ppermute | solution.py:860
  92.2 2.1 %collective-permute-done.29.refs_6_ = f32[64,512]{1,0:T(8,128)S(1)} collective-permute-done((f32[64,512]{1,0:T(8,128)S(1)}, f32[64,512]{1,0:T(8,128)S(1)}, u32[]{:S(2)}, u32[]{:S(2)}) %collective-permute-start.29) | collective-permute-done | bytes 131104 | tf_op jit(solution)/shard_map/ppermute | solution.py:860
  95.6 4.2 %forward.3 = (f32[2,128,256]{2,1,0:T(8,128)S(1)}, f32[2,128,256]{2,1,0:T(8,128)S(1)}) custom-call(f32[64,512]{1,0:T(8,128)S(1)} %get-tuple-element.84.refs_0_, f32[64,512]{1,0:T(8,128)S(1)} %collective-permute-done.25.refs_1_, f32[64,512]{1,0:T(8,128)S(1)} %collective-permute-done.26.refs_2_, f32[64,512]{1,0:T(8,128)S(1)} %collective-permute-done.27.refs_3_, ...), custom_call_target="tpu_custom_call" | custom-call | bytes 15000000 | tf_op jit(solution)/shard_map/forward/pallas_call | solution.py:300
  100.0 6.6 %all-to-all-start.1 = ((f32[8,64,128]{2,1,0:T(8,128)}), f32[8,64,128]{2,1,0:T(8,128)S(1)}, u32[]{:S(2)}, u32[]{:S(2)}) async-start(f32[8,64,128]{2,1,0:T(8,128)} %pair_to_facets.1), calls=%async_computation.1 | async-start | bytes 524288 | tf_op jit(solution)/shard_map/all_to_all | solution.py:922
  106.6 6.1 %backward.3 = f32[8,72,512]{2,1,0:T(8,128)} custom-call(f32[2,128,256]{2,1,0:T(8,128)S(1)} %get-tuple-element.91.mine_ref, f32[2,128,256]{2,1,0:T(8,128)S(1)} %collective-permute-done.31.theirs_ref, f32[2,128,256]{2,1,0:T(8,128)S(1)} %pad_maximum_fusion.1.data_ref, s16[2,2,2,512,256]{4,3,2,1,0:T(8,128)(2,1)S(1)} %screens.1.refs_8_.trig_ref, ...), custom_call_target="tpu_custom_call" | custom-call | bytes 15000000 | tf_op jit(solution)/shard_map/backward/pallas_call | solution.py:359
  113.7 4.0 %all-to-all-start.2 = ((f32[8,72,512]{2,1,0:T(8,128)}), f32[8,72,512]{2,1,0:T(8,128)S(1)}, u32[]{:S(2)}, u32[]{:S(2)}) async-start(f32[8,72,512]{2,1,0:T(8,128)} %backward.3), calls=%async_computation.2 | async-start | bytes 2359296 | tf_op jit(solution)/shard_map/all_to_all | solution.py:926
  118.1 6.2 %middle.1 = (f32[9,8,32,128]{3,2,1,0:T(8,128)}, f32[8,80,128]{2,1,0:T(8,128)}, f32[8,40,128]{2,1,0:T(8,128)S(1)}, f32[8,40,128]{2,1,0:T(8,128)S(1)}, f32[8,80,128]{2,1,0:T(8,128)}) custom-call(f32[9,8]{1,0:T(8,128)S(1)} %pad_maximum_fusion.2.scal_ref, f32[8,32,128]{2,1,0:T(8,128)} %before_ref.1, f32[8,64,128]{2,1,0:T(8,128)S(1)} %all-to-all-done.1.pair_ref, ...), custom_call_target="tpu_custom_call" | custom-call | bytes 21000000 | tf_op jit(solution)/shard_map/middle/pallas_call | solution.py:775
  124.3 4.3 %collective-permute-start.23 = (f32[8,40,128]{2,1,0:T(8,128)S(1)}, f32[8,40,128]{2,1,0:T(8,128)S(1)}, u32[]{:S(2)}, u32[]{:S(2)}) collective-permute-start(f32[8,40,128]{2,1,0:T(8,128)S(1)} %get-tuple-element.88), channel_id=1, source_target_pairs={{0,16},{16,32},{32,48},{48,64},{64,80},{80,96},{96,112},{1,17},{17... | collective-permute-start | bytes 491528 | tf_op jit(solution)/shard_map/ppermute | solution.py:868
  128.6 3.2 %collective-permute-start.24 = (f32[8,40,128]{2,1,0:T(8,128)S(1)}, f32[8,40,128]{2,1,0:T(8,128)S(1)}, u32[]{:S(2)}, u32[]{:S(2)}) collective-permute-start(f32[8,40,128]{2,1,0:T(8,128)S(1)} %get-tuple-element.89), channel_id=1, source_target_pairs={{16,0},{32,16},{48,32},{64,48},{80,64},{96,80},{112,96},{17,1},{33... | collective-permute-start | bytes 491528 | tf_op jit(solution)/shard_map/ppermute | solution.py:868
  135.4 7.0 %all-to-all-start.3 = ((f32[8,48,128]{2,1,0:T(8,128)}), f32[8,48,128]{2,1,0:T(8,128)S(1)}, u32[]{:S(2)}, u32[]{:S(2)}) async-start(f32[8,48,128]{2,1,0:T(8,128)} %to_facets.1), calls=%async_computation.3 | async-start | bytes 393216 | tf_op jit(solution)/shard_map/all_to_all | solution.py:939
  142.5 1.9 %collective-permute-start.33 = (f32[8,2,8,128]{3,2,1,0:T(8,128)S(1)}, f32[8,2,8,128]{3,2,1,0:T(8,128)S(1)}, u32[]{:S(2)}, u32[]{:S(2)}) collective-permute-start(f32[8,2,8,128]{3,2,1,0:T(8,128)S(1)} %get-tuple-element.101), channel_id=1, source_target_pairs={{0,1},{1,2},{2,3},{3,4},{4,5},{5,6},{6,7},{7,8},{8,9},{9,10},{10,1... | collective-permute-start | bytes 196616 | tf_op jit(solution)/shard_map/ppermute | solution.py:868
  144.4 5.8 %collective-permute-start.34 = (f32[8,2,8,128]{3,2,1,0:T(8,128)S(1)}, f32[8,2,8,128]{3,2,1,0:T(8,128)S(1)}, u32[]{:S(2)}, u32[]{:S(2)}) collective-permute-start(f32[8,2,8,128]{3,2,1,0:T(8,128)S(1)} %get-tuple-element.100), channel_id=1, source_target_pairs={{1,0},{2,1},{3,2},{4,3},{5,4},{6,5},{7,6},{8,7},{9,8},{10,9},{11,1... | collective-permute-start | bytes 196616 | tf_op jit(solution)/shard_map/ppermute | solution.py:868
  150.2 1.8 %collective-permute-done.34.below_ref = f32[8,2,8,128]{3,2,1,0:T(8,128)S(1)} collective-permute-done((f32[8,2,8,128]{3,2,1,0:T(8,128)S(1)}, f32[8,2,8,128]{3,2,1,0:T(8,128)S(1)}, u32[]{:S(2)}, u32[]{:S(2)}) %collective-permute-start.34) | collective-permute-done | bytes 65568 | tf_op jit(solution)/shard_map/ppermute | solution.py:868
  152.1 4.3 %last.1 = (f32[8,32,128]{2,1,0:T(8,128)}, f32[9,8,32,128]{3,2,1,0:T(8,128)}) custom-call(f32[9,8]{1,0:T(8,128)S(1)} %pad_maximum_fusion.2.scal_ref, f32[8,80,128]{2,1,0:T(8,128)S(1)} %copy-done.3, f32[8,80,128]{2,1,0:T(8,128)S(1)} %bitcast.24, f32[8,2,8,128]{3,2,1,0:T(8,128)S(1)} %collective-permute-done.33.above_ref, ...), custom_call_target="tpu_custom_call" | custom-call | bytes 12000000 | tf_op jit(solution)/shard_map/last/pallas_call | solution.py:821
  (134 shorter events, 33.0 us)
Async XLA Ops:
  0.7 13.4 %collective-permute-start = (f32[1024,256]{1,0:T(8,128)}, f32[1024,256]{1,0:T(8,128)S(1)}, u32[]{:S(2)}, u32[]{:S(2)}) collective-permute-start(f32[1024,256]{1,0:T(8,128)} %bitcast.25), channel_id=1, source_target_pairs={{0,1},{1,0},{2,3},{3,2},{4,5},{5,4},{6,7},{7,6},{8,9},{9,8},{10,11... | collective-permute-start | bytes 3145736 | tf_op jit(solution)/shard_map/ppermute | solution.py:838
  5.8 15.6 %all-to-all-start = ((f32[8,80,128]{2,1,0:T(8,128)}), f32[8,80,128]{2,1,0:T(8,128)S(1)}, u32[]{:S(2)}, u32[]{:S(2)}) async-start(f32[8,80,128]{2,1,0:T(8,128)} %start.1), calls=%async_computation | async-start | bytes 655360 | tf_op jit(solution)/shard_map/all_to_all | solution.py:894
  21.4 23.3 %collective-permute-start.11 = (f32[512,512]{1,0:T(8,128)}, f32[512,512]{1,0:T(8,128)S(1)}, u32[]{:S(2)}, u32[]{:S(2)}) collective-permute-start(f32[512,512]{1,0:T(8,128)} %constant_dynamic-slice_fusion), channel_id=1, source_target_pairs={{0,1},{1,0},{2,3},{3,2},{4,5},{5,4},{6,7},{7,6},{8,9},{9,8},{10,11... | collective-permute-start | bytes 3145736 | tf_op jit(solution)/shard_map/ppermute | solution.py:838
  21.4 7.6 %collective-permute-start.10 = (f32[128,256]{1,0:T(8,128)S(1)}, f32[128,256]{1,0:T(8,128)S(1)}, u32[]{:S(2)}, u32[]{:S(2)}) collective-permute-start(f32[128,256]{1,0:T(8,128)S(1)} %bitcast.31), channel_id=1, source_target_pairs={{0,1},{1,0},{2,3},{3,2},{4,5},{5,4},{6,7},{7,6},{8,9},{9,8},{10,11... | collective-permute-start | bytes 393224 | tf_op jit(solution)/shard_map/ppermute | solution.py:838
  24.6 6.8 %collective-permute-start.5 = (f32[64,512]{1,0:T(8,128)S(1)}, f32[64,512]{1,0:T(8,128)S(1)}, u32[]{:S(2)}, u32[]{:S(2)}) collective-permute-start(f32[64,512]{1,0:T(8,128)S(1)} %join_rows.1.refs_0_), channel_id=1, source_target_pairs={{0,8},{8,0},{1,9},{9,1},{2,10},{10,2},{3,11},{11,3},{4,12},{12,4},... | collective-permute-start | bytes 393224 | tf_op jit(solution)/shard_map/ppermute | solution.py:856
  25.4 8.4 %collective-permute-start.2 = (f32[64,512]{1,0:T(8,128)S(1)}, f32[64,512]{1,0:T(8,128)S(1)}, u32[]{:S(2)}, u32[]{:S(2)}) collective-permute-start(f32[64,512]{1,0:T(8,128)S(1)} %join_rows.1.refs_0_), channel_id=1, source_target_pairs={{0,6},{2,0},{4,2},{6,4},{1,7},{3,1},{5,3},{7,5},{8,14},{10,8},{12,... | collective-permute-start | bytes 393224 | tf_op jit(solution)/shard_map/ppermute | solution.py:860
  28.2 7.1 %collective-permute-start.3 = (f32[64,512]{1,0:T(8,128)S(1)}, f32[64,512]{1,0:T(8,128)S(1)}, u32[]{:S(2)}, u32[]{:S(2)}) collective-permute-start(f32[64,512]{1,0:T(8,128)S(1)} %join_rows.1.refs_0_), channel_id=1, source_target_pairs={{0,4},{2,6},{4,0},{6,2},{1,5},{3,7},{5,1},{7,3},{8,12},{10,14},{12... | collective-permute-start | bytes 393224 | tf_op jit(solution)/shard_map/ppermute | solution.py:860
  30.5 11.6 %collective-permute-start.4 = (f32[64,512]{1,0:T(8,128)S(1)}, f32[64,512]{1,0:T(8,128)S(1)}, u32[]{:S(2)}, u32[]{:S(2)}) collective-permute-start(f32[64,512]{1,0:T(8,128)S(1)} %join_rows.1.refs_0_), channel_id=1, source_target_pairs={{0,2},{2,4},{4,6},{6,0},{1,3},{3,5},{5,7},{7,1},{8,10},{10,12},{12... | collective-permute-start | bytes 393224 | tf_op jit(solution)/shard_map/ppermute | solution.py:860
  31.4 11.3 %collective-permute-start.6 = (f32[64,512]{1,0:T(8,128)S(1)}, f32[64,512]{1,0:T(8,128)S(1)}, u32[]{:S(2)}, u32[]{:S(2)}) collective-permute-start(f32[64,512]{1,0:T(8,128)S(1)} %collective-permute-done.5.refs_4_), channel_id=1, source_target_pairs={{0,6},{2,0},{4,2},{6,4},{1,7},{3,1},{5,3},{7,5},{8,14},{10,8},{12,... | collective-permute-start | bytes 393224 | tf_op jit(solution)/shard_map/ppermute | solution.py:860
  33.8 9.6 %collective-permute-start.7 = (f32[64,512]{1,0:T(8,128)S(1)}, f32[64,512]{1,0:T(8,128)S(1)}, u32[]{:S(2)}, u32[]{:S(2)}) collective-permute-start(f32[64,512]{1,0:T(8,128)S(1)} %collective-permute-done.5.refs_4_), channel_id=1, source_target_pairs={{0,4},{2,6},{4,0},{6,2},{1,5},{3,7},{5,1},{7,3},{8,12},{10,14},{12... | collective-permute-start | bytes 393224 | tf_op jit(solution)/shard_map/ppermute | solution.py:860
  35.2 8.8 %collective-permute-start.8 = (f32[64,512]{1,0:T(8,128)S(1)}, f32[64,512]{1,0:T(8,128)S(1)}, u32[]{:S(2)}, u32[]{:S(2)}) collective-permute-start(f32[64,512]{1,0:T(8,128)S(1)} %collective-permute-done.5.refs_4_), channel_id=1, source_target_pairs={{0,2},{2,4},{4,6},{6,0},{1,3},{3,5},{5,7},{7,1},{8,10},{10,12},{12... | collective-permute-start | bytes 393224 | tf_op jit(solution)/shard_map/ppermute | solution.py:860
  58.6 11.1 %collective-permute-start.14 = (f32[72,512]{1,0:T(8,128)S(1)}, f32[72,512]{1,0:T(8,128)S(1)}, u32[]{:S(2)}, u32[]{:S(2)}) collective-permute-start(f32[72,512]{1,0:T(8,128)S(1)} %get-tuple-element.74), channel_id=1, source_target_pairs={{0,2},{2,4},{4,6},{6,0},{8,10},{10,12},{12,14},{14,8},{1,3},{3,5},... | collective-permute-start | bytes 442376 | tf_op jit(solution)/shard_map/ppermute | solution.py:851
  58.7 11.1 %collective-permute-start.15 = (f32[72,512]{1,0:T(8,128)S(1)}, f32[72,512]{1,0:T(8,128)S(1)}, u32[]{:S(2)}, u32[]{:S(2)}) collective-permute-start(f32[72,512]{1,0:T(8,128)S(1)} %get-tuple-element.75), channel_id=1, source_target_pairs={{0,4},{2,6},{4,0},{6,2},{8,12},{10,14},{12,8},{14,10},{1,5},{3,7},... | collective-permute-start | bytes 442376 | tf_op jit(solution)/shard_map/ppermute | solution.py:851
  60.7 10.2 %collective-permute-start.16 = (f32[72,512]{1,0:T(8,128)S(1)}, f32[72,512]{1,0:T(8,128)S(1)}, u32[]{:S(2)}, u32[]{:S(2)}) collective-permute-start(f32[72,512]{1,0:T(8,128)S(1)} %get-tuple-element.76), channel_id=1, source_target_pairs={{0,6},{2,0},{4,2},{6,4},{8,14},{10,8},{12,10},{14,12},{1,7},{3,1},... | collective-permute-start | bytes 442376 | tf_op jit(solution)/shard_map/ppermute | solution.py:851
  62.2 8.7 %collective-permute-start.17 = (f32[72,512]{1,0:T(8,128)S(1)}, f32[72,512]{1,0:T(8,128)S(1)}, u32[]{:S(2)}, u32[]{:S(2)}) collective-permute-start(f32[72,512]{1,0:T(8,128)S(1)} %get-tuple-element.77), channel_id=1, source_target_pairs={{0,8},{2,10},{4,12},{6,14},{8,0},{10,2},{12,4},{14,6},{1,9},{3,11}... | collective-permute-start | bytes 442376 | tf_op jit(solution)/shard_map/ppermute | solution.py:851
  63.5 10.2 %collective-permute-start.18 = (f32[72,512]{1,0:T(8,128)S(1)}, f32[72,512]{1,0:T(8,128)S(1)}, u32[]{:S(2)}, u32[]{:S(2)}) collective-permute-start(f32[72,512]{1,0:T(8,128)S(1)} %get-tuple-element.78), channel_id=1, source_target_pairs={{0,10},{2,12},{4,14},{6,8},{8,2},{10,4},{12,6},{14,0},{1,11},{3,13... | collective-permute-start | bytes 442376 | tf_op jit(solution)/shard_map/ppermute | solution.py:851
  69.7 9.2 %collective-permute-start.19 = (f32[72,512]{1,0:T(8,128)S(1)}, f32[72,512]{1,0:T(8,128)S(1)}, u32[]{:S(2)}, u32[]{:S(2)}) collective-permute-start(f32[72,512]{1,0:T(8,128)S(1)} %get-tuple-element.79), channel_id=1, source_target_pairs={{0,12},{2,14},{4,8},{6,10},{8,4},{10,6},{12,0},{14,2},{1,13},{3,15... | collective-permute-start | bytes 442376 | tf_op jit(solution)/shard_map/ppermute | solution.py:851
  69.7 9.4 %collective-permute-start.20 = (f32[72,512]{1,0:T(8,128)S(1)}, f32[72,512]{1,0:T(8,128)S(1)}, u32[]{:S(2)}, u32[]{:S(2)}) collective-permute-start(f32[72,512]{1,0:T(8,128)S(1)} %get-tuple-element.80), channel_id=1, source_target_pairs={{0,14},{2,8},{4,10},{6,12},{8,6},{10,0},{12,2},{14,4},{1,15},{3,9}... | collective-permute-start | bytes 442376 | tf_op jit(solution)/shard_map/ppermute | solution.py:851
  79.2 7.4 %collective-permute-start.21 = (f32[2,40,512]{2,1,0:T(8,128)S(1)}, f32[2,40,512]{2,1,0:T(8,128)S(1)}, u32[]{:S(2)}, u32[]{:S(2)}) collective-permute-start(f32[2,40,512]{2,1,0:T(8,128)S(1)} %get-tuple-element.83), channel_id=1, source_target_pairs={{0,1},{1,0},{2,3},{3,2},{4,5},{5,4},{6,7},{7,6},{8,9},{9,8},{10,11... | collective-permute-start | bytes 491528 | tf_op jit(solution)/shard_map/ppermute | solution.py:838
  80.3 8.7 %collective-permute-start.26 = (f32[64,512]{1,0:T(8,128)S(1)}, f32[64,512]{1,0:T(8,128)S(1)}, u32[]{:S(2)}, u32[]{:S(2)}) collective-permute-start(f32[64,512]{1,0:T(8,128)S(1)} %get-tuple-element.84.refs_0_), channel_id=1, source_target_pairs={{0,4},{2,6},{4,0},{6,2},{1,5},{3,7},{5,1},{7,3},{8,12},{10,14},{12... | collective-permute-start | bytes 393224 | tf_op jit(solution)/shard_map/ppermute | solution.py:860
  81.3 9.5 %collective-permute-start.27 = (f32[64,512]{1,0:T(8,128)S(1)}, f32[64,512]{1,0:T(8,128)S(1)}, u32[]{:S(2)}, u32[]{:S(2)}) collective-permute-start(f32[64,512]{1,0:T(8,128)S(1)} %get-tuple-element.84.refs_0_), channel_id=1, source_target_pairs={{0,2},{2,4},{4,6},{6,0},{1,3},{3,5},{5,7},{7,1},{8,10},{10,12},{12... | collective-permute-start | bytes 393224 | tf_op jit(solution)/shard_map/ppermute | solution.py:860
  85.3 6.9 %collective-permute-start.28 = (f32[64,512]{1,0:T(8,128)S(1)}, f32[64,512]{1,0:T(8,128)S(1)}, u32[]{:S(2)}, u32[]{:S(2)}) collective-permute-start(f32[64,512]{1,0:T(8,128)S(1)} %collective-permute-done.22.refs_4_), channel_id=1, source_target_pairs={{0,6},{2,0},{4,2},{6,4},{1,7},{3,1},{5,3},{7,5},{8,14},{10,8},{12,... | collective-permute-start | bytes 393224 | tf_op jit(solution)/shard_map/ppermute | solution.py:860
  86.5 7.8 %collective-permute-start.29 = (f32[64,512]{1,0:T(8,128)S(1)}, f32[64,512]{1,0:T(8,128)S(1)}, u32[]{:S(2)}, u32[]{:S(2)}) collective-permute-start(f32[64,512]{1,0:T(8,128)S(1)} %collective-permute-done.22.refs_4_), channel_id=1, source_target_pairs={{0,4},{2,6},{4,0},{6,2},{1,5},{3,7},{5,1},{7,3},{8,12},{10,14},{12... | collective-permute-start | bytes 393224 | tf_op jit(solution)/shard_map/ppermute | solution.py:860
  86.6 9.0 %collective-permute-start.30 = (f32[64,512]{1,0:T(8,128)S(1)}, f32[64,512]{1,0:T(8,128)S(1)}, u32[]{:S(2)}, u32[]{:S(2)}) collective-permute-start(f32[64,512]{1,0:T(8,128)S(1)} %collective-permute-done.22.refs_4_), channel_id=1, source_target_pairs={{0,2},{2,4},{4,6},{6,0},{1,3},{3,5},{5,7},{7,1},{8,10},{10,12},{12... | collective-permute-start | bytes 393224 | tf_op jit(solution)/shard_map/ppermute | solution.py:860
  99.9 6.7 %collective-permute-start.31 = (f32[2,128,256]{2,1,0:T(8,128)S(1)}, f32[2,128,256]{2,1,0:T(8,128)S(1)}, u32[]{:S(2)}, u32[]{:S(2)}) collective-permute-start(f32[2,128,256]{2,1,0:T(8,128)S(1)} %get-tuple-element.92), channel_id=1, source_target_pairs={{0,1},{1,0},{2,3},{3,2},{4,5},{5,4},{6,7},{7,6},{8,9},{9,8},{10,11... | collective-permute-start | bytes 786440 | tf_op jit(solution)/shard_map/ppermute | solution.py:838
  100.0 13.7 %all-to-all-start.1 = ((f32[8,64,128]{2,1,0:T(8,128)}), f32[8,64,128]{2,1,0:T(8,128)S(1)}, u32[]{:S(2)}, u32[]{:S(2)}) async-start(f32[8,64,128]{2,1,0:T(8,128)} %pair_to_facets.1), calls=%async_computation.1 | async-start | bytes 524288 | tf_op jit(solution)/shard_map/all_to_all | solution.py:922
  113.7 19.5 %all-to-all-start.2 = ((f32[8,72,512]{2,1,0:T(8,128)}), f32[8,72,512]{2,1,0:T(8,128)S(1)}, u32[]{:S(2)}, u32[]{:S(2)}) async-start(f32[8,72,512]{2,1,0:T(8,128)} %backward.3), calls=%async_computation.2 | async-start | bytes 2359296 | tf_op jit(solution)/shard_map/all_to_all | solution.py:926
  124.3 18.1 %collective-permute-start.23 = (f32[8,40,128]{2,1,0:T(8,128)S(1)}, f32[8,40,128]{2,1,0:T(8,128)S(1)}, u32[]{:S(2)}, u32[]{:S(2)}) collective-permute-start(f32[8,40,128]{2,1,0:T(8,128)S(1)} %get-tuple-element.88), channel_id=1, source_target_pairs={{0,16},{16,32},{32,48},{48,64},{64,80},{80,96},{96,112},{1,17},{17... | collective-permute-start | bytes 491528 | tf_op jit(solution)/shard_map/ppermute | solution.py:868
  128.6 13.8 %collective-permute-start.24 = (f32[8,40,128]{2,1,0:T(8,128)S(1)}, f32[8,40,128]{2,1,0:T(8,128)S(1)}, u32[]{:S(2)}, u32[]{:S(2)}) collective-permute-start(f32[8,40,128]{2,1,0:T(8,128)S(1)} %get-tuple-element.89), channel_id=1, source_target_pairs={{16,0},{32,16},{48,32},{64,48},{80,64},{96,80},{112,96},{17,1},{33... | collective-permute-start | bytes 491528 | tf_op jit(solution)/shard_map/ppermute | solution.py:868
  135.4 16.6 %all-to-all-start.3 = ((f32[8,48,128]{2,1,0:T(8,128)}), f32[8,48,128]{2,1,0:T(8,128)S(1)}, u32[]{:S(2)}, u32[]{:S(2)}) async-start(f32[8,48,128]{2,1,0:T(8,128)} %to_facets.1), calls=%async_computation.3 | async-start | bytes 393216 | tf_op jit(solution)/shard_map/all_to_all | solution.py:939
  142.5 7.7 %collective-permute-start.33 = (f32[8,2,8,128]{3,2,1,0:T(8,128)S(1)}, f32[8,2,8,128]{3,2,1,0:T(8,128)S(1)}, u32[]{:S(2)}, u32[]{:S(2)}) collective-permute-start(f32[8,2,8,128]{3,2,1,0:T(8,128)S(1)} %get-tuple-element.101), channel_id=1, source_target_pairs={{0,1},{1,2},{2,3},{3,4},{4,5},{5,6},{6,7},{7,8},{8,9},{9,10},{10,1... | collective-permute-start | bytes 196616 | tf_op jit(solution)/shard_map/ppermute | solution.py:868
  144.4 7.6 %collective-permute-start.34 = (f32[8,2,8,128]{3,2,1,0:T(8,128)S(1)}, f32[8,2,8,128]{3,2,1,0:T(8,128)S(1)}, u32[]{:S(2)}, u32[]{:S(2)}) collective-permute-start(f32[8,2,8,128]{3,2,1,0:T(8,128)S(1)} %get-tuple-element.100), channel_id=1, source_target_pairs={{1,0},{2,1},{3,2},{4,3},{5,4},{6,5},{7,6},{8,7},{9,8},{10,9},{11,1... | collective-permute-start | bytes 196616 | tf_op jit(solution)/shard_map/ppermute | solution.py:868
  (34 other events, 200.5 us)

commit v5 on v4

--- a/solution.py
+++ b/solution.py
@@ -891,10 +891,12 @@
     )
 
     packed = start(filters.transpose(2, 1, 0), level_counts, sky_image, dual_coefs)
+
+    weight_own = grid_weight[0, 0]
+    weight_other, phase, packed = lax.optimization_barrier(
+        (swapped(weight_own), phase_screen[0, 0], packed)
+    )
     sent = lax.all_to_all(packed, "chan", 0, 0, tiled=True)
-
-    weight_own = grid_weight[0, 0]
-    weight_other, phase = lax.optimization_barrier((swapped(weight_own), phase_screen[0, 0]))
     phase_other = half_of(phase, 1 - half, 512, 1)
     data_own = visibilities[0, 0].reshape(128, 256)
     data = jnp.stack([data_own, swapped(data_own)])
@@ -902,8 +904,8 @@
     rows_other = swapped(rows_own.astype(F32)).astype(jnp.int32)
     left, right = tables(jnp.stack([rows_own, rows_other]))
     grid = gridding(weight_own, weight_other)
-    sent, grid, phase_other = lax.optimization_barrier((sent, grid, phase_other))
-    trig = screens(phase, swapped(phase_other))
+    sent, grid, phase_other = lax.optimization_barrier((sent, grid, swapped(phase_other)))
+    trig = screens(phase, phase_other)
 
     own, other, term_own, term_other = split(sent)
     strip = join_rows(own, swapped(other))

time: 159 us -> 160 us (level)
  waiting for transfers between devices: 36.8 us -> 31.6 us
  starting transfers between devices: 66 us -> 68.6 us
  local copies, waits for them, and re-layouts: 5.05 us -> 7.17 us
    ppermute x7, starting transfers between devices: 6.75 us -> 10.2 us  [to_chips(): arrived.append(lax.ppermute(pieces[i], CHIPS, route))]
    ppermute x7, waiting for transfers between devices: 13.8 us -> 10.3 us  [to_chips(): arrived.append(lax.ppermute(pieces[i], CHIPS, route))]
    ppermute x10, waiting for transfers between devices: 5.52 us -> 3.74 us  [swapped(): return lax.ppermute(value, 'core', [(0, 1), (1, 0)])]
    unnamed x54 -> x36, local copies, waits for them, and re-layouts: 3.48 us -> 4.27 us
  transfers between devices with their start and end apart: 39 -> 39, of which waited for: 19 -> 19; matrix products, arithmetic and copies ran while one was open for 1% -> 1% of each run, Pallas kernels for 17% -> 19%
where the time goes in v5:
time: 160 us; the launch traced here: 157 us
  starting transfers between devices  68.6 us (43%)
  Pallas kernels  48.5 us (30%)
  waiting for transfers between devices  31.6 us (20%)
  local copies, waits for them, and re-layouts  7.17 us (4%)
    ppermute x4, starting transfers between devices, neighbours(): lax.ppermute(value, axis, [(i, i + step) for i in range(count) if 0 <= i...  15.2 us
    ppermute x12, starting transfers between devices, along_x(): return lax.ppermute(value, 'x', [(i, (i + step) % 4) for i in range(4)])  14.1 us
    pallas_call x2, Pallas kernels, backward(): pl.pallas_call(backward_kernel, in_specs=[VMEM] * len(args) + [ANY] * 2,...  11.2 us
    ppermute x7, waiting for transfers between devices, to_chips(): arrived.append(lax.ppermute(pieces[i], CHIPS, route))  10.3 us
    ppermute x7, starting transfers between devices, to_chips(): arrived.append(lax.ppermute(pieces[i], CHIPS, route))  10.2 us
    pallas_call x2, Pallas kernels, forward(): pl.pallas_call(functools.partial(forward_kernel, windows=windows), in_spe...  9.69 us
    ppermute x12, waiting for transfers between devices, along_x(): return lax.ppermute(value, 'x', [(i, (i + step) % 4) for i in range(4)])  9.14 us
    all_to_all x1, starting transfers between devices, per_device(): sent = lax.all_to_all(packed, 'chan', 0, 0, tiled=True)  8.28 us
  transfers between devices with their start and end apart: 39, of which 19 were waited for; matrix products, arithmetic and copies ran while one was open for 1% of the time, Pallas kernels for 19%

profile of v5, /device:TPU:24, one launch (start us, length us, event | category | flops | bytes accessed | tf_op | source)
XLA Modules:
  0.0 157.2 jit_solution(17087634549475292272)
XLA Ops:
  1.4 4.2 %start.1 = f32[8,80,128]{2,1,0:T(8,128)} custom-call(f32[3,2,9]{2,1,0:T(2,128)S(1)} %bitcast.27, s32[9]{0:T(128)} %level_ref.1, f32[8,32,128]{2,1,0:T(8,128)} %before_ref.1, f32[9,8,32,128]{3,2,1,0:T(8,128)} %dual_ref.3), custom_call_target="tpu_custom_call" | custom-call | bytes 12000000 | tf_op jit(solution)/shard_map/start/pallas_call | solution.py:719
  6.7 2.4 %constant_dynamic-slice_fusion = f32[512,512]{1,0:T(8,128)} fusion(f32[512,1024]{1,0:T(8,128)} %bitcast.29, s32[]{:T(128)S(6)} %select_n.16), kind=kLoop, calls=%fused_computation.17 | loop fusion | bytes 2097156 | tf_op jit(solution)/shard_map/dynamic_slice | solution.py:874
  9.6 8.3 %all-to-all-start = ((f32[8,80,128]{2,1,0:T(8,128)}), f32[8,80,128]{2,1,0:T(8,128)S(1)}, u32[]{:S(2)}, u32[]{:S(2)}) async-start(f32[8,80,128]{2,1,0:T(8,128)} %start.1), calls=%async_computation | async-start | bytes 655360 | tf_op jit(solution)/shard_map/all_to_all | solution.py:899
  19.1 3.7 %gridding.1.refs_10_.rest_2_.rest_1_ = bf16[2,2,2,2,256,256]{5,4,3,2,1,0:T(8,128)(2,1)} custom-call(f32[1024,256]{1,0:T(8,128)S(1)} %bitcast.26, f32[1024,256]{1,0:T(8,128)S(1)} %copy-done.3, bf16[1024,256]{1,0:T(8,128)(2,1)S(1)} %copy-done.4, f32[256,8]{1,0:T(8,128)S(1)} %copy-done.8), custom_call_target="tpu_custom_call" | custom-call | bytes 9000000 | tf_op jit(solution)/shard_map/gridding/pallas_call | solution.py:228
  22.8 2.0 %all-to-all-done.sent_ref = f32[8,80,128]{2,1,0:T(8,128)S(1)} async-done(((f32[8,80,128]{2,1,0:T(8,128)}), f32[8,80,128]{2,1,0:T(8,128)S(1)}, u32[]{:S(2)}, u32[]{:S(2)}) %all-to-all-start) | async-done | bytes 327712 | tf_op jit(solution)/shard_map/all_to_all | solution.py:899
  28.0 2.8 %collective-permute-start.3 = (f32[64,512]{1,0:T(8,128)S(1)}, f32[64,512]{1,0:T(8,128)S(1)}, u32[]{:S(2)}, u32[]{:S(2)}) collective-permute-start(f32[64,512]{1,0:T(8,128)S(1)} %join_rows.1.refs_0_), channel_id=1, source_target_pairs={{0,6},{2,0},{4,2},{6,4},{1,7},{3,1},{5,3},{7,5},{8,14},{10,8},{12,... | collective-permute-start | bytes 393224 | tf_op jit(solution)/shard_map/ppermute | solution.py:860
  32.9 2.8 %collective-permute-start.7 = (f32[64,512]{1,0:T(8,128)}, f32[64,512]{1,0:T(8,128)}, u32[]{:S(2)}, u32[]{:S(2)}) collective-permute-start(f32[64,512]{1,0:T(8,128)} %collective-permute-done.6.refs_4_), channel_id=1, source_target_pairs={{0,6},{2,0},{4,2},{6,4},{1,7},{3,1},{5,3},{7,5},{8,14},{10,8},{12,... | collective-permute-start | bytes 393224 | tf_op jit(solution)/shard_map/ppermute | solution.py:860
  38.8 2.6 %tables.1 = (bf16[2,256,512]{2,1,0:T(8,128)(2,1)}, bf16[2,512,256]{2,1,0:T(8,128)(2,1)}) custom-call(s32[2,128,1]{2,1,0:T(8,128)S(1)} %copy.23.gcol_ref, s32[2,1,128]{2,1,0:T(1,128)S(1)} %bitcast.28), custom_call_target="tpu_custom_call" | custom-call | bytes 6000000 | tf_op jit(solution)/shard_map/tables/pallas_call | solution.py:157
  41.4 2.8 %screens.1.refs_8_.trig_ref = s16[2,2,2,512,256]{4,3,2,1,0:T(8,128)(2,1)S(1)} custom-call(f32[512,512]{1,0:T(8,128)S(1)} %collective-permute-done.1.other_ref, f32[512,1024]{1,0:T(8,128)} %bitcast.30), custom_call_target="tpu_custom_call" | custom-call | bytes 12000000 | tf_op jit(solution)/shard_map/screens/pallas_call | solution.py:124
  46.8 5.4 %forward.2 = (f32[2,128,256]{2,1,0:T(8,128)S(1)}, f32[2,128,256]{2,1,0:T(8,128)S(1)}, f32[72,512]{1,0:T(8,128)S(1)}) custom-call(f32[64,512]{1,0:T(8,128)S(1)} %join_rows.1.refs_0_, f32[64,512]{1,0:T(8,128)S(1)} %copy-done.7, f32[64,512]{1,0:T(8,128)} %collective-permute-done.4.refs_2_, f32[64,512]{1,0:T(8,128)} %collective-permute-done.5.refs_3_, ...), custom_call_target="tpu_custom_call" | custom-call | bytes 15000000 | tf_op jit(solution)/shard_map/forward/pallas_call | solution.py:300
  53.8 5.1 %backward.2 = (f32[72,512]{1,0:T(8,128)S(1)}, f32[72,512]{1,0:T(8,128)S(1)}, f32[72,512]{1,0:T(8,128)S(1)}, f32[72,512]{1,0:T(8,128)S(1)}, f32[72,512]{1,0:T(8,1...) custom-call(f32[2,128,256]{2,1,0:T(8,128)S(1)} %get-tuple-element.70.mine_ref, ...), custom_call_target="tpu_custom_call" | custom-call | bytes 15000000 | tf_op jit(solution)/shard_map/backward/pallas_call | solution.py:359
  59.3 2.5 %collective-permute-start.15 = (f32[72,512]{1,0:T(8,128)S(1)}, f32[72,512]{1,0:T(8,128)S(1)}, u32[]{:S(2)}, u32[]{:S(2)}) collective-permute-start(f32[72,512]{1,0:T(8,128)S(1)} %get-tuple-element.77), channel_id=1, source_target_pairs={{0,4},{2,6},{4,0},{6,2},{8,12},{10,14},{12,8},{14,10},{1,5},{3,7},... | collective-permute-start | bytes 442376 | tf_op jit(solution)/shard_map/ppermute | solution.py:851
  61.8 2.5 %collective-permute-start.16 = (f32[72,512]{1,0:T(8,128)S(1)}, f32[72,512]{1,0:T(8,128)S(1)}, u32[]{:S(2)}, u32[]{:S(2)}) collective-permute-start(f32[72,512]{1,0:T(8,128)S(1)} %get-tuple-element.78), channel_id=1, source_target_pairs={{0,6},{2,0},{4,2},{6,4},{8,14},{10,8},{12,10},{14,12},{1,7},{3,1},... | collective-permute-start | bytes 442376 | tf_op jit(solution)/shard_map/ppermute | solution.py:851
  65.7 3.4 %collective-permute-done.14.refs_1_ = f32[72,512]{1,0:T(8,128)S(1)} collective-permute-done((f32[72,512]{1,0:T(8,128)S(1)}, f32[72,512]{1,0:T(8,128)S(1)}, u32[]{:S(2)}, u32[]{:S(2)}) %collective-permute-start.14) | collective-permute-done | bytes 147488 | tf_op jit(solution)/shard_map/ppermute | solution.py:851
  69.2 3.2 %collective-permute-start.19 = (f32[72,512]{1,0:T(8,128)S(1)}, f32[72,512]{1,0:T(8,128)S(1)}, u32[]{:S(2)}, u32[]{:S(2)}) collective-permute-start(f32[72,512]{1,0:T(8,128)S(1)} %get-tuple-element.81), channel_id=1, source_target_pairs={{0,12},{2,14},{4,8},{6,10},{8,4},{10,6},{12,0},{14,2},{1,13},{3,15... | collective-permute-start | bytes 442376 | tf_op jit(solution)/shard_map/ppermute | solution.py:851
  72.7 2.9 %collective-permute-done.18.refs_5_ = f32[72,512]{1,0:T(8,128)S(1)} collective-permute-done((f32[72,512]{1,0:T(8,128)S(1)}, f32[72,512]{1,0:T(8,128)S(1)}, u32[]{:S(2)}, u32[]{:S(2)}) %collective-permute-start.18) | collective-permute-done | bytes 147488 | tf_op jit(solution)/shard_map/ppermute | solution.py:851
  75.6 2.4 %collective-permute-done.19.refs_6_ = f32[72,512]{1,0:T(8,128)S(1)} collective-permute-done((f32[72,512]{1,0:T(8,128)S(1)}, f32[72,512]{1,0:T(8,128)S(1)}, u32[]{:S(2)}, u32[]{:S(2)}) %collective-permute-start.19) | collective-permute-done | bytes 147488 | tf_op jit(solution)/shard_map/ppermute | solution.py:851
  83.7 1.9 %collective-permute-done.22.refs_4_ = f32[64,512]{1,0:T(8,128)S(1)} collective-permute-done((f32[64,512]{1,0:T(8,128)S(1)}, f32[64,512]{1,0:T(8,128)S(1)}, u32[]{:S(2)}, u32[]{:S(2)}) %collective-permute-start.22) | collective-permute-done | bytes 131104 | tf_op jit(solution)/shard_map/ppermute | solution.py:856
  89.6 2.6 %collective-permute-done.27.refs_3_ = f32[64,512]{1,0:T(8,128)S(1)} collective-permute-done((f32[64,512]{1,0:T(8,128)S(1)}, f32[64,512]{1,0:T(8,128)S(1)}, u32[]{:S(2)}, u32[]{:S(2)}) %collective-permute-start.27) | collective-permute-done | bytes 131104 | tf_op jit(solution)/shard_map/ppermute | solution.py:860
  92.6 2.2 %collective-permute-done.29.refs_6_ = f32[64,512]{1,0:T(8,128)S(1)} collective-permute-done((f32[64,512]{1,0:T(8,128)S(1)}, f32[64,512]{1,0:T(8,128)S(1)}, u32[]{:S(2)}, u32[]{:S(2)}) %collective-permute-start.29) | collective-permute-done | bytes 131104 | tf_op jit(solution)/shard_map/ppermute | solution.py:860
  96.3 4.2 %forward.3 = (f32[2,128,256]{2,1,0:T(8,128)S(1)}, f32[2,128,256]{2,1,0:T(8,128)S(1)}) custom-call(f32[64,512]{1,0:T(8,128)S(1)} %get-tuple-element.86.refs_0_, f32[64,512]{1,0:T(8,128)S(1)} %collective-permute-done.25.refs_1_, f32[64,512]{1,0:T(8,128)S(1)} %collective-permute-done.26.refs_2_, f32[64,512]{1,0:T(8,128)S(1)} %collective-permute-done.27.refs_3_, ...), custom_call_target="tpu_custom_call" | custom-call | bytes 15000000 | tf_op jit(solution)/shard_map/forward/pallas_call | solution.py:300
  100.6 6.5 %all-to-all-start.1 = ((f32[8,64,128]{2,1,0:T(8,128)}), f32[8,64,128]{2,1,0:T(8,128)S(1)}, u32[]{:S(2)}, u32[]{:S(2)}) async-start(f32[8,64,128]{2,1,0:T(8,128)} %pair_to_facets.1), calls=%async_computation.1 | async-start | bytes 524288 | tf_op jit(solution)/shard_map/all_to_all | solution.py:924
  107.1 6.1 %backward.3 = f32[8,72,512]{2,1,0:T(8,128)} custom-call(f32[2,128,256]{2,1,0:T(8,128)S(1)} %get-tuple-element.93.mine_ref, f32[2,128,256]{2,1,0:T(8,128)S(1)} %collective-permute-done.31.theirs_ref, f32[2,128,256]{2,1,0:T(8,128)S(1)} %pad_maximum_fusion.1.data_ref, s16[2,2,2,512,256]{4,3,2,1,0:T(8,128)(2,1)S(1)} %screens.1.refs_8_.trig_ref, ...), custom_call_target="tpu_custom_call" | custom-call | bytes 15000000 | tf_op jit(solution)/shard_map/backward/pallas_call | solution.py:359
  114.2 4.1 %all-to-all-start.2 = ((f32[8,72,512]{2,1,0:T(8,128)}), f32[8,72,512]{2,1,0:T(8,128)S(1)}, u32[]{:S(2)}, u32[]{:S(2)}) async-start(f32[8,72,512]{2,1,0:T(8,128)} %backward.3), calls=%async_computation.2 | async-start | bytes 2359296 | tf_op jit(solution)/shard_map/all_to_all | solution.py:928
  118.8 6.2 %middle.1 = (f32[9,8,32,128]{3,2,1,0:T(8,128)}, f32[8,80,128]{2,1,0:T(8,128)}, f32[8,40,128]{2,1,0:T(8,128)S(1)}, f32[8,40,128]{2,1,0:T(8,128)S(1)}, f32[8,80,128]{2,1,0:T(8,128)}) custom-call(f32[9,8]{1,0:T(8,128)S(1)} %pad_maximum_fusion.2.scal_ref, f32[8,32,128]{2,1,0:T(8,128)} %before_ref.1, f32[8,64,128]{2,1,0:T(8,128)S(1)} %all-to-all-done.1.pair_ref, ...), custom_call_target="tpu_custom_call" | custom-call | bytes 21000000 | tf_op jit(solution)/shard_map/middle/pallas_call | solution.py:775
  125.0 4.2 %collective-permute-start.23 = (f32[8,40,128]{2,1,0:T(8,128)S(1)}, f32[8,40,128]{2,1,0:T(8,128)S(1)}, u32[]{:S(2)}, u32[]{:S(2)}) collective-permute-start(f32[8,40,128]{2,1,0:T(8,128)S(1)} %get-tuple-element.90), channel_id=1, source_target_pairs={{0,16},{16,32},{32,48},{48,64},{64,80},{80,96},{96,112},{1,17},{17... | collective-permute-start | bytes 491528 | tf_op jit(solution)/shard_map/ppermute | solution.py:868
  129.3 3.2 %collective-permute-start.24 = (f32[8,40,128]{2,1,0:T(8,128)S(1)}, f32[8,40,128]{2,1,0:T(8,128)S(1)}, u32[]{:S(2)}, u32[]{:S(2)}) collective-permute-start(f32[8,40,128]{2,1,0:T(8,128)S(1)} %get-tuple-element.91), channel_id=1, source_target_pairs={{16,0},{32,16},{48,32},{64,48},{80,64},{96,80},{112,96},{17,1},{33... | collective-permute-start | bytes 491528 | tf_op jit(solution)/shard_map/ppermute | solution.py:868
  136.2 7.0 %all-to-all-start.3 = ((f32[8,48,128]{2,1,0:T(8,128)}), f32[8,48,128]{2,1,0:T(8,128)S(1)}, u32[]{:S(2)}, u32[]{:S(2)}) async-start(f32[8,48,128]{2,1,0:T(8,128)} %to_facets.1), calls=%async_computation.3 | async-start | bytes 393216 | tf_op jit(solution)/shard_map/all_to_all | solution.py:941
  143.2 1.9 %collective-permute-start.33 = (f32[8,2,8,128]{3,2,1,0:T(8,128)S(1)}, f32[8,2,8,128]{3,2,1,0:T(8,128)S(1)}, u32[]{:S(2)}, u32[]{:S(2)}) collective-permute-start(f32[8,2,8,128]{3,2,1,0:T(8,128)S(1)} %get-tuple-element.103), channel_id=1, source_target_pairs={{0,1},{1,2},{2,3},{3,4},{4,5},{5,6},{6,7},{7,8},{8,9},{9,10},{10,1... | collective-permute-start | bytes 196616 | tf_op jit(solution)/shard_map/ppermute | solution.py:868
  145.2 5.8 %collective-permute-start.34 = (f32[8,2,8,128]{3,2,1,0:T(8,128)S(1)}, f32[8,2,8,128]{3,2,1,0:T(8,128)S(1)}, u32[]{:S(2)}, u32[]{:S(2)}) collective-permute-start(f32[8,2,8,128]{3,2,1,0:T(8,128)S(1)} %get-tuple-element.102), channel_id=1, source_target_pairs={{1,0},{2,1},{3,2},{4,3},{5,4},{6,5},{7,6},{8,7},{9,8},{10,9},{11,1... | collective-permute-start | bytes 196616 | tf_op jit(solution)/shard_map/ppermute | solution.py:868
  151.0 1.8 %collective-permute-done.34.below_ref = f32[8,2,8,128]{3,2,1,0:T(8,128)S(1)} collective-permute-done((f32[8,2,8,128]{3,2,1,0:T(8,128)S(1)}, f32[8,2,8,128]{3,2,1,0:T(8,128)S(1)}, u32[]{:S(2)}, u32[]{:S(2)}) %collective-permute-start.34) | collective-permute-done | bytes 65568 | tf_op jit(solution)/shard_map/ppermute | solution.py:868
  152.8 4.4 %last.1 = (f32[8,32,128]{2,1,0:T(8,128)}, f32[9,8,32,128]{3,2,1,0:T(8,128)}) custom-call(f32[9,8]{1,0:T(8,128)S(1)} %pad_maximum_fusion.2.scal_ref, f32[8,80,128]{2,1,0:T(8,128)S(1)} %copy-done.5, f32[8,80,128]{2,1,0:T(8,128)S(1)} %bitcast.24, f32[8,2,8,128]{3,2,1,0:T(8,128)S(1)} %collective-permute-done.33.above_ref, ...), custom_call_target="tpu_custom_call" | custom-call | bytes 12000000 | tf_op jit(solution)/shard_map/last/pallas_call | solution.py:821
  (116 shorter events, 34.9 us)
Async XLA Ops:
  9.1 15.8 %collective-permute-start.1 = (f32[512,512]{1,0:T(8,128)}, f32[512,512]{1,0:T(8,128)S(1)}, u32[]{:S(2)}, u32[]{:S(2)}) collective-permute-start(f32[512,512]{1,0:T(8,128)} %constant_dynamic-slice_fusion), channel_id=1, source_target_pairs={{0,1},{1,0},{2,3},{3,2},{4,5},{5,4},{6,7},{7,6},{8,9},{9,8},{10,11... | collective-permute-start | bytes 3145736 | tf_op jit(solution)/shard_map/ppermute | solution.py:838
  9.6 15.3 %all-to-all-start = ((f32[8,80,128]{2,1,0:T(8,128)}), f32[8,80,128]{2,1,0:T(8,128)S(1)}, u32[]{:S(2)}, u32[]{:S(2)}) async-start(f32[8,80,128]{2,1,0:T(8,128)} %start.1), calls=%async_computation | async-start | bytes 655360 | tf_op jit(solution)/shard_map/all_to_all | solution.py:899
  17.9 13.8 %collective-permute-start.11 = (f32[128,256]{1,0:T(8,128)S(1)}, f32[128,256]{1,0:T(8,128)S(1)}, u32[]{:S(2)}, u32[]{:S(2)}) collective-permute-start(f32[128,256]{1,0:T(8,128)S(1)} %bitcast.31), channel_id=1, source_target_pairs={{0,1},{1,0},{2,3},{3,2},{4,5},{5,4},{6,7},{7,6},{8,9},{9,8},{10,11... | collective-permute-start | bytes 393224 | tf_op jit(solution)/shard_map/ppermute | solution.py:838
  28.0 9.1 %collective-permute-start.3 = (f32[64,512]{1,0:T(8,128)S(1)}, f32[64,512]{1,0:T(8,128)S(1)}, u32[]{:S(2)}, u32[]{:S(2)}) collective-permute-start(f32[64,512]{1,0:T(8,128)S(1)} %join_rows.1.refs_0_), channel_id=1, source_target_pairs={{0,6},{2,0},{4,2},{6,4},{1,7},{3,1},{5,3},{7,5},{8,14},{10,8},{12,... | collective-permute-start | bytes 393224 | tf_op jit(solution)/shard_map/ppermute | solution.py:860
  30.8 14.4 %collective-permute-start.4 = (f32[64,512]{1,0:T(8,128)S(1)}, f32[64,512]{1,0:T(8,128)}, u32[]{:S(2)}, u32[]{:S(2)}) collective-permute-start(f32[64,512]{1,0:T(8,128)S(1)} %join_rows.1.refs_0_), channel_id=1, source_target_pairs={{0,4},{2,6},{4,0},{6,2},{1,5},{3,7},{5,1},{7,3},{8,12},{10,14},{12... | collective-permute-start | bytes 393224 | tf_op jit(solution)/shard_map/ppermute | solution.py:860
  31.6 13.6 %collective-permute-start.5 = (f32[64,512]{1,0:T(8,128)S(1)}, f32[64,512]{1,0:T(8,128)}, u32[]{:S(2)}, u32[]{:S(2)}) collective-permute-start(f32[64,512]{1,0:T(8,128)S(1)} %join_rows.1.refs_0_), channel_id=1, source_target_pairs={{0,2},{2,4},{4,6},{6,0},{1,3},{3,5},{5,7},{7,1},{8,10},{10,12},{12... | collective-permute-start | bytes 393224 | tf_op jit(solution)/shard_map/ppermute | solution.py:860
  32.9 12.3 %collective-permute-start.7 = (f32[64,512]{1,0:T(8,128)}, f32[64,512]{1,0:T(8,128)}, u32[]{:S(2)}, u32[]{:S(2)}) collective-permute-start(f32[64,512]{1,0:T(8,128)} %collective-permute-done.6.refs_4_), channel_id=1, source_target_pairs={{0,6},{2,0},{4,2},{6,4},{1,7},{3,1},{5,3},{7,5},{8,14},{10,8},{12,... | collective-permute-start | bytes 393224 | tf_op jit(solution)/shard_map/ppermute | solution.py:860
  36.3 8.9 %collective-permute-start.8 = (f32[64,512]{1,0:T(8,128)}, f32[64,512]{1,0:T(8,128)}, u32[]{:S(2)}, u32[]{:S(2)}) collective-permute-start(f32[64,512]{1,0:T(8,128)} %collective-permute-done.6.refs_4_), channel_id=1, source_target_pairs={{0,4},{2,6},{4,0},{6,2},{1,5},{3,7},{5,1},{7,3},{8,12},{10,14},{12... | collective-permute-start | bytes 393224 | tf_op jit(solution)/shard_map/ppermute | solution.py:860
  37.7 9.0 %collective-permute-start.9 = (f32[64,512]{1,0:T(8,128)}, f32[64,512]{1,0:T(8,128)}, u32[]{:S(2)}, u32[]{:S(2)}) collective-permute-start(f32[64,512]{1,0:T(8,128)} %collective-permute-done.6.refs_4_), channel_id=1, source_target_pairs={{0,2},{2,4},{4,6},{6,0},{1,3},{3,5},{5,7},{7,1},{8,10},{10,12},{12... | collective-permute-start | bytes 393224 | tf_op jit(solution)/shard_map/ppermute | solution.py:860
  59.0 10.2 %collective-permute-start.14 = (f32[72,512]{1,0:T(8,128)S(1)}, f32[72,512]{1,0:T(8,128)S(1)}, u32[]{:S(2)}, u32[]{:S(2)}) collective-permute-start(f32[72,512]{1,0:T(8,128)S(1)} %get-tuple-element.76), channel_id=1, source_target_pairs={{0,2},{2,4},{4,6},{6,0},{8,10},{10,12},{12,14},{14,8},{1,3},{3,5},... | collective-permute-start | bytes 442376 | tf_op jit(solution)/shard_map/ppermute | solution.py:851
  59.3 13.1 %collective-permute-start.15 = (f32[72,512]{1,0:T(8,128)S(1)}, f32[72,512]{1,0:T(8,128)S(1)}, u32[]{:S(2)}, u32[]{:S(2)}) collective-permute-start(f32[72,512]{1,0:T(8,128)S(1)} %get-tuple-element.77), channel_id=1, source_target_pairs={{0,4},{2,6},{4,0},{6,2},{8,12},{10,14},{12,8},{14,10},{1,5},{3,7},... | collective-permute-start | bytes 442376 | tf_op jit(solution)/shard_map/ppermute | solution.py:851
  61.8 10.8 %collective-permute-start.16 = (f32[72,512]{1,0:T(8,128)S(1)}, f32[72,512]{1,0:T(8,128)S(1)}, u32[]{:S(2)}, u32[]{:S(2)}) collective-permute-start(f32[72,512]{1,0:T(8,128)S(1)} %get-tuple-element.78), channel_id=1, source_target_pairs={{0,6},{2,0},{4,2},{6,4},{8,14},{10,8},{12,10},{14,12},{1,7},{3,1},... | collective-permute-start | bytes 442376 | tf_op jit(solution)/shard_map/ppermute | solution.py:851
  64.4 8.3 %collective-permute-start.17 = (f32[72,512]{1,0:T(8,128)S(1)}, f32[72,512]{1,0:T(8,128)S(1)}, u32[]{:S(2)}, u32[]{:S(2)}) collective-permute-start(f32[72,512]{1,0:T(8,128)S(1)} %get-tuple-element.79), channel_id=1, source_target_pairs={{0,8},{2,10},{4,12},{6,14},{8,0},{10,2},{12,4},{14,6},{1,9},{3,11}... | collective-permute-start | bytes 442376 | tf_op jit(solution)/shard_map/ppermute | solution.py:851
  65.7 9.8 %collective-permute-start.18 = (f32[72,512]{1,0:T(8,128)S(1)}, f32[72,512]{1,0:T(8,128)S(1)}, u32[]{:S(2)}, u32[]{:S(2)}) collective-permute-start(f32[72,512]{1,0:T(8,128)S(1)} %get-tuple-element.80), channel_id=1, source_target_pairs={{0,10},{2,12},{4,14},{6,8},{8,2},{10,4},{12,6},{14,0},{1,11},{3,13... | collective-permute-start | bytes 442376 | tf_op jit(solution)/shard_map/ppermute | solution.py:851
  69.2 8.8 %collective-permute-start.19 = (f32[72,512]{1,0:T(8,128)S(1)}, f32[72,512]{1,0:T(8,128)S(1)}, u32[]{:S(2)}, u32[]{:S(2)}) collective-permute-start(f32[72,512]{1,0:T(8,128)S(1)} %get-tuple-element.81), channel_id=1, source_target_pairs={{0,12},{2,14},{4,8},{6,10},{8,4},{10,6},{12,0},{14,2},{1,13},{3,15... | collective-permute-start | bytes 442376 | tf_op jit(solution)/shard_map/ppermute | solution.py:851
  72.4 7.1 %collective-permute-start.20 = (f32[72,512]{1,0:T(8,128)S(1)}, f32[72,512]{1,0:T(8,128)S(1)}, u32[]{:S(2)}, u32[]{:S(2)}) collective-permute-start(f32[72,512]{1,0:T(8,128)S(1)} %get-tuple-element.82), channel_id=1, source_target_pairs={{0,14},{2,8},{4,10},{6,12},{8,6},{10,0},{12,2},{14,4},{1,15},{3,9}... | collective-permute-start | bytes 442376 | tf_op jit(solution)/shard_map/ppermute | solution.py:851
  79.6 8.9 %collective-permute-start.21 = (f32[2,40,512]{2,1,0:T(8,128)S(1)}, f32[2,40,512]{2,1,0:T(8,128)S(1)}, u32[]{:S(2)}, u32[]{:S(2)}) collective-permute-start(f32[2,40,512]{2,1,0:T(8,128)S(1)} %get-tuple-element.85), channel_id=1, source_target_pairs={{0,1},{1,0},{2,3},{3,2},{4,5},{5,4},{6,7},{7,6},{8,9},{9,8},{10,11... | collective-permute-start | bytes 491528 | tf_op jit(solution)/shard_map/ppermute | solution.py:838
  79.7 5.9 %collective-permute-start.22 = (f32[64,512]{1,0:T(8,128)S(1)}, f32[64,512]{1,0:T(8,128)S(1)}, u32[]{:S(2)}, u32[]{:S(2)}) collective-permute-start(f32[64,512]{1,0:T(8,128)S(1)} %get-tuple-element.86.refs_0_), channel_id=1, source_target_pairs={{0,8},{8,0},{1,9},{9,1},{2,10},{10,2},{3,11},{11,3},{4,12},{12,4},... | collective-permute-start | bytes 393224 | tf_op jit(solution)/shard_map/ppermute | solution.py:856
  80.6 6.3 %collective-permute-start.25 = (f32[64,512]{1,0:T(8,128)S(1)}, f32[64,512]{1,0:T(8,128)S(1)}, u32[]{:S(2)}, u32[]{:S(2)}) collective-permute-start(f32[64,512]{1,0:T(8,128)S(1)} %get-tuple-element.86.refs_0_), channel_id=1, source_target_pairs={{0,6},{2,0},{4,2},{6,4},{1,7},{3,1},{5,3},{7,5},{8,14},{10,8},{12,... | collective-permute-start | bytes 393224 | tf_op jit(solution)/shard_map/ppermute | solution.py:860
  81.1 8.6 %collective-permute-start.26 = (f32[64,512]{1,0:T(8,128)S(1)}, f32[64,512]{1,0:T(8,128)S(1)}, u32[]{:S(2)}, u32[]{:S(2)}) collective-permute-start(f32[64,512]{1,0:T(8,128)S(1)} %get-tuple-element.86.refs_0_), channel_id=1, source_target_pairs={{0,4},{2,6},{4,0},{6,2},{1,5},{3,7},{5,1},{7,3},{8,12},{10,14},{12... | collective-permute-start | bytes 393224 | tf_op jit(solution)/shard_map/ppermute | solution.py:860
  82.4 9.8 %collective-permute-start.27 = (f32[64,512]{1,0:T(8,128)S(1)}, f32[64,512]{1,0:T(8,128)S(1)}, u32[]{:S(2)}, u32[]{:S(2)}) collective-permute-start(f32[64,512]{1,0:T(8,128)S(1)} %get-tuple-element.86.refs_0_), channel_id=1, source_target_pairs={{0,2},{2,4},{4,6},{6,0},{1,3},{3,5},{5,7},{7,1},{8,10},{10,12},{12... | collective-permute-start | bytes 393224 | tf_op jit(solution)/shard_map/ppermute | solution.py:860
  85.6 7.0 %collective-permute-start.28 = (f32[64,512]{1,0:T(8,128)S(1)}, f32[64,512]{1,0:T(8,128)S(1)}, u32[]{:S(2)}, u32[]{:S(2)}) collective-permute-start(f32[64,512]{1,0:T(8,128)S(1)} %collective-permute-done.22.refs_4_), channel_id=1, source_target_pairs={{0,6},{2,0},{4,2},{6,4},{1,7},{3,1},{5,3},{7,5},{8,14},{10,8},{12,... | collective-permute-start | bytes 393224 | tf_op jit(solution)/shard_map/ppermute | solution.py:860
  87.0 7.9 %collective-permute-start.29 = (f32[64,512]{1,0:T(8,128)S(1)}, f32[64,512]{1,0:T(8,128)S(1)}, u32[]{:S(2)}, u32[]{:S(2)}) collective-permute-start(f32[64,512]{1,0:T(8,128)S(1)} %collective-permute-done.22.refs_4_), channel_id=1, source_target_pairs={{0,4},{2,6},{4,0},{6,2},{1,5},{3,7},{5,1},{7,3},{8,12},{10,14},{12... | collective-permute-start | bytes 393224 | tf_op jit(solution)/shard_map/ppermute | solution.py:860
  88.5 7.8 %collective-permute-start.30 = (f32[64,512]{1,0:T(8,128)S(1)}, f32[64,512]{1,0:T(8,128)S(1)}, u32[]{:S(2)}, u32[]{:S(2)}) collective-permute-start(f32[64,512]{1,0:T(8,128)S(1)} %collective-permute-done.22.refs_4_), channel_id=1, source_target_pairs={{0,2},{2,4},{4,6},{6,0},{1,3},{3,5},{5,7},{7,1},{8,10},{10,12},{12... | collective-permute-start | bytes 393224 | tf_op jit(solution)/shard_map/ppermute | solution.py:860
  100.5 6.6 %collective-permute-start.31 = (f32[2,128,256]{2,1,0:T(8,128)S(1)}, f32[2,128,256]{2,1,0:T(8,128)S(1)}, u32[]{:S(2)}, u32[]{:S(2)}) collective-permute-start(f32[2,128,256]{2,1,0:T(8,128)S(1)} %get-tuple-element.94), channel_id=1, source_target_pairs={{0,1},{1,0},{2,3},{3,2},{4,5},{5,4},{6,7},{7,6},{8,9},{9,8},{10,11... | collective-permute-start | bytes 786440 | tf_op jit(solution)/shard_map/ppermute | solution.py:838
  100.6 13.6 %all-to-all-start.1 = ((f32[8,64,128]{2,1,0:T(8,128)}), f32[8,64,128]{2,1,0:T(8,128)S(1)}, u32[]{:S(2)}, u32[]{:S(2)}) async-start(f32[8,64,128]{2,1,0:T(8,128)} %pair_to_facets.1), calls=%async_computation.1 | async-start | bytes 524288 | tf_op jit(solution)/shard_map/all_to_all | solution.py:924
  114.2 19.7 %all-to-all-start.2 = ((f32[8,72,512]{2,1,0:T(8,128)}), f32[8,72,512]{2,1,0:T(8,128)S(1)}, u32[]{:S(2)}, u32[]{:S(2)}) async-start(f32[8,72,512]{2,1,0:T(8,128)} %backward.3), calls=%async_computation.2 | async-start | bytes 2359296 | tf_op jit(solution)/shard_map/all_to_all | solution.py:928
  125.0 18.1 %collective-permute-start.23 = (f32[8,40,128]{2,1,0:T(8,128)S(1)}, f32[8,40,128]{2,1,0:T(8,128)S(1)}, u32[]{:S(2)}, u32[]{:S(2)}) collective-permute-start(f32[8,40,128]{2,1,0:T(8,128)S(1)} %get-tuple-element.90), channel_id=1, source_target_pairs={{0,16},{16,32},{32,48},{48,64},{64,80},{80,96},{96,112},{1,17},{17... | collective-permute-start | bytes 491528 | tf_op jit(solution)/shard_map/ppermute | solution.py:868
  129.3 13.8 %collective-permute-start.24 = (f32[8,40,128]{2,1,0:T(8,128)S(1)}, f32[8,40,128]{2,1,0:T(8,128)S(1)}, u32[]{:S(2)}, u32[]{:S(2)}) collective-permute-start(f32[8,40,128]{2,1,0:T(8,128)S(1)} %get-tuple-element.91), channel_id=1, source_target_pairs={{16,0},{32,16},{48,32},{64,48},{80,64},{96,80},{112,96},{17,1},{33... | collective-permute-start | bytes 491528 | tf_op jit(solution)/shard_map/ppermute | solution.py:868
  136.2 16.6 %all-to-all-start.3 = ((f32[8,48,128]{2,1,0:T(8,128)}), f32[8,48,128]{2,1,0:T(8,128)S(1)}, u32[]{:S(2)}, u32[]{:S(2)}) async-start(f32[8,48,128]{2,1,0:T(8,128)} %to_facets.1), calls=%async_computation.3 | async-start | bytes 393216 | tf_op jit(solution)/shard_map/all_to_all | solution.py:941
  143.2 7.7 %collective-permute-start.33 = (f32[8,2,8,128]{3,2,1,0:T(8,128)S(1)}, f32[8,2,8,128]{3,2,1,0:T(8,128)S(1)}, u32[]{:S(2)}, u32[]{:S(2)}) collective-permute-start(f32[8,2,8,128]{3,2,1,0:T(8,128)S(1)} %get-tuple-element.103), channel_id=1, source_target_pairs={{0,1},{1,2},{2,3},{3,4},{4,5},{5,6},{6,7},{7,8},{8,9},{9,10},{10,1... | collective-permute-start | bytes 196616 | tf_op jit(solution)/shard_map/ppermute | solution.py:868
  145.2 7.6 %collective-permute-start.34 = (f32[8,2,8,128]{3,2,1,0:T(8,128)S(1)}, f32[8,2,8,128]{3,2,1,0:T(8,128)S(1)}, u32[]{:S(2)}, u32[]{:S(2)}) collective-permute-start(f32[8,2,8,128]{3,2,1,0:T(8,128)S(1)} %get-tuple-element.102), channel_id=1, source_target_pairs={{1,0},{2,1},{3,2},{4,3},{5,4},{6,5},{7,6},{8,7},{9,8},{10,9},{11,1... | collective-permute-start | bytes 196616 | tf_op jit(solution)/shard_map/ppermute | solution.py:868
  (25 other events, 156.1 us)
